TPU v7x, 256 devices: a whole 4x4x8 slice. The times are simulated.
256 devices in a mesh: fsdp: 8 (over z_lo, core), seq: 32 (over y, z_hi, x).
Axes of the slice: x: 4, y: 4, z: 8 (z_hi: 2, z_lo: 4; z = z_hi * 4 + z_lo), core: 2. Of those that a mesh axis runs over, the one named last changes fastest.
Arguments:
- query_tiles: bfloat16 [55296, 3072], P('seq', 'fsdp'), may hold values from -50 to 50
- key_tiles: bfloat16 [55296, 3072], P('seq', 'fsdp'), may hold values from -50 to 50
- value_tiles: bfloat16 [55296, 3072], P('seq', 'fsdp'), may hold values from -6 to 6
- slab_counts: int32 [32], P('seq'), may hold values from 1 to 3, 64 in all
- out_weight: bfloat16 [3072, 5120], P('seq', 'fsdp'), may hold values from -1.5 to 1.5
- out_bias: float32 [5120], P('fsdp'), may hold values from -3 to 3
Outputs:
- block_out: bfloat16 [5120, 55296], P('fsdp', 'seq')
Inputs may be any that keep to these rules, and one draw needn't show every extreme that they name: slab_counts[d] is the number of consecutive tile frames held by device d of seq; they sum to 64, and some device holds 3.
All inputs are finite; a program needn't handle non-finite values.
Results may differ from a plain program's by a relative error of at most 0.024.
Values may be sent and summed in bfloat16 or wider, within the bound.
No kernel may reach another device: no remote copies, remote signals or barrier semaphores. Data moves between devices by JAX's collectives and lax.ppermute only.
A program may use at most 128 MiB of HBM per device.

v0:
```python
import jax
import jax.numpy as jnp
from jax import lax
from jax.sharding import PartitionSpec as P

HEAD = 128
TILE_TOK = 192
TILES_WIDE = 3


def from_behind(value, axis, steps):
    count = lax.axis_size(axis)
    first, last = (max(0, -steps), min(count, count - steps))
    return lax.ppermute(value, axis, [(source, source + steps) for source in range(first, last)])


def on_device(query_tiles, key_tiles, value_tiles, slab_counts, out_weight, out_bias):
    frame_rows = TILE_TOK * TILES_WIDE
    local_width = query_tiles.shape[1]
    head_local = local_width // HEAD
    slot_total = query_tiles.shape[0] // frame_rows
    row_total = slot_total * frame_rows
    live_count = slab_counts[0]
    shaped = (slot_total, frame_rows, head_local, HEAD)
    local_query = query_tiles.reshape(shaped)
    local_key = key_tiles.reshape(shaped)
    local_value = value_tiles.reshape(shaped)
    last_key = lax.dynamic_index_in_dim(local_key, live_count - 1, 0, keepdims=False)
    last_value = lax.dynamic_index_in_dim(local_value, live_count - 1, 0, keepdims=False)
    left_key, left_value = from_behind((last_key, last_value), "seq", 1)
    right_key, right_value = from_behind((local_key[0], local_value[0]), "seq", -1)
    position = lax.axis_index("seq")
    seq_width = lax.axis_size("seq")
    slot_index = jnp.arange(slot_total, dtype=jnp.int32)
    has_next = slot_index + 1 < live_count

    def window(local, left_side, right_side):
        before = jnp.concatenate([left_side[None], local[:-1]], axis=0)
        after = jnp.concatenate([local[1:], right_side[None]], axis=0)
        after = jnp.where(has_next[:, None, None, None], after, right_side[None])
        return jnp.concatenate([before, local, after], axis=1)

    key_set = window(local_key, left_key, right_key)
    value_set = window(local_value, left_value, right_value)
    prev_ok = (slot_index > 0) | (position > 0)
    next_ok = has_next | (position < seq_width - 1)
    block_ids = jnp.arange(3 * frame_rows, dtype=jnp.int32) // frame_rows
    block_ok = ((block_ids[None, :] != 0) | prev_ok[:, None]) & (
        (block_ids[None, :] != 2) | next_ok[:, None]
    )
    query_tile = jnp.arange(frame_rows, dtype=jnp.int32) // TILE_TOK
    key_tile = jnp.arange(3 * frame_rows, dtype=jnp.int32) % frame_rows // TILE_TOK
    near_tiles = jnp.abs(query_tile[:, None] - key_tile[None, :]) <= 1

    def slot_attend(item):
        query_slot, key_slot, value_slot, slot_ok = item
        scores = jnp.einsum(
            "qhd,khd->hqk", query_slot, key_slot, preferred_element_type=jnp.float32
        ) * HEAD ** (-0.5)
        allowed = slot_ok[None, None, :] & near_tiles[None]
        scores = jnp.where(allowed, scores, -1e30)
        highest = jnp.max(scores, axis=-1, keepdims=True)
        expo = jnp.exp(scores - highest)
        weights = (expo / jnp.sum(expo, axis=-1, keepdims=True)).astype(jnp.bfloat16)
        return jnp.einsum(
            "hqk,khd->qhd", weights, value_slot, preferred_element_type=jnp.float32
        ).astype(jnp.bfloat16)

    attended = lax.map(slot_attend, (local_query, key_set, value_set, block_ok)).reshape(
        row_total, local_width
    )
    full_rows = lax.all_gather(out_weight, "seq", axis=0, tiled=True)
    contract = (((0,), (1,)), ((), ()))
    head_weight = lax.all_to_all(full_rows, "fsdp", split_axis=0, concat_axis=1, tiled=True)
    projected = lax.psum_scatter(
        lax.dot_general(head_weight, attended, contract, preferred_element_type=jnp.float32).astype(
            jnp.bfloat16
        ),
        "fsdp",
        scatter_dimension=0,
        tiled=True,
    ).astype(jnp.float32)
    row_live = jnp.arange(row_total, dtype=jnp.int32) // frame_rows < live_count
    return jnp.where(row_live[None, :], projected + out_bias[:, None], 0.0).astype(jnp.bfloat16)


def solution(mesh):
    return jax.shard_map(
        on_device,
        mesh=mesh,
        in_specs=(
            P("seq", "fsdp"),
            P("seq", "fsdp"),
            P("seq", "fsdp"),
            P("seq"),
            P("seq", "fsdp"),
            P("fsdp"),
        ),
        out_specs=P("fsdp", "seq"),
        check_vma=False,
    )
```

profile of v0, /device:TPU:9, one launch (start us, length us, event | category | flops | bytes accessed | tf_op | source)
XLA Modules:
  0.0 503.6 jit_solution(10722676770961125811)
XLA Ops:
  7.9 3.7 reshape.119
  12.6 3.1 collective-permute-start.2
  17.1 9.7 %collective-permute-start.3 = (bf16[576,3,128]{2,0,1:T(8,128)(2,1)}, bf16[576,3,128]{2,0,1:T(8,128)(2,1)}, u32[]{:S(2)}, u32[]{:S(2)}) collective-permute-start(bf16[576,3,128]{2,0,1:T(8,128)(2,1)} %copy.79), channel_id=1, source_target_pairs={{1,0},{2,1},{3,2},{4,3},{5,4},{6,5},{7,6},{8,7},{9,8},{10,9},{11,1... | collective-permute-start | bytes 1327112 | tf_op jit(solution)/shard_map/ppermute | solution.py:14
  28.0 3.4 collective-permute-start.1
  31.4 3.6 reshape.117
  38.5 2.8 fusion.50
  41.4 3.4 reshape.122
  47.5 3.4 reshape.124
  51.0 3.4 reshape.123
  54.4 3.4 reshape.121
  57.8 4.6 reshape.118
  62.4 2.9 copy.84
  70.3 3.0 maximum_select_fusion.1
  73.3 29.7 %pad_maximum_fusion.1 = bf16[3,1728,3,128]{3,2,1,0:T(4,128)(2,1)S(1)} fusion(bf16[3,576,3,128]{3,2,1,0:T(4,128)(2,1)S(1)} %get-tuple-element.121, bf16[3,576,3,128]{3,2,1,0:T(4,128)(2,1)S(1)} %reshape.119, bf16[2,576,3,128]{3,2,1,0:T(4,128)(2,1)S(1)} %copy-done.2, bf16[1,576,3,128]{3,2,1,0:T(4,128)(2,1)S(1)} %bitcast.69), kind=kLoop, calls=%fused_computation.30 | loop fusion | flops 5971968 | bytes 7962624 | tf_op jit(solution)/shard_map/concatenate | solution.py:41
  107.1 29.5 %pad_maximum_fusion = bf16[3,1728,3,128]{3,2,1,0:T(4,128)(2,1)S(1)} fusion(bf16[3,576,3,128]{3,2,1,0:T(4,128)(2,1)S(1)} %get-tuple-element.122, bf16[3,576,3,128]{3,2,1,0:T(4,128)(2,1)S(1)} %reshape.117, bf16[2,576,3,128]{3,2,1,0:T(4,128)(2,1)S(1)} %copy-done, bf16[1,576,3,128]{3,2,1,0:T(4,128)(2,1)S(1)} %bitcast.70), kind=kLoop, calls=%fused_computation.29 | loop fusion | flops 5971968 | bytes 7962624 | tf_op jit(solution)/shard_map/concatenate | solution.py:41
  139.2 13.9 %all-gather.2.cloned.1.call-done = bf16[3072,640]{1,0:T(8,128)(2,1)} async-done(((bf16[96,640]{1,0:T(8,128)(2,1)}), bf16[3072,640]{1,0:T(8,128)(2,1)}) %all-gather.2.cloned.1.call-update) | async-done | bytes 3932176 | tf_op jit(solution)/shard_map/all_gather | solution.py:72
  153.0 6.6 %all-to-all-start = ((bf16[8,384,640]{2,1,0:T(8,128)(2,1)}), bf16[8,384,640]{2,1,0:T(8,128)(2,1)}, u32[]{:S(2)}, u32[]{:S(2)}) async-start(bf16[8,384,640]{2,1,0:T(8,128)(2,1)} %bitcast.67), calls=%async_computation | async-start | bytes 7864320 | tf_op jit(solution)/shard_map/all_to_all | solution.py:74
  159.7 102.6 %while.11 = (s32[]{:T(128)}, bf16[3,576,3,128]{3,1,2,0:T(8,128)(2,1)S(1)}, bf16[3,1728,3,128]{3,1,2,0:T(8,128)(2,1)}, pred[3,1728]{1,0:T(4,128)(4,1)S(1)}, bf16[...) while((s32[]{:T(128)}, ...), condition=%wide.region_3.4_spmd.clone, body=%wide.region_0.3_spmd.clone.sunk | while | flops 1556915968 | bytes 53781408 | solution.py:69
  161.2 7.7 %fusion.64 = f32[3,576,1728]{2,1,0:T(8,128)} fusion(bf16[3,1728,3,128]{3,1,2,0:T(8,128)(2,1)} %get-tuple-element.203, s32[]{:T(128)} %get-tuple-element.189, bf16[3,576,3,128]{3,1,2,0:T(8,128)(2,1)} %get-tuple-element.202), kind=kOutput, calls=%fused_computation.12.clone.1 | convolution fusion | flops 764411904 | bytes 13714432 | tf_op jit(solution)/shard_map/while/body/eval_jaxpr/qhd,khd->hqk/dot_general | solution.py:57
  169.0 18.3 %fusion.66 = (f32[3,576]{1,0:T(4,128)S(1)}, f32[3,576,1728]{2,1,0:T(8,128)}) fusion(f32[3,576,1728]{2,1,0:T(8,128)} %fusion.64, pred[576,1728]{1,0:T(8,128)(4,1)S(1)} %fusion.65), kind=kOutput, calls=%fused_computation.76.clone.1 | output fusion | flops 17917632 | bytes 24890112 | tf_op jit(solution)/shard_map/while/body/eval_jaxpr/sub | solution.py:63
  187.2 6.8 %fusion.67 = bf16[3,576,3,128]{3,1,2,0:T(8,128)(2,1)S(1)} fusion(bf16[3,576,3,128]{3,1,2,0:T(8,128)(2,1)S(1)} %get-tuple-element.190, s32[]{:T(128)} %get-tuple-element.189, bf16[3,1728,3,128]{3,1,2,0:T(8,128)(2,1)} %get-tuple-element.200, f32[3,576,1728]{2,1,0:T(8,128)} %get-tuple-element.178, f32[3,576]{1,0:T(4,128)S(1)} %get-tuple-element.179), kind=kOutput, calls=%fused_computation.19.clone.1 | convolution fusion | flops 770605056 | bytes 14167040 | tf_op jit(solution)/shard_map/while/body/eval_jaxpr/hqk,khd->qhd/dot_general | solution.py:65
  195.4 7.7 %fusion.64 = f32[3,576,1728]{2,1,0:T(8,128)} fusion(bf16[3,1728,3,128]{3,1,2,0:T(8,128)(2,1)} %get-tuple-element.203, s32[]{:T(128)} %get-tuple-element.189, bf16[3,576,3,128]{3,1,2,0:T(8,128)(2,1)} %get-tuple-element.202), kind=kOutput, calls=%fused_computation.12.clone.1 | convolution fusion | flops 764411904 | bytes 13714432 | tf_op jit(solution)/shard_map/while/body/eval_jaxpr/qhd,khd->hqk/dot_general | solution.py:57
  203.1 18.3 %fusion.66 = (f32[3,576]{1,0:T(4,128)S(1)}, f32[3,576,1728]{2,1,0:T(8,128)}) fusion(f32[3,576,1728]{2,1,0:T(8,128)} %fusion.64, pred[576,1728]{1,0:T(8,128)(4,1)S(1)} %fusion.65), kind=kOutput, calls=%fused_computation.76.clone.1 | output fusion | flops 17917632 | bytes 24890112 | tf_op jit(solution)/shard_map/while/body/eval_jaxpr/sub | solution.py:63
  221.3 6.8 %fusion.67 = bf16[3,576,3,128]{3,1,2,0:T(8,128)(2,1)S(1)} fusion(bf16[3,576,3,128]{3,1,2,0:T(8,128)(2,1)S(1)} %get-tuple-element.190, s32[]{:T(128)} %get-tuple-element.189, bf16[3,1728,3,128]{3,1,2,0:T(8,128)(2,1)} %get-tuple-element.200, f32[3,576,1728]{2,1,0:T(8,128)} %get-tuple-element.178, f32[3,576]{1,0:T(4,128)S(1)} %get-tuple-element.179), kind=kOutput, calls=%fused_computation.19.clone.1 | convolution fusion | flops 770605056 | bytes 14167040 | tf_op jit(solution)/shard_map/while/body/eval_jaxpr/hqk,khd->qhd/dot_general | solution.py:65
  229.5 7.7 %fusion.64 = f32[3,576,1728]{2,1,0:T(8,128)} fusion(bf16[3,1728,3,128]{3,1,2,0:T(8,128)(2,1)} %get-tuple-element.203, s32[]{:T(128)} %get-tuple-element.189, bf16[3,576,3,128]{3,1,2,0:T(8,128)(2,1)} %get-tuple-element.202), kind=kOutput, calls=%fused_computation.12.clone.1 | convolution fusion | flops 764411904 | bytes 13714432 | tf_op jit(solution)/shard_map/while/body/eval_jaxpr/qhd,khd->hqk/dot_general | solution.py:57
  237.2 18.3 %fusion.66 = (f32[3,576]{1,0:T(4,128)S(1)}, f32[3,576,1728]{2,1,0:T(8,128)}) fusion(f32[3,576,1728]{2,1,0:T(8,128)} %fusion.64, pred[576,1728]{1,0:T(8,128)(4,1)S(1)} %fusion.65), kind=kOutput, calls=%fused_computation.76.clone.1 | output fusion | flops 17917632 | bytes 24890112 | tf_op jit(solution)/shard_map/while/body/eval_jaxpr/sub | solution.py:63
  255.5 6.8 %fusion.67 = bf16[3,576,3,128]{3,1,2,0:T(8,128)(2,1)S(1)} fusion(bf16[3,576,3,128]{3,1,2,0:T(8,128)(2,1)S(1)} %get-tuple-element.190, s32[]{:T(128)} %get-tuple-element.189, bf16[3,1728,3,128]{3,1,2,0:T(8,128)(2,1)} %get-tuple-element.200, f32[3,576,1728]{2,1,0:T(8,128)} %get-tuple-element.178, f32[3,576]{1,0:T(4,128)S(1)} %get-tuple-element.179), kind=kOutput, calls=%fused_computation.19.clone.1 | convolution fusion | flops 770605056 | bytes 14167040 | tf_op jit(solution)/shard_map/while/body/eval_jaxpr/hqk,khd->qhd/dot_general | solution.py:65
  263.4 6.5 %copy.87 = bf16[384,8,640]{0,2,1:T(8,128)(2,1)} copy(bf16[384,8,640]{2,0,1:T(8,128)(2,1)} %bitcast.10) | data formatting | bytes 7864320 | tf_op jit(solution)/shard_map/all_to_all | solution.py:74
  270.0 14.5 %fusion.29 = bf16[5120,1728]{0,1:T(8,128)(2,1)} fusion(bf16[384,5120]{0,1:T(8,128)(2,1)} %bitcast.68, bf16[216,8,3,128]{3,2,1,0:T(4,128)(2,1)S(1)} %bitcast.73), kind=kOutput, calls=%fused_computation.28 | convolution fusion | flops 6803619840 | bytes 22953984 | tf_op jit(solution)/shard_map/dot_general | solution.py:76
  284.4 22.9 %copy.92 = bf16[5120,1728]{1,0:T(8,128)(2,1)} copy(bf16[5120,1728]{0,1:T(8,128)(2,1)} %fusion.29) | data formatting | bytes 35389440
  307.4 183.6 %reduce-scatter.4.cloned.1.call-done = bf16[640,1728]{1,0:T(8,128)(2,1)} async-done(((bf16[5120,1728]{1,0:T(8,128)(2,1)}), bf16[640,1728]{1,0:T(8,128)(2,1)}) %reduce-scatter.4.cloned.1.call-update) | async-done | bytes 2211856
  491.0 3.4 copy.93
  (59 shorter events, 29.4 us)
Async XLA Ops:
  6.5 9.2 %slice-start.1 = ((bf16[1728,384]{1,0:T(8,128)(2,1)}), bf16[576,384]{1,0:T(8,128)(2,1)S(1)}, s32[]{:S(2)}) async-start(bf16[1728,384]{1,0:T(8,128)(2,1)} %param.9), calls=%async_computation.5 | async-start | bytes 884736 | tf_op jit(solution)/shard_map/slice | solution.py:31
  6.5 146.5 %all-gather.2.cloned.1.call-start = ((), (), s32[]{:S(2)}) async-start(), calls=%async_computation.2 | async-start | bytes 4055040 | tf_op jit(solution)/shard_map/all_gather | solution.py:72
  7.9 18.9 %slice-start = ((bf16[1728,384]{1,0:T(8,128)(2,1)}), bf16[576,384]{1,0:T(8,128)(2,1)S(1)}, s32[]{:S(2)}) async-start(bf16[1728,384]{1,0:T(8,128)(2,1)} %param.10), calls=%async_computation.4 | async-start | bytes 884736 | tf_op jit(solution)/shard_map/slice | solution.py:31
  12.6 53.4 %collective-permute-start.2 = (bf16[576,3,128]{2,0,1:T(8,128)(2,1)}, bf16[576,3,128]{2,0,1:T(8,128)(2,1)}, u32[]{:S(2)}, u32[]{:S(2)}) collective-permute-start(bf16[576,3,128]{2,0,1:T(8,128)(2,1)} %bitcast.50), channel_id=1, source_target_pairs={{0,1},{1,2},{2,3},{3,4},{4,5},{5,6},{6,7},{7,8},{8,9},{9,10},{10,1... | collective-permute-start | bytes 1327112 | tf_op jit(solution)/shard_map/ppermute | solution.py:14
  17.1 50.4 %collective-permute-start.3 = (bf16[576,3,128]{2,0,1:T(8,128)(2,1)}, bf16[576,3,128]{2,0,1:T(8,128)(2,1)}, u32[]{:S(2)}, u32[]{:S(2)}) collective-permute-start(bf16[576,3,128]{2,0,1:T(8,128)(2,1)} %copy.79), channel_id=1, source_target_pairs={{1,0},{2,1},{3,2},{4,3},{5,4},{6,5},{7,6},{8,7},{9,8},{10,9},{11,1... | collective-permute-start | bytes 1327112 | tf_op jit(solution)/shard_map/ppermute | solution.py:14
  28.0 40.8 %collective-permute-start.1 = (bf16[576,3,128]{2,0,1:T(8,128)(2,1)}, bf16[576,3,128]{2,0,1:T(8,128)(2,1)}, u32[]{:S(2)}, u32[]{:S(2)}) collective-permute-start(bf16[576,3,128]{2,0,1:T(8,128)(2,1)} %copy.69), channel_id=1, source_target_pairs={{1,0},{2,1},{3,2},{4,3},{5,4},{6,5},{7,6},{8,7},{9,8},{10,9},{11,1... | collective-permute-start | bytes 1327112 | tf_op jit(solution)/shard_map/ppermute | solution.py:14
  36.1 69.6 %collective-permute-start = (bf16[576,3,128]{2,0,1:T(8,128)(2,1)}, bf16[576,3,128]{2,0,1:T(8,128)(2,1)}, u32[]{:S(2)}, u32[]{:S(2)}) collective-permute-start(bf16[576,3,128]{2,0,1:T(8,128)(2,1)} %bitcast.51), channel_id=1, source_target_pairs={{0,1},{1,2},{2,3},{3,4},{4,5},{5,6},{6,7},{7,8},{8,9},{9,10},{10,1... | collective-permute-start | bytes 1327112 | tf_op jit(solution)/shard_map/ppermute | solution.py:14
  62.4 7.9 %copy-start.1 = (bf16[2,576,3,128]{3,2,1,0:T(4,128)(2,1)S(1)}, bf16[2,576,3,128]{3,2,1,0:T(4,128)(2,1)}, u32[]{:S(2)}) copy-start(bf16[2,576,3,128]{3,2,1,0:T(4,128)(2,1)} %reshape.122) | copy-start | bytes 2654212
  62.4 7.9 %copy-start.3 = (bf16[2,576,3,128]{3,2,1,0:T(4,128)(2,1)S(1)}, bf16[2,576,3,128]{3,2,1,0:T(4,128)(2,1)}, u32[]{:S(2)}) copy-start(bf16[2,576,3,128]{3,2,1,0:T(4,128)(2,1)} %reshape.124) | copy-start | bytes 2654212
  70.3 3.0 copy-start.2
  103.0 4.0 copy-start
  153.0 6.6 %copy-start.4 = (bf16[3,576,3,128]{3,1,2,0:T(8,128)(2,1)S(1)}, bf16[3,576,3,128]{3,1,2,0:T(8,128)(2,1)}, u32[]{:S(2)}) copy-start(bf16[3,576,3,128]{3,1,2,0:T(8,128)(2,1)} %custom-call) | copy-start | bytes 3981316
  153.0 6.6 %copy-start.5 = (s32[576]{0:T(1024)S(1)}, s32[576]{0:T(1024)}, u32[]{:S(2)}) copy-start(s32[576]{0:T(1024)} %add_select_fusion.2) | copy-start | bytes 6916
  153.0 110.4 %all-to-all-start = ((bf16[8,384,640]{2,1,0:T(8,128)(2,1)}), bf16[8,384,640]{2,1,0:T(8,128)(2,1)}, u32[]{:S(2)}, u32[]{:S(2)}) async-start(bf16[8,384,640]{2,1,0:T(8,128)(2,1)} %bitcast.67), calls=%async_computation | async-start | bytes 7864320 | tf_op jit(solution)/shard_map/all_to_all | solution.py:74
  159.7 331.4 %reduce-scatter.4.cloned.1.call-start = ((), (), s32[]{:S(2)}) async-start(), calls=%async_computation.3 | async-start | bytes 20643840
  307.4 187.0 %copy-start.6 = (f32[640]{0:T(1024)S(1)}, f32[640]{0:T(1024)}, u32[]{:S(2)}) copy-start(f32[640]{0:T(1024)} %param.13) | copy-start | bytes 7684
Sparse Core Ops, SparseCore 0:
  10.7 142.2 all-gather.1
  307.5 183.4 reduce-scatter.3
where the time goes:
time: 511 us; the launch traced here: 504 us
  waiting for transfers between devices  198 us (39%)
  other arithmetic  124 us (24%)
  local copies, waits for them, and re-layouts  83.5 us (16%)
  matrix products  58 us (11%)
  starting transfers between devices  25.2 us (5%)
  between operations  14.6 us (3%)
    unnamed x3, waiting for transfers between devices  184 us
    concatenate x2, other arithmetic, window(): return jnp.concatenate([before, local, after], axis=1)  59.2 us
    sub x3, other arithmetic, slot_attend(): expo = jnp.exp(scores - highest)  54.8 us
    unnamed x19, local copies, waits for them, and re-layouts  34.4 us
    dot_general x3, matrix products, slot_attend(): jnp.einsum('qhd,khd->hqk', query_slot, key_slot, preferred_element_type=j...  23.2 us
    dot_general x3, matrix products, slot_attend(): jnp.einsum('hqk,khd->qhd', weights, value_slot, preferred_element_type=jn...  20.3 us
    ppermute x4, starting transfers between devices, from_behind(): lax.ppermute(value, axis, [(source, source + steps) for source in range(f...  18.6 us
    dot_general x1, matrix products, on_device(): lax.dot_general(head_weight, attended, contract, preferred_element_type=j...  14.5 us
  transfers between devices with their start and end apart: 7, of which 2 were waited for; matrix products, arithmetic and copies ran while one was open for 43% of the time, Pallas kernels for 0%

commit v1 on v0

v1 whole, which is shorter than its diff:
```python
import functools

import jax
import jax.numpy as jnp
from jax import lax
from jax.experimental import pallas as pl
from jax.experimental.pallas import tpu as pltpu
from jax.sharding import Mesh
from jax.sharding import PartitionSpec as P

HEAD = 128
TILE = 192
FRAME = 576
LN2 = 0.6931471805599453
SCALE = HEAD**-0.5 / LN2
FAR = 1e30
SEQ = ("y", "zh", "x")
FSDP = ("zl", "core")
VMEM = 48 * 1024 * 1024


def attend_body(halo_total, info, q_ref, k_ref, v_ref, *rest):
    halos, (o_ref, kbuf, vbuf) = rest[:halo_total], rest[-3:]
    slot, prev_from, next_from, prev_ok, next_ok, active = (info[i] for i in range(6))

    @pl.when(pl.program_id(0) == 0)
    def _():
        vbuf[:, HEAD:] = jnp.ones((3 * FRAME, HEAD), jnp.bfloat16)

    @pl.when(active == 0)
    def _():
        o_ref[...] = jnp.zeros_like(o_ref)

    def fill(place, source):
        rows = pl.ds(place * FRAME, FRAME)

        @pl.when(source < 3)
        def _():
            local = pl.ds(pl.multiple_of(jnp.clip(source, 0, 2) * FRAME, FRAME), FRAME)
            kbuf[rows, :] = k_ref[local, :]
            vbuf[rows, :HEAD] = v_ref[local, :]

        for i in range(len(halos)):

            @pl.when(source == 3 + i)
            def _():
                kbuf[rows, :] = halos[i][:FRAME, :]
                vbuf[rows, :HEAD] = halos[i][FRAME:, :]

    @pl.when(active == 1)
    def _():
        fill(0, prev_from)
        fill(1, slot)
        fill(2, next_from)
        off = [jnp.where(prev_ok == 1, 0.0, FAR), jnp.float32(0.0), jnp.where(next_ok == 1, 0.0, FAR)]
        for w in range(3):
            low, high = max(0, w - 1) * TILE, min(3, w + 2) * TILE
            q = q_ref[pl.ds(pl.multiple_of(slot * FRAME + w * TILE, TILE), TILE), :]
            scores, tops = [], []
            for f in range(3):
                keys = kbuf[f * FRAME + low : f * FRAME + high, :]
                s = lax.dot_general(q, keys, (((1,), (1,)), ((), ())), preferred_element_type=jnp.float32)
                scores.append(s)
                tops.append(jnp.max(s, axis=1, keepdims=True) * SCALE - off[f])
            top = jnp.maximum(jnp.maximum(tops[0], tops[1]), tops[2])
            total = None
            for f in range(3):
                p = jnp.exp2(scores[f] * SCALE - (top + off[f])).astype(jnp.bfloat16)
                part = jnp.dot(
                    p, vbuf[f * FRAME + low : f * FRAME + high, :], preferred_element_type=jnp.float32
                )
                total = part if total is None else total + part
            o_ref[w * TILE : (w + 1) * TILE, :] = (total[:, :HEAD] / total[:, HEAD:]).astype(jnp.bfloat16)


def attend(info, query, key, value, halos, after):
    rows, width = query.shape
    heads = width // HEAD
    column = lambda h, info: (0, h)
    whole = pl.BlockSpec((rows, HEAD), column)
    one = pl.BlockSpec((FRAME, HEAD), column)
    two = pl.BlockSpec((2 * FRAME, HEAD), column)
    return pl.pallas_call(
        functools.partial(attend_body, len(halos)),
        out_shape=jax.ShapeDtypeStruct((FRAME, width), jnp.bfloat16),
        grid_spec=pltpu.PrefetchScalarGridSpec(
            num_scalar_prefetch=1,
            grid=(heads,),
            in_specs=[whole] * 3 + [two] * len(halos) + [pl.BlockSpec(memory_space=pl.ANY)] * len(after),
            out_specs=one,
            scratch_shapes=[
                pltpu.VMEM((3 * FRAME, HEAD), jnp.bfloat16),
                pltpu.VMEM((3 * FRAME, 2 * HEAD), jnp.bfloat16),
            ],
        ),
        compiler_params=pltpu.CompilerParams(vmem_limit_bytes=VMEM),
        cost_estimate=pl.CostEstimate(flops=4 * 10**9, bytes_accessed=6 * 10**6, transcendentals=3 * 10**6),
    )(info, query, key, value, *halos, *after)


def project_body(info, x0, x1, x2, x3, w_ref, mine_ref, other_ref):
    total = None
    for k, x in enumerate((x0, x1, x2, x3)):
        width = x.shape[1]
        rows = pl.ds(pl.multiple_of(info[k] * width, width), width)
        part = jnp.dot(x[...], w_ref[rows, :], preferred_element_type=jnp.float32)
        total = part if total is None else total + part

    @pl.when(pl.program_id(0) == 0)
    def _():
        other_ref[...] = total.astype(jnp.bfloat16)

    @pl.when(pl.program_id(0) == 1)
    def _():
        mine_ref[...] = total


def project(order, pieces, weight):
    rows, width = pieces[0].shape
    depth, both = weight.shape
    columns = both // 2
    fixed = lambda j, info: (0, 0)
    return pl.pallas_call(
        project_body,
        out_shape=(
            jax.ShapeDtypeStruct((rows, columns), jnp.float32),
            jax.ShapeDtypeStruct((rows, columns), jnp.bfloat16),
        ),
        grid_spec=pltpu.PrefetchScalarGridSpec(
            num_scalar_prefetch=1,
            grid=(2,),
            in_specs=[pl.BlockSpec((rows, width), fixed)] * 4
            + [pl.BlockSpec((depth, columns), lambda j, info: (0, 1 - j))],
            out_specs=[pl.BlockSpec((rows, columns), fixed)] * 2,
        ),
        compiler_params=pltpu.CompilerParams(vmem_limit_bytes=VMEM),
        cost_estimate=pl.CostEstimate(
            flops=2 * rows * depth * both, bytes_accessed=2 * depth * (both + rows), transcendentals=0
        ),
    )(order, *pieces, weight)


def finish_body(info, mine_ref, received_ref, bias_ref, *rest):
    value = mine_ref[...] + received_ref[...].astype(jnp.float32) + bias_ref[...]
    rest[-1][...] = jnp.where(info[1] == 1, value, 0.0).astype(jnp.bfloat16)


def finish(info, mine, received, bias, out):
    rows, columns = mine.shape
    whole = pl.BlockSpec((rows, columns), lambda j, info: (0, 0))
    extra = [] if out is None else [out]
    return pl.pallas_call(
        finish_body,
        out_shape=jax.ShapeDtypeStruct((3 * rows, columns), jnp.bfloat16),
        grid_spec=pltpu.PrefetchScalarGridSpec(
            num_scalar_prefetch=1,
            grid=(1,),
            in_specs=[whole, whole, pl.BlockSpec((1, columns), lambda j, info: (0, 0))]
            + [pl.BlockSpec(memory_space=pl.ANY)] * len(extra),
            out_specs=pl.BlockSpec((rows, columns), lambda j, info: (info[0], 0)),
        ),
        input_output_aliases={4: 0} if extra else {},
        compiler_params=pltpu.CompilerParams(vmem_limit_bytes=VMEM),
    )(info, mine, received, bias.reshape(1, columns), *extra)


def lay_body(info, own_ref, beside_ref, across_ref, askew_ref, out_ref):
    columns = own_ref.shape[1]
    home = info[0] == 1
    out_ref[:, :columns] = jnp.where(home, own_ref[...], across_ref[...])
    out_ref[:, columns:] = jnp.where(home, beside_ref[...], askew_ref[...])


def lay(info, own, beside, across, askew):
    rows, columns = own.shape
    vmem = pl.BlockSpec(memory_space=pltpu.VMEM)
    return pl.pallas_call(
        lay_body,
        out_shape=jax.ShapeDtypeStruct((rows, 2 * columns), own.dtype),
        in_specs=[pl.BlockSpec(memory_space=pltpu.SMEM)] + [vmem] * 4,
        out_specs=vmem,
    )(info, own, beside, across, askew)


def on_device(query, key, value, slab_counts, out_weight, out_bias):
    count = slab_counts[0]
    x, zh, zl, core = (lax.axis_index(name) for name in ("x", "zh", "zl", "core"))
    seq = lax.axis_index(SEQ)
    seq_width = lax.axis_size(SEQ)
    even = x % 2 == 0
    last = count - 1

    near, away = [], []
    for s in range(seq_width):
        near.append((s, s + 1 if s % 2 == 0 else s - 1))
        t = s - 1 if s % 2 == 0 else s + 1
        if 0 <= t < seq_width:
            away.append((s, t))

    def frame_of(array, index):
        return lax.dynamic_slice_in_dim(array, index * FRAME, FRAME, 0)

    near_slot = jnp.where(even, last, 0)
    away_slot = jnp.where(even, 0, last)
    both = jnp.concatenate([frame_of(key, near_slot), frame_of(value, near_slot)], axis=0)
    near_halo = [lax.ppermute(both, SEQ, near)]
    both = jnp.concatenate([frame_of(key, away_slot), frame_of(value, away_slot)], axis=0)
    away_halo = [lax.ppermute(both, SEQ, away)]

    pair = ("core", "zh")
    beside = lax.ppermute(out_weight, pair, [(2, 0), (1, 3)])
    across = lax.ppermute(out_weight, pair, [(0, 1), (3, 2)])
    askew = lax.ppermute(out_weight, pair, [(2, 1), (1, 2)])
    near_end = jnp.where(even, last, 0)
    away_end = jnp.where(even, 0, last)
    slots = [
        jnp.where(count == 3, 1, jnp.where(count == 2, 2, 1)),
        jnp.where(count == 1, 2, near_end),
        jnp.where(count == 1, 0, away_end),
    ]
    actives = [count == 3, count >= 2, count >= 1]
    lines = lax.axis_size("zl")

    def along(value, steps):
        return lax.ppermute(value, "zl", [(i, (i + steps) % lines) for i in range(lines)])

    gathered = []
    for c, halos in enumerate(([], near_halo, near_halo + away_halo)):
        slot = slots[c]
        prev_from = jnp.where(slot > 0, slot - 1, jnp.where(even, 4, 3))
        next_from = jnp.where(slot < last, slot + 1, jnp.where(even, 3, 4))
        prev_ok = (slot > 0) | (seq > 0)
        next_ok = (slot < last) | (seq < seq_width - 1)
        info = jnp.stack(
            [v.astype(jnp.int32) for v in (slot, prev_from, next_from, prev_ok, next_ok, actives[c])]
        )
        chunk = attend(info, query, key, value, halos, [])
        ahead, behind = along(chunk, 1), along(chunk, -1)
        gathered.append([chunk, ahead, along(chunk, 2) if c == 0 else along(ahead, 1), behind])

    laid = lay((zh == core).astype(jnp.int32).reshape(1), out_weight, beside, across, askew)
    weight = lax.all_gather(laid, ("y", "x"), axis=0, tiled=True)
    order = jnp.stack([(zl - k) % lines for k in range(lines)]).astype(jnp.int32)
    out = None
    for slot, active, pieces in zip(slots, actives, gathered):
        own, other = project(order, pieces, weight)
        received = lax.ppermute(other, "core", [(0, 1), (1, 0)])
        info = jnp.stack([slot.astype(jnp.int32), active.astype(jnp.int32)])
        out = finish(info, own, received, out_bias, out)
    return out.T


def solution(mesh):
    fine = Mesh(mesh.devices.reshape(4, 2, 4, 2, 4), FSDP + SEQ)
    tiles = P(SEQ, FSDP)
    return jax.shard_map(
        on_device,
        mesh=fine,
        in_specs=(tiles, tiles, tiles, P(SEQ), tiles, P(FSDP)),
        out_specs=P(FSDP, SEQ),
        check_vma=False,
    )
```

time: 511 us -> 193 us (0.38); the launches traced: 504 us -> 193 us
  waiting for transfers between devices: 198 us -> 72.4 us
  other arithmetic: 124 us -> 2.31 us
  local copies, waits for them, and re-layouts: 83.5 us -> 5.18 us
  matrix products: 58 us -> 0 us
  Pallas kernels: 0 us -> 40.1 us
  starting transfers between devices: 25.2 us -> 58.7 us
    unnamed x3 -> x1, waiting for transfers between devices: 184 us -> 0.02 us
    ppermute x4 -> x17, waiting for transfers between devices: 0.01 us -> 72.4 us  [the longest x9 47.2 us: along(): lax.ppermute(value, 'zl', [(i, (i + steps) % lines) for i in range(lines)])]
    dot_general x7 -> x0, matrix products: 58 us -> none  [the longest x3 23.2 us: slot_attend(): jnp.einsum('qhd,khd->hqk', query_slot, key_slot, preferred_element_type=j...]
    concatenate x2, other arithmetic: 59.2 us -> 2.01 us  [the longest x1 1.01 us: on_device(): jnp.concatenate([frame_of(key, away_slot), frame_of(value, away_slot)], a...]
    sub x3 -> x0, other arithmetic: 54.8 us -> none  [slot_attend(): expo = jnp.exp(scores - highest)]
    ppermute x4 -> x17, starting transfers between devices: 18.6 us -> 58.7 us  [the longest x9 39.2 us: along(): lax.ppermute(value, 'zl', [(i, (i + steps) % lines) for i in range(lines)])]
    pallas_call x0 -> x10, Pallas kernels: none -> 40.1 us  [the longest x3 18.6 us: project(): pl.pallas_call(project_body, out_shape=(jax.ShapeDtypeStruct((rows, colum...]
    unnamed x19 -> x16, local copies, waits for them, and re-layouts: 34.4 us -> 3.3 us
  transfers between devices with their start and end apart: 7 -> 18, of which waited for: 2 -> 7; matrix products, arithmetic and copies ran while one was open for 43% -> 2% of each run, Pallas kernels for 0% -> 19%
where the time goes in v1:
time: 193 us
  waiting for transfers between devices  72.4 us (38%)
  starting transfers between devices  58.7 us (30%)
  Pallas kernels  40.1 us (21%)
  between operations  14.3 us (7%)
  local copies, waits for them, and re-layouts  5.18 us (3%)
  other arithmetic  2.31 us (1%)
    ppermute x9, waiting for transfers between devices, along(): lax.ppermute(value, 'zl', [(i, (i + steps) % lines) for i in range(lines)])  47.2 us
    ppermute x9, starting transfers between devices, along(): lax.ppermute(value, 'zl', [(i, (i + steps) % lines) for i in range(lines)])  39.2 us
    pallas_call x3, Pallas kernels, project(): pl.pallas_call(project_body, out_shape=(jax.ShapeDtypeStruct((rows, colum...  18.6 us
    pallas_call x3, Pallas kernels, attend(): pl.pallas_call(functools.partial(attend_body, len(halos)), out_shape=jax....  14.7 us
    ppermute x1, waiting for transfers between devices, on_device(): away_halo = [lax.ppermute(both, SEQ, away)]  11.8 us
    ppermute x1, starting transfers between devices, on_device(): beside = lax.ppermute(out_weight, pair, [(2, 0), (1, 3)])  10.4 us
    ppermute x1, waiting for transfers between devices, on_device(): askew = lax.ppermute(out_weight, pair, [(2, 1), (1, 2)])  8.66 us
    pallas_call x3, Pallas kernels, finish(): pl.pallas_call(finish_body, out_shape=jax.ShapeDtypeStruct((3 * rows, col...  4.92 us
  transfers between devices with their start and end apart: 18, of which 7 were waited for; matrix products, arithmetic and copies ran while one was open for 2% of the time, Pallas kernels for 19%

profile of v1, /device:TPU:9, one launch (start us, length us, event | category | flops | bytes accessed | tf_op | source)
XLA Modules:
  0.0 193.0 jit_solution(15304545625330139630)
XLA Ops:
  6.5 1.3 collective-permute-start.6
  7.8 10.4 %collective-permute-start.5 = (bf16[96,640]{1,0:T(8,128)(2,1)}, bf16[96,640]{1,0:T(8,128)(2,1)S(1)}, u32[]{:S(2)}, u32[]{:S(2)}) collective-permute-start(bf16[96,640]{1,0:T(8,128)(2,1)} %own_ref.1), channel_id=1, source_target_pairs={{32,0},{4,36},{33,1},{5,37},{34,2},{6,38},{35,3},{7,39},{40,8},{12... | collective-permute-start | bytes 368648 | tf_op jit(solution)/shard_map/ppermute | solution.py:211
  18.2 1.9 collective-permute-start.7
  20.2 8.7 %collective-permute-done.7.askew_ref = bf16[96,640]{1,0:T(8,128)(2,1)S(1)} collective-permute-done((bf16[96,640]{1,0:T(8,128)(2,1)}, bf16[96,640]{1,0:T(8,128)(2,1)S(1)}, u32[]{:S(2)}, u32[]{:S(2)}) %collective-permute-start.7) | collective-permute-done | bytes 122912 | tf_op jit(solution)/shard_map/ppermute | solution.py:213
  29.5 1.8 shard_map.65
  32.0 1.6 constant_dynamic-slice_fusion
  36.9 1.9 collective-permute-start.1
  39.0 1.3 copy-done.2
  40.3 2.5 %shard_map.69.x0 = bf16[576,384]{1,0:T(8,128)(2,1)} custom-call(s32[6]{0:T(128)S(1)} %stack.133.info, bf16[1728,384]{1,0:T(8,128)(2,1)S(1)} %copy-done.2, bf16[1728,384]{1,0:T(8,128)(2,1)S(1)} %copy-done, bf16[1728,384]{1,0:T(8,128)(2,1)S(1)} %copy-done.1), custom_call_target="tpu_custom_call" | custom-call | flops 4000000000 | bytes 6000000 | tf_op jit(solution)/shard_map/pallas_call | solution.py:83
  42.9 1.4 collective-permute-start.15
  44.3 1.5 collective-permute-start.14
  45.9 4.8 %collective-permute-done.rest_0_ = bf16[1152,384]{1,0:T(8,128)(2,1)S(1)} collective-permute-done((bf16[1152,384]{1,0:T(8,128)(2,1)}, bf16[1152,384]{1,0:T(8,128)(2,1)S(1)}, u32[]{:S(2)}, u32[]{:S(2)}) %collective-permute-start) | collective-permute-done | bytes 884768 | tf_op jit(solution)/shard_map/ppermute | solution.py:206
  50.7 1.3 copy-done.3
  52.0 2.6 %shard_map.67.x0 = bf16[576,384]{1,0:T(8,128)(2,1)} custom-call(s32[6]{0:T(128)S(1)} %stack.125.info, bf16[1728,384]{1,0:T(8,128)(2,1)S(1)} %copy-done.3, bf16[1728,384]{1,0:T(8,128)(2,1)S(1)} %copy-done, bf16[1728,384]{1,0:T(8,128)(2,1)S(1)} %copy-done.1, bf16[1152,384]{1,0:T(8,128)(2,1)S(1)} %collective-permute-done.rest_0_), custom_call_target="tpu_custom_call" | custom-call | flops 4000000000 | bytes 6000000 | tf_op jit(solution)/shard_map/pallas_call | solution.py:83
  54.7 1.4 collective-permute-start.9
  56.0 11.8 %collective-permute-done.1.rest_1_ = bf16[1152,384]{1,0:T(8,128)(2,1)} collective-permute-done((bf16[1152,384]{1,0:T(8,128)(2,1)}, bf16[1152,384]{1,0:T(8,128)(2,1)}, u32[]{:S(2)}, u32[]{:S(2)}) %collective-permute-start.1) | collective-permute-done | bytes 884768 | tf_op jit(solution)/shard_map/ppermute | solution.py:208
  67.8 9.5 %shard_map.64.x0 = bf16[576,384]{1,0:T(8,128)(2,1)} custom-call(s32[6]{0:T(128)S(1)} %stack.116.info, bf16[1728,384]{1,0:T(8,128)(2,1)S(1)} %copy-done.3, bf16[1728,384]{1,0:T(8,128)(2,1)S(1)} %copy-done, bf16[1728,384]{1,0:T(8,128)(2,1)S(1)} %copy-done.1, bf16[1152,384]{1,0:T(8,128)(2,1)S(1)} %collective-permute-done.rest_0_, ...), custom_call_target="tpu_custom_call" | custom-call | flops 4000000000 | bytes 6000000 | tf_op jit(solution)/shard_map/pallas_call | solution.py:83
  77.3 13.0 %collective-permute-start.2 = (bf16[576,384]{1,0:T(8,128)(2,1)}, bf16[576,384]{1,0:T(8,128)(2,1)S(1)}, u32[]{:S(2)}, u32[]{:S(2)}) collective-permute-start(bf16[576,384]{1,0:T(8,128)(2,1)} %shard_map.64.x0), channel_id=1, source_target_pairs={{0,64},{64,128},{128,192},{192,0},{1,65},{65,129},{129,193},{193,1... | collective-permute-start | bytes 1327112 | tf_op jit(solution)/shard_map/ppermute | solution.py:225
  90.3 9.5 %collective-permute-start.13 = (bf16[576,384]{1,0:T(8,128)(2,1)}, bf16[576,384]{1,0:T(8,128)(2,1)S(1)}, u32[]{:S(2)}, u32[]{:S(2)}) collective-permute-start(bf16[576,384]{1,0:T(8,128)(2,1)} %shard_map.69.x0), channel_id=1, source_target_pairs={{0,64},{64,128},{128,192},{192,0},{1,65},{65,129},{129,193},{193,1... | collective-permute-start | bytes 1327112 | tf_op jit(solution)/shard_map/ppermute | solution.py:225
  99.9 5.9 %collective-permute-done.9.x1 = bf16[576,384]{1,0:T(8,128)(2,1)} collective-permute-done((bf16[576,384]{1,0:T(8,128)(2,1)}, bf16[576,384]{1,0:T(8,128)(2,1)}, u32[]{:S(2)}, u32[]{:S(2)}) %collective-permute-start.9) | collective-permute-done | bytes 442400 | tf_op jit(solution)/shard_map/ppermute | solution.py:225
  105.8 10.8 %collective-permute-start.10 = (bf16[576,384]{1,0:T(8,128)(2,1)}, bf16[576,384]{1,0:T(8,128)(2,1)S(1)}, u32[]{:S(2)}, u32[]{:S(2)}) collective-permute-start(bf16[576,384]{1,0:T(8,128)(2,1)} %collective-permute-done.9.x1), channel_id=1, source_target_pairs={{0,64},{64,128},{128,192},{192,0},{1,65},{65,129},{129,193},{193,1... | collective-permute-start | bytes 1327112 | tf_op jit(solution)/shard_map/ppermute | solution.py:225
  116.6 22.2 %collective-permute-done.14.x2 = bf16[576,384]{1,0:T(8,128)(2,1)} collective-permute-done((bf16[576,384]{1,0:T(8,128)(2,1)}, bf16[576,384]{1,0:T(8,128)(2,1)}, u32[]{:S(2)}, u32[]{:S(2)}) %collective-permute-start.14) | collective-permute-done | bytes 442400 | tf_op jit(solution)/shard_map/ppermute | solution.py:225
  138.9 1.5 collective-permute-start.3
  140.4 6.3 %shard_map.70 = (f32[576,640]{1,0:T(8,128)S(1)}, bf16[576,640]{1,0:T(8,128)(2,1)S(1)}) custom-call(s32[4]{0:T(128)S(1)} %pad_add_fusion.1.info, bf16[576,384]{1,0:T(8,128)(2,1)} %shard_map.69.x0, bf16[576,384]{1,0:T(8,128)(2,1)S(1)} %collective-permute-done.13.x1, bf16[576,384]{1,0:T(8,128)(2,1)} %collective-permute-done.14.x2, ...), custom_call_target="tpu_custom_call" | custom-call | flops 2264924160 | bytes 5701632 | tf_op jit(solution)/shard_map/pallas_call | solution.py:123
  146.8 1.4 collective-permute-start.16
  148.2 9.4 %collective-permute-done.11.x3 = bf16[576,384]{1,0:T(8,128)(2,1)S(1)} collective-permute-done((bf16[576,384]{1,0:T(8,128)(2,1)}, bf16[576,384]{1,0:T(8,128)(2,1)S(1)}, u32[]{:S(2)}, u32[]{:S(2)}) %collective-permute-start.11) | collective-permute-done | bytes 442400 | tf_op jit(solution)/shard_map/ppermute | solution.py:225
  157.6 6.2 %shard_map.68 = (f32[576,640]{1,0:T(8,128)S(1)}, bf16[576,640]{1,0:T(8,128)(2,1)S(1)}) custom-call(s32[4]{0:T(128)S(1)} %pad_add_fusion.1.info, bf16[576,384]{1,0:T(8,128)(2,1)} %shard_map.67.x0, bf16[576,384]{1,0:T(8,128)(2,1)} %collective-permute-done.9.x1, bf16[576,384]{1,0:T(8,128)(2,1)S(1)} %collective-permute-done.10.x2, ...), custom_call_target="tpu_custom_call" | custom-call | flops 2264924160 | bytes 5701632 | tf_op jit(solution)/shard_map/pallas_call | solution.py:123
  164.7 9.6 %collective-permute-done.4.x3 = bf16[576,384]{1,0:T(8,128)(2,1)S(1)} collective-permute-done((bf16[576,384]{1,0:T(8,128)(2,1)}, bf16[576,384]{1,0:T(8,128)(2,1)S(1)}, u32[]{:S(2)}, u32[]{:S(2)}) %collective-permute-start.4) | collective-permute-done | bytes 442400 | tf_op jit(solution)/shard_map/ppermute | solution.py:225
  174.3 6.1 %shard_map.66 = (f32[576,640]{1,0:T(8,128)S(1)}, bf16[576,640]{1,0:T(8,128)(2,1)S(1)}) custom-call(s32[4]{0:T(128)S(1)} %pad_add_fusion.1.info, bf16[576,384]{1,0:T(8,128)(2,1)} %shard_map.64.x0, bf16[576,384]{1,0:T(8,128)(2,1)S(1)} %collective-permute-done.2.x1, bf16[576,384]{1,0:T(8,128)(2,1)S(1)} %collective-permute-done.3.x2, ...), custom_call_target="tpu_custom_call" | custom-call | flops 2264924160 | bytes 5701632 | tf_op jit(solution)/shard_map/pallas_call | solution.py:123
  181.2 1.6 shard_map.71.rest_0_
  182.9 1.6 shard_map.72.rest_0_
  184.5 1.6 shard_map.73
  (42 shorter events, 5.9 us)
Async XLA Ops:
  6.5 133.9 %all-gather.2.cloned.1.call-start = ((), (), s32[]{:S(2)}) async-start(), calls=%async_computation | async-start | bytes 4177920 | tf_op jit(solution)/shard_map/all_gather | solution.py:242
  6.5 13.6 %collective-permute-start.6 = (bf16[96,640]{1,0:T(8,128)(2,1)}, bf16[96,640]{1,0:T(8,128)(2,1)S(1)}, u32[]{:S(2)}, u32[]{:S(2)}) collective-permute-start(bf16[96,640]{1,0:T(8,128)(2,1)} %own_ref.1), channel_id=1, source_target_pairs={{0,4},{36,32},{1,5},{37,33},{2,6},{38,34},{3,7},{39,35},{8,12},{44... | collective-permute-start | bytes 368648 | tf_op jit(solution)/shard_map/ppermute | solution.py:212
  7.8 12.4 %collective-permute-start.5 = (bf16[96,640]{1,0:T(8,128)(2,1)}, bf16[96,640]{1,0:T(8,128)(2,1)S(1)}, u32[]{:S(2)}, u32[]{:S(2)}) collective-permute-start(bf16[96,640]{1,0:T(8,128)(2,1)} %own_ref.1), channel_id=1, source_target_pairs={{32,0},{4,36},{33,1},{5,37},{34,2},{6,38},{35,3},{7,39},{40,8},{12... | collective-permute-start | bytes 368648 | tf_op jit(solution)/shard_map/ppermute | solution.py:211
  18.2 10.6 %collective-permute-start.7 = (bf16[96,640]{1,0:T(8,128)(2,1)}, bf16[96,640]{1,0:T(8,128)(2,1)S(1)}, u32[]{:S(2)}, u32[]{:S(2)}) collective-permute-start(bf16[96,640]{1,0:T(8,128)(2,1)} %own_ref.1), channel_id=1, source_target_pairs={{32,4},{4,32},{33,5},{5,33},{34,6},{6,34},{35,7},{7,35},{40,12},{1... | collective-permute-start | bytes 368648 | tf_op jit(solution)/shard_map/ppermute | solution.py:213
  20.2 8.7 %copy-start.4 = (bf16[96,640]{1,0:T(8,128)(2,1)}, bf16[96,640]{1,0:T(8,128)(2,1)S(1)}, u32[]{:S(2)}) copy-start(bf16[96,640]{1,0:T(8,128)(2,1)S(1)} %collective-permute-done.6.across_ref) | copy-start | bytes 368644
  20.2 8.7 %copy-start.5 = (bf16[96,640]{1,0:T(8,128)(2,1)}, bf16[96,640]{1,0:T(8,128)(2,1)S(1)}, u32[]{:S(2)}) copy-start(bf16[96,640]{1,0:T(8,128)(2,1)S(1)} %collective-permute-done.5.beside_ref) | copy-start | bytes 368644
  28.9 0.6 copy-start.6
  33.7 5.3 %copy-start = (bf16[1728,384]{1,0:T(8,128)(2,1)S(1)}, bf16[1728,384]{1,0:T(8,128)(2,1)}, u32[]{:S(2)}) copy-start(bf16[1728,384]{1,0:T(8,128)(2,1)} %k_ref.5) | copy-start | bytes 3981316
  33.7 5.3 %copy-start.1 = (bf16[1728,384]{1,0:T(8,128)(2,1)S(1)}, bf16[1728,384]{1,0:T(8,128)(2,1)}, u32[]{:S(2)}) copy-start(bf16[1728,384]{1,0:T(8,128)(2,1)} %v_ref.5) | copy-start | bytes 3981316
  34.7 16.0 %collective-permute-start = (bf16[1152,384]{1,0:T(8,128)(2,1)}, bf16[1152,384]{1,0:T(8,128)(2,1)S(1)}, u32[]{:S(2)}, u32[]{:S(2)}) collective-permute-start(bf16[1152,384]{1,0:T(8,128)(2,1)} %pad_maximum_fusion), channel_id=1, source_target_pairs={{0,1},{1,0},{2,3},{3,2},{4,5},{5,4},{6,7},{7,6},{8,9},{9,8},{10,11... | collective-permute-start | bytes 2654216 | tf_op jit(solution)/shard_map/ppermute | solution.py:206
  36.9 30.9 %collective-permute-start.1 = (bf16[1152,384]{1,0:T(8,128)(2,1)}, bf16[1152,384]{1,0:T(8,128)(2,1)}, u32[]{:S(2)}, u32[]{:S(2)}) collective-permute-start(bf16[1152,384]{1,0:T(8,128)(2,1)} %pad_maximum_fusion.1), channel_id=1, source_target_pairs={{1,2},{2,1},{3,4},{4,3},{5,6},{6,5},{7,8},{8,7},{9,10},{10,9},{11,... | collective-permute-start | bytes 2654216 | tf_op jit(solution)/shard_map/ppermute | solution.py:208
  39.0 1.3 copy-start.2
  42.9 57.0 %collective-permute-start.15 = (bf16[576,384]{1,0:T(8,128)(2,1)}, bf16[576,384]{1,0:T(8,128)(2,1)}, u32[]{:S(2)}, u32[]{:S(2)}) collective-permute-start(bf16[576,384]{1,0:T(8,128)(2,1)} %shard_map.69.x0), channel_id=1, source_target_pairs={{0,192},{64,0},{128,64},{192,128},{1,193},{65,1},{129,65},{193,129... | collective-permute-start | bytes 1327112 | tf_op jit(solution)/shard_map/ppermute | solution.py:225
  44.3 94.6 %collective-permute-start.14 = (bf16[576,384]{1,0:T(8,128)(2,1)}, bf16[576,384]{1,0:T(8,128)(2,1)}, u32[]{:S(2)}, u32[]{:S(2)}) collective-permute-start(bf16[576,384]{1,0:T(8,128)(2,1)} %shard_map.69.x0), channel_id=1, source_target_pairs={{0,128},{64,192},{128,0},{192,64},{1,129},{65,193},{129,1},{193,65... | collective-permute-start | bytes 1327112 | tf_op jit(solution)/shard_map/ppermute | solution.py:225
  50.7 1.3 copy-start.3
  54.7 51.1 %collective-permute-start.9 = (bf16[576,384]{1,0:T(8,128)(2,1)}, bf16[576,384]{1,0:T(8,128)(2,1)}, u32[]{:S(2)}, u32[]{:S(2)}) collective-permute-start(bf16[576,384]{1,0:T(8,128)(2,1)} %shard_map.67.x0), channel_id=1, source_target_pairs={{0,64},{64,128},{128,192},{192,0},{1,65},{65,129},{129,193},{193,1... | collective-permute-start | bytes 1327112 | tf_op jit(solution)/shard_map/ppermute | solution.py:225
  77.3 61.6 %collective-permute-start.2 = (bf16[576,384]{1,0:T(8,128)(2,1)}, bf16[576,384]{1,0:T(8,128)(2,1)S(1)}, u32[]{:S(2)}, u32[]{:S(2)}) collective-permute-start(bf16[576,384]{1,0:T(8,128)(2,1)} %shard_map.64.x0), channel_id=1, source_target_pairs={{0,64},{64,128},{128,192},{192,0},{1,65},{65,129},{129,193},{193,1... | collective-permute-start | bytes 1327112 | tf_op jit(solution)/shard_map/ppermute | solution.py:225
  90.3 50.1 %collective-permute-start.13 = (bf16[576,384]{1,0:T(8,128)(2,1)}, bf16[576,384]{1,0:T(8,128)(2,1)S(1)}, u32[]{:S(2)}, u32[]{:S(2)}) collective-permute-start(bf16[576,384]{1,0:T(8,128)(2,1)} %shard_map.69.x0), channel_id=1, source_target_pairs={{0,64},{64,128},{128,192},{192,0},{1,65},{65,129},{129,193},{193,1... | collective-permute-start | bytes 1327112 | tf_op jit(solution)/shard_map/ppermute | solution.py:225
  99.9 57.7 %collective-permute-start.11 = (bf16[576,384]{1,0:T(8,128)(2,1)}, bf16[576,384]{1,0:T(8,128)(2,1)S(1)}, u32[]{:S(2)}, u32[]{:S(2)}) collective-permute-start(bf16[576,384]{1,0:T(8,128)(2,1)} %shard_map.67.x0), channel_id=1, source_target_pairs={{0,192},{64,0},{128,64},{192,128},{1,193},{65,1},{129,65},{193,129... | collective-permute-start | bytes 1327112 | tf_op jit(solution)/shard_map/ppermute | solution.py:225
  105.8 51.8 %collective-permute-start.10 = (bf16[576,384]{1,0:T(8,128)(2,1)}, bf16[576,384]{1,0:T(8,128)(2,1)S(1)}, u32[]{:S(2)}, u32[]{:S(2)}) collective-permute-start(bf16[576,384]{1,0:T(8,128)(2,1)} %collective-permute-done.9.x1), channel_id=1, source_target_pairs={{0,64},{64,128},{128,192},{192,0},{1,65},{65,129},{129,193},{193,1... | collective-permute-start | bytes 1327112 | tf_op jit(solution)/shard_map/ppermute | solution.py:225
  138.9 35.5 %collective-permute-start.4 = (bf16[576,384]{1,0:T(8,128)(2,1)}, bf16[576,384]{1,0:T(8,128)(2,1)S(1)}, u32[]{:S(2)}, u32[]{:S(2)}) collective-permute-start(bf16[576,384]{1,0:T(8,128)(2,1)} %shard_map.64.x0), channel_id=1, source_target_pairs={{0,192},{64,0},{128,64},{192,128},{1,193},{65,1},{129,65},{193,129... | collective-permute-start | bytes 1327112 | tf_op jit(solution)/shard_map/ppermute | solution.py:225
  138.9 35.4 %collective-permute-start.3 = (bf16[576,384]{1,0:T(8,128)(2,1)S(1)}, bf16[576,384]{1,0:T(8,128)(2,1)S(1)}, u32[]{:S(2)}, u32[]{:S(2)}) collective-permute-start(bf16[576,384]{1,0:T(8,128)(2,1)S(1)} %collective-permute-done.2.x1), channel_id=1, source_target_pairs={{0,64},{64,128},{128,192},{192,0},{1,65},{65,129},{129,193},{193,1... | collective-permute-start | bytes 1327112 | tf_op jit(solution)/shard_map/ppermute | solution.py:225
  146.8 34.4 %collective-permute-start.16 = (bf16[576,640]{1,0:T(8,128)(2,1)S(1)}, bf16[576,640]{1,0:T(8,128)(2,1)S(1)}, u32[]{:S(2)}, u32[]{:S(2)}) collective-permute-start(bf16[576,640]{1,0:T(8,128)(2,1)S(1)} %get-tuple-element.16), channel_id=1, source_target_pairs={{0,32},{32,0},{1,33},{33,1},{2,34},{34,2},{3,35},{35,3},{4,36},{36... | collective-permute-start | bytes 2211848 | tf_op jit(solution)/shard_map/ppermute | solution.py:247
  163.8 17.2 %copy-start.7 = (f32[640]{0:T(1024)S(1)}, f32[640]{0:T(1024)}, u32[]{:S(2)}) copy-start(f32[640]{0:T(1024)} %param.11) | copy-start | bytes 7684
  163.8 19.0 %collective-permute-start.12 = (bf16[576,640]{1,0:T(8,128)(2,1)S(1)}, bf16[576,640]{1,0:T(8,128)(2,1)S(1)}, u32[]{:S(2)}, u32[]{:S(2)}) collective-permute-start(bf16[576,640]{1,0:T(8,128)(2,1)S(1)} %get-tuple-element.14), channel_id=1, source_target_pairs={{0,32},{32,0},{1,33},{33,1},{2,34},{34,2},{3,35},{35,3},{4,36},{36... | collective-permute-start | bytes 2211848 | tf_op jit(solution)/shard_map/ppermute | solution.py:247
  180.4 4.1 %collective-permute-start.8 = (bf16[576,640]{1,0:T(8,128)(2,1)S(1)}, bf16[576,640]{1,0:T(8,128)(2,1)S(1)}, u32[]{:S(2)}, u32[]{:S(2)}) collective-permute-start(bf16[576,640]{1,0:T(8,128)(2,1)S(1)} %get-tuple-element.12), channel_id=1, source_target_pairs={{0,32},{32,0},{1,33},{33,1},{2,34},{34,2},{3,35},{35,3},{4,36},{36... | collective-permute-start | bytes 2211848 | tf_op jit(solution)/shard_map/ppermute | solution.py:247
Sparse Core Ops, SparseCore 0:
  31.5 67.8 all-gather.1

commit v2 on v1

v2 whole, which is shorter than its diff:
```python
import functools

import jax
import jax.numpy as jnp
from jax import lax
from jax.experimental import pallas as pl
from jax.experimental.pallas import tpu as pltpu
from jax.sharding import Mesh
from jax.sharding import PartitionSpec as P

HEAD = 128
TILE = 192
FRAME = 576
LN2 = 0.6931471805599453
SCALE = HEAD**-0.5 / LN2
FAR = 1e30
SEQ = ("y", "zh", "x")
FSDP = ("zl", "core")
VMEM = 48 * 1024 * 1024
FREE = pl.CostEstimate(flops=0, bytes_accessed=0, transcendentals=0)


def attend_body(halo_total, info, q_ref, k_ref, v_ref, *rest):
    halos, (o_ref, kbuf, vbuf) = rest[:halo_total], rest[-3:]
    slot, prev_from, next_from, prev_ok, next_ok, active = (info[i] for i in range(6))

    @pl.when(pl.program_id(0) == 0)
    def _():
        vbuf[:, HEAD:] = jnp.ones((3 * FRAME, HEAD), jnp.bfloat16)

    @pl.when(active == 0)
    def _():
        o_ref[...] = jnp.zeros_like(o_ref)

    def fill(place, source):
        rows = pl.ds(place * FRAME, FRAME)

        @pl.when(source < 3)
        def _():
            local = pl.ds(pl.multiple_of(jnp.clip(source, 0, 2) * FRAME, FRAME), FRAME)
            kbuf[rows, :] = k_ref[local, :]
            vbuf[rows, :HEAD] = v_ref[local, :]

        for i in range(halo_total // 2):

            @pl.when(source == 3 + i)
            def _():
                kbuf[rows, :] = halos[2 * i][...]
                vbuf[rows, :HEAD] = halos[2 * i + 1][...]

    @pl.when(active == 1)
    def _():
        fill(0, prev_from)
        fill(1, slot)
        fill(2, next_from)
        off = [jnp.where(prev_ok == 1, 0.0, FAR), jnp.float32(0.0), jnp.where(next_ok == 1, 0.0, FAR)]
        for w in range(3):
            low, high = max(0, w - 1) * TILE, min(3, w + 2) * TILE
            q = q_ref[pl.ds(pl.multiple_of(slot * FRAME + w * TILE, TILE), TILE), :]
            scores, tops = [], []
            for f in range(3):
                keys = kbuf[f * FRAME + low : f * FRAME + high, :]
                s = lax.dot_general(q, keys, (((1,), (1,)), ((), ())), preferred_element_type=jnp.float32)
                scores.append(s)
                tops.append(jnp.max(s, axis=1, keepdims=True) * SCALE - off[f])
            top = jnp.maximum(jnp.maximum(tops[0], tops[1]), tops[2])
            total = None
            for f in range(3):
                p = jnp.exp2(scores[f] * SCALE - (top + off[f])).astype(jnp.bfloat16)
                part = jnp.dot(
                    p, vbuf[f * FRAME + low : f * FRAME + high, :], preferred_element_type=jnp.float32
                )
                total = part if total is None else total + part
            o_ref[w * TILE : (w + 1) * TILE, :] = (total[:, :HEAD] / total[:, HEAD:]).astype(jnp.bfloat16)


def attend(info, query, key, value, halos, after):
    rows, width = query.shape
    heads = width // HEAD
    column = lambda h, info: (0, h)
    whole = pl.BlockSpec((rows, HEAD), column)
    one = pl.BlockSpec((FRAME, HEAD), column)
    where = [pl.BlockSpec((FRAME, HEAD), lambda h, info, r=r: (r, h)) for _, r in halos]
    return pl.pallas_call(
        functools.partial(attend_body, len(halos)),
        out_shape=jax.ShapeDtypeStruct((FRAME, width), jnp.bfloat16),
        grid_spec=pltpu.PrefetchScalarGridSpec(
            num_scalar_prefetch=1,
            grid=(heads,),
            in_specs=[whole] * 3 + where + [pl.BlockSpec(memory_space=pl.ANY)] * len(after),
            out_specs=one,
            scratch_shapes=[
                pltpu.VMEM((3 * FRAME, HEAD), jnp.bfloat16),
                pltpu.VMEM((3 * FRAME, 2 * HEAD), jnp.bfloat16),
            ],
        ),
        compiler_params=pltpu.CompilerParams(vmem_limit_bytes=VMEM),
        cost_estimate=FREE,
    )(info, query, key, value, *[array for array, _ in halos], *after)


def share(info, at, pieces, w_ref):
    total = None
    for k, piece in enumerate(pieces):
        width = piece.shape[1]
        rows = pl.ds(pl.multiple_of(info[at + k] * width, width), width)
        part = jnp.dot(piece[...], w_ref[rows, :], preferred_element_type=jnp.float32)
        total = part if total is None else total + part
    return total


def hand_out(total, mine_ref, other_ref):
    @pl.when(pl.program_id(0) == 0)
    def _():
        other_ref[...] = total.astype(jnp.bfloat16)

    @pl.when(pl.program_id(0) == 1)
    def _():
        mine_ref[...] = total


def project_body(split, info, *refs):
    groups, at = [], 0
    for size in split:
        groups.append(refs[at : at + size])
        at += size
    w_ref, outs = refs[at], refs[at + 1 :]
    hand_out(share(info, 0, groups[0], w_ref), outs[0], outs[1])
    if len(groups) == 2:
        outs[2][...] = share(info, len(groups[0]), groups[1], w_ref)


def project_last_body(info, piece, w_ref, so_far, mine_ref, other_ref):
    hand_out(share(info, 1, [piece], w_ref) + so_far[...], mine_ref, other_ref)


def project(order, whole, part, weight, so_far=None):
    rows, width = whole[0].shape
    depth, both = weight.shape
    columns = both // 2
    fixed = lambda j, info: (0, 0)
    side = lambda j, info: (0, 1 - j)
    block = pl.BlockSpec((rows, columns), side)
    out_shape = [
        jax.ShapeDtypeStruct((rows, columns), jnp.float32),
        jax.ShapeDtypeStruct((rows, columns), jnp.bfloat16),
    ]
    out_specs = [pl.BlockSpec((rows, columns), fixed)] * 2
    in_specs = [pl.BlockSpec((rows, width), fixed)] * (len(whole) + len(part))
    if part:
        out_shape.append(jax.ShapeDtypeStruct((rows, both), jnp.float32))
        out_specs.append(block)
    if so_far is None:
        body, more = functools.partial(project_body, [len(g) for g in (whole, part) if g]), []
        in_specs.append(pl.BlockSpec((depth, columns), side))
    else:
        body, more = project_last_body, [so_far]
        in_specs += [pl.BlockSpec((width, columns), lambda j, info: (info[0], 1 - j)), block]
    return pl.pallas_call(
        body,
        out_shape=out_shape,
        grid_spec=pltpu.PrefetchScalarGridSpec(
            num_scalar_prefetch=1, grid=(2,), in_specs=in_specs, out_specs=out_specs
        ),
        compiler_params=pltpu.CompilerParams(vmem_limit_bytes=VMEM),
        cost_estimate=FREE,
    )(order, *whole, *part, weight, *more)


def finish_body(total, info, *refs):
    bias_ref, out_ref = refs[2 * total], refs[-1]
    for i in range(total):

        @pl.when(pl.program_id(0) == i)
        def _():
            value = refs[2 * i][...] + refs[2 * i + 1][...].astype(jnp.float32) + bias_ref[...]
            out_ref[...] = jnp.where(info[total + i] == 1, value, 0.0).astype(jnp.bfloat16)


def finish(info, parts, bias, out):
    rows, columns = parts[0].shape
    total = len(parts) // 2
    whole = pl.BlockSpec((rows, columns), lambda j, info: (0, 0))
    extra = [] if out is None else [out]
    return pl.pallas_call(
        functools.partial(finish_body, total),
        out_shape=jax.ShapeDtypeStruct((3 * rows, columns), jnp.bfloat16),
        grid_spec=pltpu.PrefetchScalarGridSpec(
            num_scalar_prefetch=1,
            grid=(total,),
            in_specs=[whole] * len(parts)
            + [pl.BlockSpec((1, columns), lambda j, info: (0, 0))]
            + [pl.BlockSpec(memory_space=pl.ANY)] * len(extra),
            out_specs=pl.BlockSpec((rows, columns), lambda j, info: (info[j], 0)),
        ),
        input_output_aliases={2 + len(parts): 0} if extra else {},
        compiler_params=pltpu.CompilerParams(vmem_limit_bytes=VMEM),
        cost_estimate=FREE,
    )(info, *parts, bias.reshape(1, columns), *extra)


def pack_body(info, k0_ref, v0_ref, k1_ref, v1_ref, near_ref, key_ref, value_ref):
    near_ref[:FRAME, :] = k0_ref[...]
    near_ref[FRAME:, :] = v0_ref[...]
    key_ref[...] = k1_ref[...]
    value_ref[...] = v1_ref[...]


def pack(info, key, value):
    width = key.shape[1]
    frames = [pl.BlockSpec((FRAME, width), lambda i, info, c=c: (info[c], 0)) for c in (0, 0, 1, 1)]
    heights = (2 * FRAME, FRAME, FRAME)
    return pl.pallas_call(
        pack_body,
        out_shape=[jax.ShapeDtypeStruct((rows, width), key.dtype) for rows in heights],
        grid_spec=pltpu.PrefetchScalarGridSpec(
            num_scalar_prefetch=1,
            grid=(1,),
            in_specs=frames,
            out_specs=[pl.BlockSpec((rows, width), lambda i, info: (0, 0)) for rows in heights],
        ),
        compiler_params=pltpu.CompilerParams(vmem_limit_bytes=VMEM),
        cost_estimate=FREE,
    )(info, key, value, key, value)


def lay_body(info, own_ref, beside_ref, across_ref, askew_ref, *rest):
    out_ref = rest[-1]
    columns = own_ref.shape[1]
    home = info[0] == 1
    out_ref[:, :columns] = jnp.where(home, own_ref[...], across_ref[...])
    out_ref[:, columns:] = jnp.where(home, beside_ref[...], askew_ref[...])


def lay(info, own, beside, across, askew, after):
    rows, columns = own.shape
    vmem = pl.BlockSpec(memory_space=pltpu.VMEM)
    return pl.pallas_call(
        lay_body,
        out_shape=jax.ShapeDtypeStruct((rows, 2 * columns), own.dtype),
        in_specs=[pl.BlockSpec(memory_space=pltpu.SMEM)] + [vmem] * 4
        + [pl.BlockSpec(memory_space=pl.ANY)] * len(after),
        out_specs=vmem,
        cost_estimate=FREE,
    )(info, own, beside, across, askew, *after)


def on_device(query, key, value, slab_counts, out_weight, out_bias):
    count = slab_counts[0]
    x, zh, zl, core = (lax.axis_index(name) for name in ("x", "zh", "zl", "core"))
    seq = lax.axis_index(SEQ)
    seq_width, row = lax.axis_size(SEQ), lax.axis_size("x")
    even = x % 2 == 0
    last = count - 1

    near_slot = jnp.where(even, last, 0)
    away_slot = jnp.where(even, 0, last)
    near_pack, away_key, away_value = pack(jnp.stack([near_slot, away_slot]), key, value)
    near = lax.ppermute(near_pack, "x", [(0, 1), (1, 0), (2, 3), (3, 2)])
    key_round = lax.ppermute(away_key, "x", [(0, 3), (3, 0), (1, 2), (2, 1)])
    value_side = lax.ppermute(away_value, "x", [(0, 1), (3, 2)])
    value_inner = lax.ppermute(away_value, "x", [(1, 2), (2, 1)])

    def across_rows(value, up, down):
        rows = range(seq_width // row - 1)
        pairs = [(r * row + up, (r + 1) * row + up) for r in rows]
        pairs += [((r + 1) * row + down, r * row + down) for r in rows]
        return lax.ppermute(value, SEQ, pairs)

    key_far = across_rows(key_round, 0, 3)
    value_far = lax.ppermute(across_rows(value_side, 2, 1), "x", [(2, 0), (1, 3)])
    near_halo = [(near, 0), (near, 1)]
    inner_halo = [(key_round, 0), (value_inner, 0)]
    far_halo = [(key_far, 0), (value_far, 0)]

    slots = [
        jnp.where(count == 3, 1, jnp.where(count == 2, 2, 1)),
        jnp.where(count == 1, 2, near_slot),
        jnp.where(count == 1, 0, away_slot),
    ]
    actives = [count == 3, count >= 2, count >= 1]
    away_from = jnp.where((x == 1) | (x == 2), 4, 5)

    def frame(c, halos, after):
        slot = slots[c]
        prev_from = jnp.where(slot > 0, slot - 1, jnp.where(even, away_from, 3))
        next_from = jnp.where(slot < last, slot + 1, jnp.where(even, 3, away_from))
        prev_ok = (slot > 0) | (seq > 0)
        next_ok = (slot < last) | (seq < seq_width - 1)
        info = jnp.stack(
            [v.astype(jnp.int32) for v in (slot, prev_from, next_from, prev_ok, next_ok, actives[c])]
        )
        return attend(info, query, key, value, halos, after)

    lines = lax.axis_size("zl")

    def along(value, steps):
        return lax.ppermute(value, "zl", [(i, (i + steps) % lines) for i in range(lines)])

    a = frame(0, [], [])
    a1, a3 = along(a, 1), along(a, -1)
    b = frame(1, near_halo, [])
    b1, b3 = along(b, 1), along(b, -1)
    c = frame(2, near_halo + inner_halo + far_halo, [a1, a3, b1, b3])
    a2, b2 = along(a1, 1), along(b1, 1)
    c1, c3 = along(c, 1), along(c, -1)
    c2 = along(c1, 1)

    pair = ("core", "zh")
    beside = lax.ppermute(out_weight, pair, [(2, 0), (1, 3)])
    across = lax.ppermute(out_weight, pair, [(0, 1), (3, 2)])
    askew = lax.ppermute(out_weight, pair, [(2, 1), (1, 2)])
    home = (zh == core).astype(jnp.int32).reshape(1)
    laid = lay(home, out_weight, beside, across, askew, [key_round, value_side, near, a1])
    weight = lax.all_gather(laid, ("y", "x"), axis=0, tiled=True)

    order = [((zl - k) % lines).astype(jnp.int32) for k in range(lines)]

    def swap(value):
        return lax.ppermute(value, "core", [(0, 1), (1, 0)])

    def put(indices, parts, out):
        info = jnp.stack([v[i].astype(jnp.int32) for v in (slots, actives) for i in indices])
        return finish(info, parts, out_bias, out)

    own_a, other_a = project(jnp.stack(order), [a, a1, a2, a3], [], weight)
    out = put([0], [own_a, swap(other_a)], None)
    turns = jnp.stack(order + [order[0], order[1], order[3]])
    own_b, other_b, so_far = project(turns, [b, b1, b2, b3], [c, c1, c3], weight)
    own_c, other_c = project(jnp.stack([order[2], jnp.zeros_like(order[2])]), [c2], [], weight, so_far)
    out = put([1, 2], [own_b, swap(other_b), own_c, swap(other_c)], out)
    return out.T


def solution(mesh):
    fine = Mesh(mesh.devices.reshape(4, 2, 4, 2, 4), FSDP + SEQ)
    tiles = P(SEQ, FSDP)
    return jax.shard_map(
        on_device,
        mesh=fine,
        in_specs=(tiles, tiles, tiles, P(SEQ), tiles, P(FSDP)),
        out_specs=P(FSDP, SEQ),
        check_vma=False,
    )
```

time: 193 us -> 190 us (0.984)
  the two profiles are of different devices: /device:TPU:9 before, /device:TPU:19 now
where the time goes in v2:
time: 190 us
  waiting for transfers between devices  81.9 us (43%)
  starting transfers between devices  43.1 us (23%)
  Pallas kernels  41 us (22%)
  between operations  14.3 us (8%)
  local copies, waits for them, and re-layouts  9.04 us (5%)
    ppermute x9, waiting for transfers between devices, along(): lax.ppermute(value, 'zl', [(i, (i + steps) % lines) for i in range(lines)])  57 us
    pallas_call x3, Pallas kernels, project(): pl.pallas_call(body, out_shape=out_shape, grid_spec=pltpu.PrefetchScalarG...  19.5 us
    ppermute x9, starting transfers between devices, along(): lax.ppermute(value, 'zl', [(i, (i + steps) % lines) for i in range(lines)])  18.3 us
    ppermute x1, waiting for transfers between devices, on_device(): across = lax.ppermute(out_weight, pair, [(0, 1), (3, 2)])  17.8 us
    pallas_call x3, Pallas kernels, attend(): pl.pallas_call(functools.partial(attend_body, len(halos)), out_shape=jax....  14.2 us
    unnamed x24, local copies, waits for them, and re-layouts  8.7 us
    ppermute x1, starting transfers between devices, on_device(): askew = lax.ppermute(out_weight, pair, [(2, 1), (1, 2)])  5.96 us
    ppermute x1, waiting for transfers between devices, on_device(): askew = lax.ppermute(out_weight, pair, [(2, 1), (1, 2)])  4.53 us
  transfers between devices with their start and end apart: 23, of which 11 were waited for; matrix products, arithmetic and copies ran while one was open for 0% of the time, Pallas kernels for 19%

profile of v2, /device:TPU:19, one launch (start us, length us, event | category | flops | bytes accessed | tf_op | source)
XLA Modules:
  0.0 189.7 jit_solution(15089041747600325422)
XLA Ops:
  9.9 1.9 %shard_map.64 = (bf16[1152,384]{1,0:T(8,128)(2,1)}, bf16[576,384]{1,0:T(8,128)(2,1)}, bf16[576,384]{1,0:T(8,128)(2,1)}) custom-call(s32[2]{0:T(128)S(1)} %pad_add_fusion.1.info, bf16[1728,384]{1,0:T(8,128)(2,1)S(1)} %copy-done, bf16[1728,384]{1,0:T(8,128)(2,1)S(1)} %copy-done.2, bf16[1728,384]{1,0:T(8,128)(2,1)S(1)} %copy-done, bf16[1728,384]{1,0:T(8,128)(2,1)S(1)} %copy-done.2), custom_call_target="tpu_custom_call" | custom-call | tf_op jit(solution)/shard_map/pallas_call | solution.py:213
  12.1 1.9 collective-permute-start.4
  16.7 2.5 %shard_map.66.refs_0_ = bf16[576,384]{1,0:T(8,128)(2,1)} custom-call(s32[6]{0:T(128)S(1)} %stack.154.info, bf16[1728,384]{1,0:T(8,128)(2,1)S(1)} %copy-done.7, bf16[1728,384]{1,0:T(8,128)(2,1)S(1)} %copy-done.1, bf16[1728,384]{1,0:T(8,128)(2,1)S(1)} %copy-done.3), custom_call_target="tpu_custom_call" | custom-call | tf_op jit(solution)/shard_map/pallas_call | solution.py:84
  19.2 1.6 collective-permute-start.10
  20.9 4.1 %collective-permute-start.14 = (bf16[96,640]{1,0:T(8,128)(2,1)}, bf16[96,640]{1,0:T(8,128)(2,1)}, u32[]{:S(2)}, u32[]{:S(2)}) collective-permute-start(bf16[96,640]{1,0:T(8,128)(2,1)} %own_ref.1), channel_id=1, source_target_pairs={{32,0},{4,36},{33,1},{5,37},{34,2},{6,38},{35,3},{7,39},{40,8},{12... | collective-permute-start | bytes 368648 | tf_op jit(solution)/shard_map/ppermute | solution.py:310
  26.9 17.8 %collective-permute-done.15.across_ref = bf16[96,640]{1,0:T(8,128)(2,1)} collective-permute-done((bf16[96,640]{1,0:T(8,128)(2,1)}, bf16[96,640]{1,0:T(8,128)(2,1)}, u32[]{:S(2)}, u32[]{:S(2)}) %collective-permute-start.15) | collective-permute-done | bytes 122912 | tf_op jit(solution)/shard_map/ppermute | solution.py:311
  44.7 6.0 %collective-permute-start.16 = (bf16[96,640]{1,0:T(8,128)(2,1)}, bf16[96,640]{1,0:T(8,128)(2,1)}, u32[]{:S(2)}, u32[]{:S(2)}) collective-permute-start(bf16[96,640]{1,0:T(8,128)(2,1)} %own_ref.1), channel_id=1, source_target_pairs={{32,4},{4,32},{33,5},{5,33},{34,6},{6,34},{35,7},{7,35},{40,12},{1... | collective-permute-start | bytes 368648 | tf_op jit(solution)/shard_map/ppermute | solution.py:312
  50.7 4.5 %collective-permute-done.16.askew_ref = bf16[96,640]{1,0:T(8,128)(2,1)} collective-permute-done((bf16[96,640]{1,0:T(8,128)(2,1)}, bf16[96,640]{1,0:T(8,128)(2,1)}, u32[]{:S(2)}, u32[]{:S(2)}) %collective-permute-start.16) | collective-permute-done | bytes 122912 | tf_op jit(solution)/shard_map/ppermute | solution.py:312
  56.1 1.8 shard_map.68
  58.0 1.9 %collective-permute-start.5 = (bf16[576,384]{1,0:T(8,128)(2,1)}, bf16[576,384]{1,0:T(8,128)(2,1)}, u32[]{:S(2)}, u32[]{:S(2)}) collective-permute-start(bf16[576,384]{1,0:T(8,128)(2,1)} %get-tuple-element.17), channel_id=1, source_target_pairs={{1,2},{2,1},{5,6},{6,5},{9,10},{10,9},{13,14},{14,13},{17,18},{18,... | collective-permute-start | bytes 1327112 | tf_op jit(solution)/shard_map/ppermute | solution.py:262
  59.9 1.9 %collective-permute-start.8 = (bf16[576,384]{1,0:T(8,128)(2,1)}, bf16[576,384]{1,0:T(8,128)(2,1)}, u32[]{:S(2)}, u32[]{:S(2)}) collective-permute-start(bf16[576,384]{1,0:T(8,128)(2,1)} %collective-permute-done.7.rest_1_), channel_id=1, source_target_pairs={{2,6},{6,10},{10,14},{14,18},{18,22},{22,26},{26,30},{5,1},{9,5},{... | collective-permute-start | bytes 1327112 | tf_op jit(solution)/shard_map/ppermute | solution.py:268
  61.8 4.7 %collective-permute-start.11 = (bf16[576,384]{1,0:T(8,128)(2,1)}, bf16[576,384]{1,0:T(8,128)(2,1)}, u32[]{:S(2)}, u32[]{:S(2)}) collective-permute-start(bf16[576,384]{1,0:T(8,128)(2,1)} %shard_map.66.refs_0_), channel_id=1, source_target_pairs={{0,192},{64,0},{128,64},{192,128},{1,193},{65,1},{129,65},{193,129... | collective-permute-start | bytes 1327112 | tf_op jit(solution)/shard_map/ppermute | solution.py:298
  66.6 1.4 collective-permute-start.6
  70.5 2.6 %shard_map.65.refs_0_ = bf16[576,384]{1,0:T(8,128)(2,1)} custom-call(s32[6]{0:T(128)S(1)} %stack.137.info, bf16[1728,384]{1,0:T(8,128)(2,1)S(1)} %copy-done.8, bf16[1728,384]{1,0:T(8,128)(2,1)S(1)} %copy-done.1, bf16[1728,384]{1,0:T(8,128)(2,1)S(1)} %copy-done.3, bf16[1152,384]{1,0:T(8,128)(2,1)S(1)} %copy-done.5, bf16[1152,384]{1,0:T(8,128)(2,1)S(1)} %copy-done.5), custom_call_target="tpu_custom_call" | custom-call | tf_op jit(solution)/shard_map/pallas_call | solution.py:84
  73.2 3.3 %collective-permute-start.3 = (bf16[576,384]{1,0:T(8,128)(2,1)}, bf16[576,384]{1,0:T(8,128)(2,1)S(1)}, u32[]{:S(2)}, u32[]{:S(2)}) collective-permute-start(bf16[576,384]{1,0:T(8,128)(2,1)} %shard_map.65.refs_0_), channel_id=1, source_target_pairs={{0,192},{64,0},{128,64},{192,128},{1,193},{65,1},{129,65},{193,129... | collective-permute-start | bytes 1327112 | tf_op jit(solution)/shard_map/ppermute | solution.py:298
  76.4 1.7 collective-permute-done.8
  78.1 3.4 %collective-permute-start.9 = (bf16[576,384]{1,0:T(8,128)(2,1)}, bf16[576,384]{1,0:T(8,128)(2,1)S(1)}, u32[]{:S(2)}, u32[]{:S(2)}) collective-permute-start(bf16[576,384]{1,0:T(8,128)(2,1)} %collective-permute-done.8), channel_id=1, source_target_pairs={{2,0},{1,3},{6,4},{5,7},{10,8},{9,11},{14,12},{13,15},{18,16},{17,... | collective-permute-start | bytes 1327112 | tf_op jit(solution)/shard_map/ppermute | solution.py:271
  81.7 11.8 %collective-permute-done.11.rest_7_.refs_3_ = bf16[576,384]{1,0:T(8,128)(2,1)} collective-permute-done((bf16[576,384]{1,0:T(8,128)(2,1)}, bf16[576,384]{1,0:T(8,128)(2,1)}, u32[]{:S(2)}, u32[]{:S(2)}) %collective-permute-start.11) | collective-permute-done | bytes 442400 | tf_op jit(solution)/shard_map/ppermute | solution.py:298
  93.5 12.2 %collective-permute-done.1.rest_8_.refs_1_ = bf16[576,384]{1,0:T(8,128)(2,1)S(1)} collective-permute-done((bf16[576,384]{1,0:T(8,128)(2,1)}, bf16[576,384]{1,0:T(8,128)(2,1)S(1)}, u32[]{:S(2)}, u32[]{:S(2)}) %collective-permute-start.1) | collective-permute-done | bytes 442400 | tf_op jit(solution)/shard_map/ppermute | solution.py:298
  105.6 6.8 %collective-permute-done.3.rest_9_.refs_3_ = bf16[576,384]{1,0:T(8,128)(2,1)S(1)} collective-permute-done((bf16[576,384]{1,0:T(8,128)(2,1)}, bf16[576,384]{1,0:T(8,128)(2,1)S(1)}, u32[]{:S(2)}, u32[]{:S(2)}) %collective-permute-start.3) | collective-permute-done | bytes 442400 | tf_op jit(solution)/shard_map/ppermute | solution.py:298
  113.7 9.0 %shard_map.67.refs_4_ = bf16[576,384]{1,0:T(8,128)(2,1)S(1)} custom-call(s32[6]{0:T(128)S(1)} %stack.147.info, bf16[1728,384]{1,0:T(8,128)(2,1)S(1)} %copy-done.9, bf16[1728,384]{1,0:T(8,128)(2,1)} %k_ref.5, bf16[1728,384]{1,0:T(8,128)(2,1)} %v_ref.5, bf16[1152,384]{1,0:T(8,128)(2,1)S(1)} %copy-done.6, bf16[1152,384]{1,0:T(8,128)(2,1)S(1)} %copy-done.6, ...), custom_call_target="tpu_custom_call" | custom-call | tf_op jit(solution)/shard_map/pallas_call | solution.py:84
  122.8 3.3 %collective-permute-start.12 = (bf16[576,384]{1,0:T(8,128)(2,1)S(1)}, bf16[576,384]{1,0:T(8,128)(2,1)S(1)}, u32[]{:S(2)}, u32[]{:S(2)}) collective-permute-start(bf16[576,384]{1,0:T(8,128)(2,1)S(1)} %shard_map.67.refs_4_), channel_id=1, source_target_pairs={{0,64},{64,128},{128,192},{192,0},{1,65},{65,129},{129,193},{193,1... | collective-permute-start | bytes 1327112 | tf_op jit(solution)/shard_map/ppermute | solution.py:298
  126.2 3.0 %collective-permute-start.13 = (bf16[576,384]{1,0:T(8,128)(2,1)S(1)}, bf16[576,384]{1,0:T(8,128)(2,1)S(1)}, u32[]{:S(2)}, u32[]{:S(2)}) collective-permute-start(bf16[576,384]{1,0:T(8,128)(2,1)S(1)} %shard_map.67.refs_4_), channel_id=1, source_target_pairs={{0,192},{64,0},{128,64},{192,128},{1,193},{65,1},{129,65},{193,129... | collective-permute-start | bytes 1327112 | tf_op jit(solution)/shard_map/ppermute | solution.py:298
  129.3 5.9 %collective-permute-done.12.refs_5_ = bf16[576,384]{1,0:T(8,128)(2,1)S(1)} collective-permute-done((bf16[576,384]{1,0:T(8,128)(2,1)S(1)}, bf16[576,384]{1,0:T(8,128)(2,1)S(1)}, u32[]{:S(2)}, u32[]{:S(2)}) %collective-permute-start.12) | collective-permute-done | bytes 442400 | tf_op jit(solution)/shard_map/ppermute | solution.py:298
  135.2 2.2 %collective-permute-start.18 = (bf16[576,384]{1,0:T(8,128)(2,1)S(1)}, bf16[576,384]{1,0:T(8,128)(2,1)S(1)}, u32[]{:S(2)}, u32[]{:S(2)}) collective-permute-start(bf16[576,384]{1,0:T(8,128)(2,1)S(1)} %collective-permute-done.12.refs_5_), channel_id=1, source_target_pairs={{0,64},{64,128},{128,192},{192,0},{1,65},{65,129},{129,193},{193,1... | collective-permute-start | bytes 1327112 | tf_op jit(solution)/shard_map/ppermute | solution.py:298
  137.6 7.0 %collective-permute-done.2.refs_2_ = bf16[576,384]{1,0:T(8,128)(2,1)S(1)} collective-permute-done((bf16[576,384]{1,0:T(8,128)(2,1)S(1)}, bf16[576,384]{1,0:T(8,128)(2,1)S(1)}, u32[]{:S(2)}, u32[]{:S(2)}) %collective-permute-start.2) | collective-permute-done | bytes 442400 | tf_op jit(solution)/shard_map/ppermute | solution.py:298
  144.7 13.4 %collective-permute-done.13.refs_6_ = bf16[576,384]{1,0:T(8,128)(2,1)S(1)} collective-permute-done((bf16[576,384]{1,0:T(8,128)(2,1)S(1)}, bf16[576,384]{1,0:T(8,128)(2,1)S(1)}, u32[]{:S(2)}, u32[]{:S(2)}) %collective-permute-start.13) | collective-permute-done | bytes 442400 | tf_op jit(solution)/shard_map/ppermute | solution.py:298
  158.0 10.2 %shard_map.69 = (f32[576,640]{1,0:T(8,128)S(1)}, bf16[576,640]{1,0:T(8,128)(2,1)S(1)}, f32[576,1280]{1,0:T(8,128)}) custom-call(s32[7]{0:T(128)S(1)} %stack.130.info, bf16[576,384]{1,0:T(8,128)(2,1)} %shard_map.65.refs_0_, bf16[576,384]{1,0:T(8,128)(2,1)S(1)} %collective-permute-done.1.rest_8_.refs_1_, bf16[576,384]{1,0:T(8,128)(2,1)S(1)} %collective-permute-done.2.refs_2_, ...), custom_call_target="tpu_custom_call" | custom-call | tf_op jit(solution)/shard_map/pallas_call | solution.py:159
  168.9 6.3 %shard_map.71 = (f32[576,640]{1,0:T(8,128)S(1)}, bf16[576,640]{1,0:T(8,128)(2,1)S(1)}) custom-call(s32[4]{0:T(128)S(1)} %pad_add_fusion.4.info, bf16[576,384]{1,0:T(8,128)(2,1)} %shard_map.66.refs_0_, bf16[576,384]{1,0:T(8,128)(2,1)} %collective-permute-done.10.rest_6_.rest_3_.refs_1_, bf16[576,384]{1,0:T(8,128)(2,1)S(1)} %collective-permute-done.20.refs_2_, ...), custom_call_target="tpu_custom_call" | custom-call | tf_op jit(solution)/shard_map/pallas_call | solution.py:159
  175.7 2.9 %shard_map.70 = (f32[576,640]{1,0:T(8,128)S(1)}, bf16[576,640]{1,0:T(8,128)(2,1)S(1)}) custom-call(s32[2]{0:T(128)S(1)} %pad_add_fusion.2.info, bf16[576,384]{1,0:T(8,128)(2,1)S(1)} %collective-permute-done.18.piece, bf16[1536,1280]{1,0:T(8,128)(2,1)} %all-gather.2.cloned.1.call-done.refs_7_.w_ref.refs_4_, f32[576,1280]{1,0:T(8,128)S(1)} %copy-done.10), custom_call_target="tpu_custom_call" | custom-call | tf_op jit(solution)/shard_map/pallas_call | solution.py:159
  179.1 1.6 shard_map.72.refs_5_
  180.9 1.9 %shard_map.73 = bf16[1728,640]{1,0:T(8,128)(2,1)} custom-call(s32[4]{0:T(128)S(1)} %pad_add_fusion.info, f32[576,640]{1,0:T(8,128)S(1)} %get-tuple-element.18.refs_0_, bf16[576,640]{1,0:T(8,128)(2,1)S(1)} %collective-permute-done.17.refs_1_, f32[576,640]{1,0:T(8,128)S(1)} %get-tuple-element.21.refs_2_, ...), custom_call_target="tpu_custom_call", output_to_operand_aliasing={{}: (6, {})} | custom-call | tf_op jit(solution)/shard_map/pallas_call | solution.py:185
  (59 shorter events, 14.7 us)
Async XLA Ops:
  6.5 151.5 %all-gather.2.cloned.1.call-start = ((), (), s32[]{:S(2)}) async-start(), calls=%async_computation | async-start | bytes 4177920 | tf_op jit(solution)/shard_map/all_gather | solution.py:315
  7.3 1.3 copy-start
  9.9 5.5 %copy-start.1 = (bf16[1728,384]{1,0:T(8,128)(2,1)S(1)}, bf16[1728,384]{1,0:T(8,128)(2,1)}, u32[]{:S(2)}) copy-start(bf16[1728,384]{1,0:T(8,128)(2,1)} %k_ref.5) | copy-start | bytes 3981316
  9.9 5.5 %copy-start.3 = (bf16[1728,384]{1,0:T(8,128)(2,1)S(1)}, bf16[1728,384]{1,0:T(8,128)(2,1)}, u32[]{:S(2)}) copy-start(bf16[1728,384]{1,0:T(8,128)(2,1)} %v_ref.5) | copy-start | bytes 3981316
  11.8 43.4 %collective-permute-start = (bf16[1152,384]{1,0:T(8,128)(2,1)}, bf16[1152,384]{1,0:T(8,128)(2,1)S(1)}, u32[]{:S(2)}, u32[]{:S(2)}) collective-permute-start(bf16[1152,384]{1,0:T(8,128)(2,1)} %get-tuple-element.15), channel_id=1, source_target_pairs={{0,1},{1,0},{2,3},{3,2},{4,5},{5,4},{6,7},{7,6},{8,9},{9,8},{10,11... | collective-permute-start | bytes 2654216 | tf_op jit(solution)/shard_map/ppermute | solution.py:259
  12.1 43.1 %collective-permute-start.4 = (bf16[576,384]{1,0:T(8,128)(2,1)}, bf16[576,384]{1,0:T(8,128)(2,1)}, u32[]{:S(2)}, u32[]{:S(2)}) collective-permute-start(bf16[576,384]{1,0:T(8,128)(2,1)} %get-tuple-element.16), channel_id=1, source_target_pairs={{0,3},{3,0},{1,2},{2,1},{4,7},{7,4},{5,6},{6,5},{8,11},{11,8},{9,1... | collective-permute-start | bytes 1327112 | tf_op jit(solution)/shard_map/ppermute | solution.py:260
  14.0 41.2 %collective-permute-start.7 = (bf16[576,384]{1,0:T(8,128)(2,1)}, bf16[576,384]{1,0:T(8,128)(2,1)}, u32[]{:S(2)}, u32[]{:S(2)}) collective-permute-start(bf16[576,384]{1,0:T(8,128)(2,1)} %get-tuple-element.17), channel_id=1, source_target_pairs={{0,1},{3,2},{4,5},{7,6},{8,9},{11,10},{12,13},{15,14},{16,17},{19,... | collective-permute-start | bytes 1327112 | tf_op jit(solution)/shard_map/ppermute | solution.py:261
  15.4 1.3 copy-start.7
  19.2 35.9 %collective-permute-start.10 = (bf16[576,384]{1,0:T(8,128)(2,1)}, bf16[576,384]{1,0:T(8,128)(2,1)}, u32[]{:S(2)}, u32[]{:S(2)}) collective-permute-start(bf16[576,384]{1,0:T(8,128)(2,1)} %shard_map.66.refs_0_), channel_id=1, source_target_pairs={{0,64},{64,128},{128,192},{192,0},{1,65},{65,129},{129,193},{193,1... | collective-permute-start | bytes 1327112 | tf_op jit(solution)/shard_map/ppermute | solution.py:298
  20.9 4.7 %collective-permute-start.14 = (bf16[96,640]{1,0:T(8,128)(2,1)}, bf16[96,640]{1,0:T(8,128)(2,1)}, u32[]{:S(2)}, u32[]{:S(2)}) collective-permute-start(bf16[96,640]{1,0:T(8,128)(2,1)} %own_ref.1), channel_id=1, source_target_pairs={{32,0},{4,36},{33,1},{5,37},{34,2},{6,38},{35,3},{7,39},{40,8},{12... | collective-permute-start | bytes 368648 | tf_op jit(solution)/shard_map/ppermute | solution.py:310
  25.6 19.1 %collective-permute-start.15 = (bf16[96,640]{1,0:T(8,128)(2,1)}, bf16[96,640]{1,0:T(8,128)(2,1)}, u32[]{:S(2)}, u32[]{:S(2)}) collective-permute-start(bf16[96,640]{1,0:T(8,128)(2,1)} %own_ref.1), channel_id=1, source_target_pairs={{0,4},{36,32},{1,5},{37,33},{2,6},{38,34},{3,7},{39,35},{8,12},{44... | collective-permute-start | bytes 368648 | tf_op jit(solution)/shard_map/ppermute | solution.py:311
  44.7 10.5 %collective-permute-start.16 = (bf16[96,640]{1,0:T(8,128)(2,1)}, bf16[96,640]{1,0:T(8,128)(2,1)}, u32[]{:S(2)}, u32[]{:S(2)}) collective-permute-start(bf16[96,640]{1,0:T(8,128)(2,1)} %own_ref.1), channel_id=1, source_target_pairs={{32,4},{4,32},{33,5},{5,33},{34,6},{6,34},{35,7},{7,35},{40,12},{1... | collective-permute-start | bytes 368648 | tf_op jit(solution)/shard_map/ppermute | solution.py:312
  58.0 15.2 %collective-permute-start.5 = (bf16[576,384]{1,0:T(8,128)(2,1)}, bf16[576,384]{1,0:T(8,128)(2,1)}, u32[]{:S(2)}, u32[]{:S(2)}) collective-permute-start(bf16[576,384]{1,0:T(8,128)(2,1)} %get-tuple-element.17), channel_id=1, source_target_pairs={{1,2},{2,1},{5,6},{6,5},{9,10},{10,9},{13,14},{14,13},{17,18},{18,... | collective-permute-start | bytes 1327112 | tf_op jit(solution)/shard_map/ppermute | solution.py:262
  59.9 18.2 %collective-permute-start.8 = (bf16[576,384]{1,0:T(8,128)(2,1)}, bf16[576,384]{1,0:T(8,128)(2,1)}, u32[]{:S(2)}, u32[]{:S(2)}) collective-permute-start(bf16[576,384]{1,0:T(8,128)(2,1)} %collective-permute-done.7.rest_1_), channel_id=1, source_target_pairs={{2,6},{6,10},{10,14},{14,18},{18,22},{22,26},{26,30},{5,1},{9,5},{... | collective-permute-start | bytes 1327112 | tf_op jit(solution)/shard_map/ppermute | solution.py:268
  61.8 31.6 %collective-permute-start.11 = (bf16[576,384]{1,0:T(8,128)(2,1)}, bf16[576,384]{1,0:T(8,128)(2,1)}, u32[]{:S(2)}, u32[]{:S(2)}) collective-permute-start(bf16[576,384]{1,0:T(8,128)(2,1)} %shard_map.66.refs_0_), channel_id=1, source_target_pairs={{0,192},{64,0},{128,64},{192,128},{1,193},{65,1},{129,65},{193,129... | collective-permute-start | bytes 1327112 | tf_op jit(solution)/shard_map/ppermute | solution.py:298
  66.6 26.9 %collective-permute-start.6 = (bf16[576,384]{1,0:T(8,128)(2,1)}, bf16[576,384]{1,0:T(8,128)(2,1)}, u32[]{:S(2)}, u32[]{:S(2)}) collective-permute-start(bf16[576,384]{1,0:T(8,128)(2,1)} %collective-permute-done.4.rest_2_.rest_0_), channel_id=1, source_target_pairs={{0,4},{4,8},{8,12},{12,16},{16,20},{20,24},{24,28},{7,3},{11,7},{1... | collective-permute-start | bytes 1327112 | tf_op jit(solution)/shard_map/ppermute | solution.py:268
  69.2 1.3 copy-start.8
  70.5 41.9 %copy-start.6 = (bf16[1152,384]{1,0:T(8,128)(2,1)S(1)}, bf16[1152,384]{1,0:T(8,128)(2,1)}, u32[]{:S(2)}) copy-start(bf16[1152,384]{1,0:T(8,128)(2,1)} %copy-done.4) | copy-start | bytes 2654212
  73.1 32.5 %collective-permute-start.1 = (bf16[576,384]{1,0:T(8,128)(2,1)}, bf16[576,384]{1,0:T(8,128)(2,1)S(1)}, u32[]{:S(2)}, u32[]{:S(2)}) collective-permute-start(bf16[576,384]{1,0:T(8,128)(2,1)} %shard_map.65.refs_0_), channel_id=1, source_target_pairs={{0,64},{64,128},{128,192},{192,0},{1,65},{65,129},{129,193},{193,1... | collective-permute-start | bytes 1327112 | tf_op jit(solution)/shard_map/ppermute | solution.py:298
  73.2 39.3 %collective-permute-start.3 = (bf16[576,384]{1,0:T(8,128)(2,1)}, bf16[576,384]{1,0:T(8,128)(2,1)S(1)}, u32[]{:S(2)}, u32[]{:S(2)}) collective-permute-start(bf16[576,384]{1,0:T(8,128)(2,1)} %shard_map.65.refs_0_), channel_id=1, source_target_pairs={{0,192},{64,0},{128,64},{192,128},{1,193},{65,1},{129,65},{193,129... | collective-permute-start | bytes 1327112 | tf_op jit(solution)/shard_map/ppermute | solution.py:298
  78.1 34.3 %collective-permute-start.9 = (bf16[576,384]{1,0:T(8,128)(2,1)}, bf16[576,384]{1,0:T(8,128)(2,1)S(1)}, u32[]{:S(2)}, u32[]{:S(2)}) collective-permute-start(bf16[576,384]{1,0:T(8,128)(2,1)} %collective-permute-done.8), channel_id=1, source_target_pairs={{2,0},{1,3},{6,4},{5,7},{10,8},{9,11},{14,12},{13,15},{18,16},{17,... | collective-permute-start | bytes 1327112 | tf_op jit(solution)/shard_map/ppermute | solution.py:271
  112.4 1.3 copy-start.9
  122.8 12.4 %collective-permute-start.12 = (bf16[576,384]{1,0:T(8,128)(2,1)S(1)}, bf16[576,384]{1,0:T(8,128)(2,1)S(1)}, u32[]{:S(2)}, u32[]{:S(2)}) collective-permute-start(bf16[576,384]{1,0:T(8,128)(2,1)S(1)} %shard_map.67.refs_4_), channel_id=1, source_target_pairs={{0,64},{64,128},{128,192},{192,0},{1,65},{65,129},{129,193},{193,1... | collective-permute-start | bytes 1327112 | tf_op jit(solution)/shard_map/ppermute | solution.py:298
  126.0 18.6 %collective-permute-start.2 = (bf16[576,384]{1,0:T(8,128)(2,1)S(1)}, bf16[576,384]{1,0:T(8,128)(2,1)S(1)}, u32[]{:S(2)}, u32[]{:S(2)}) collective-permute-start(bf16[576,384]{1,0:T(8,128)(2,1)S(1)} %collective-permute-done.1.rest_8_.refs_1_), channel_id=1, source_target_pairs={{0,64},{64,128},{128,192},{192,0},{1,65},{65,129},{129,193},{193,1... | collective-permute-start | bytes 1327112 | tf_op jit(solution)/shard_map/ppermute | solution.py:298
  126.2 31.8 %collective-permute-start.13 = (bf16[576,384]{1,0:T(8,128)(2,1)S(1)}, bf16[576,384]{1,0:T(8,128)(2,1)S(1)}, u32[]{:S(2)}, u32[]{:S(2)}) collective-permute-start(bf16[576,384]{1,0:T(8,128)(2,1)S(1)} %shard_map.67.refs_4_), channel_id=1, source_target_pairs={{0,192},{64,0},{128,64},{192,128},{1,193},{65,1},{129,65},{193,129... | collective-permute-start | bytes 1327112 | tf_op jit(solution)/shard_map/ppermute | solution.py:298
  129.3 39.7 %collective-permute-start.20 = (bf16[576,384]{1,0:T(8,128)(2,1)}, bf16[576,384]{1,0:T(8,128)(2,1)S(1)}, u32[]{:S(2)}, u32[]{:S(2)}) collective-permute-start(bf16[576,384]{1,0:T(8,128)(2,1)} %collective-permute-done.10.rest_6_.rest_3_.refs_1_), channel_id=1, source_target_pairs={{0,64},{64,128},{128,192},{192,0},{1,65},{65,129},{129,193},{193,1... | collective-permute-start | bytes 1327112 | tf_op jit(solution)/shard_map/ppermute | solution.py:298
  135.2 40.5 %collective-permute-start.18 = (bf16[576,384]{1,0:T(8,128)(2,1)S(1)}, bf16[576,384]{1,0:T(8,128)(2,1)S(1)}, u32[]{:S(2)}, u32[]{:S(2)}) collective-permute-start(bf16[576,384]{1,0:T(8,128)(2,1)S(1)} %collective-permute-done.12.refs_5_), channel_id=1, source_target_pairs={{0,64},{64,128},{128,192},{192,0},{1,65},{65,129},{129,193},{193,1... | collective-permute-start | bytes 1327112 | tf_op jit(solution)/shard_map/ppermute | solution.py:298
  168.3 7.4 %copy-start.10 = (f32[576,1280]{1,0:T(8,128)S(1)}, f32[576,1280]{1,0:T(8,128)}, u32[]{:S(2)}) copy-start(f32[576,1280]{1,0:T(8,128)} %get-tuple-element.20.so_far) | copy-start | bytes 8847364
  168.3 12.5 %collective-permute-start.17 = (bf16[576,640]{1,0:T(8,128)(2,1)S(1)}, bf16[576,640]{1,0:T(8,128)(2,1)S(1)}, u32[]{:S(2)}, u32[]{:S(2)}) collective-permute-start(bf16[576,640]{1,0:T(8,128)(2,1)S(1)} %get-tuple-element.19), channel_id=1, source_target_pairs={{0,32},{32,0},{1,33},{33,1},{2,34},{34,2},{3,35},{35,3},{4,36},{36... | collective-permute-start | bytes 2211848 | tf_op jit(solution)/shard_map/ppermute | solution.py:320
  175.3 3.8 %collective-permute-start.21 = (bf16[576,640]{1,0:T(8,128)(2,1)S(1)}, bf16[576,640]{1,0:T(8,128)(2,1)S(1)}, u32[]{:S(2)}, u32[]{:S(2)}) collective-permute-start(bf16[576,640]{1,0:T(8,128)(2,1)S(1)} %get-tuple-element.24), channel_id=1, source_target_pairs={{0,32},{32,0},{1,33},{33,1},{2,34},{34,2},{3,35},{35,3},{4,36},{36... | collective-permute-start | bytes 2211848 | tf_op jit(solution)/shard_map/ppermute | solution.py:320
  175.7 3.3 %copy-start.11 = (f32[640]{0:T(1024)S(1)}, f32[640]{0:T(1024)}, u32[]{:S(2)}) copy-start(f32[640]{0:T(1024)} %param.11) | copy-start | bytes 7684
  178.6 2.3 %collective-permute-start.19 = (bf16[576,640]{1,0:T(8,128)(2,1)S(1)}, bf16[576,640]{1,0:T(8,128)(2,1)S(1)}, u32[]{:S(2)}, u32[]{:S(2)}) collective-permute-start(bf16[576,640]{1,0:T(8,128)(2,1)S(1)} %get-tuple-element.22), channel_id=1, source_target_pairs={{0,32},{32,0},{1,33},{33,1},{2,34},{34,2},{3,35},{35,3},{4,36},{36... | collective-permute-start | bytes 2211848 | tf_op jit(solution)/shard_map/ppermute | solution.py:320
  (3 other events, 3.4 us)
Sparse Core Ops, SparseCore 0:
  58.1 70.1 all-gather.1

commit v3 on v2

--- a/solution.py
+++ b/solution.py
@@ -24,10 +24,6 @@
     halos, (o_ref, kbuf, vbuf) = rest[:halo_total], rest[-3:]
     slot, prev_from, next_from, prev_ok, next_ok, active = (info[i] for i in range(6))
 
-    @pl.when(pl.program_id(0) == 0)
-    def _():
-        vbuf[:, HEAD:] = jnp.ones((3 * FRAME, HEAD), jnp.bfloat16)
-
     @pl.when(active == 0)
     def _():
         o_ref[...] = jnp.zeros_like(o_ref)
@@ -39,14 +35,14 @@
         def _():
             local = pl.ds(pl.multiple_of(jnp.clip(source, 0, 2) * FRAME, FRAME), FRAME)
             kbuf[rows, :] = k_ref[local, :]
-            vbuf[rows, :HEAD] = v_ref[local, :]
+            vbuf[rows, :] = v_ref[local, :]
 
         for i in range(halo_total // 2):
 
             @pl.when(source == 3 + i)
             def _():
                 kbuf[rows, :] = halos[2 * i][...]
-                vbuf[rows, :HEAD] = halos[2 * i + 1][...]
+                vbuf[rows, :] = halos[2 * i + 1][...]
 
     @pl.when(active == 1)
     def _():
@@ -64,14 +60,14 @@
                 scores.append(s)
                 tops.append(jnp.max(s, axis=1, keepdims=True) * SCALE - off[f])
             top = jnp.maximum(jnp.maximum(tops[0], tops[1]), tops[2])
-            total = None
+            total, mass = None, None
             for f in range(3):
-                p = jnp.exp2(scores[f] * SCALE - (top + off[f])).astype(jnp.bfloat16)
-                part = jnp.dot(
-                    p, vbuf[f * FRAME + low : f * FRAME + high, :], preferred_element_type=jnp.float32
-                )
-                total = part if total is None else total + part
-            o_ref[w * TILE : (w + 1) * TILE, :] = (total[:, :HEAD] / total[:, HEAD:]).astype(jnp.bfloat16)
+                p = jnp.exp2(scores[f] * SCALE - (top + off[f]))
+                values = vbuf[f * FRAME + low : f * FRAME + high, :]
+                part = jnp.dot(p.astype(jnp.bfloat16), values, preferred_element_type=jnp.float32)
+                row = jnp.sum(p, axis=1, keepdims=True)
+                total, mass = (part, row) if total is None else (total + part, mass + row)
+            o_ref[w * TILE : (w + 1) * TILE, :] = (total / mass).astype(jnp.bfloat16)
 
 
 def attend(info, query, key, value, halos, after):
@@ -91,7 +87,7 @@
             out_specs=one,
             scratch_shapes=[
                 pltpu.VMEM((3 * FRAME, HEAD), jnp.bfloat16),
-                pltpu.VMEM((3 * FRAME, 2 * HEAD), jnp.bfloat16),
+                pltpu.VMEM((3 * FRAME, HEAD), jnp.bfloat16),
             ],
         ),
         compiler_params=pltpu.CompilerParams(vmem_limit_bytes=VMEM),
@@ -99,68 +95,74 @@
     )(info, query, key, value, *[array for array, _ in halos], *after)
 
 
-def share(info, at, pieces, w_ref):
-    total = None
+def line_up(info, at, pieces, line):
+    width = pieces[0].shape[1]
+    if len(pieces) * width < line.shape[1]:
+        line[...] = jnp.zeros_like(line)
     for k, piece in enumerate(pieces):
-        width = piece.shape[1]
-        rows = pl.ds(pl.multiple_of(info[at + k] * width, width), width)
-        part = jnp.dot(piece[...], w_ref[rows, :], preferred_element_type=jnp.float32)
-        total = part if total is None else total + part
-    return total
+        line[:, pl.ds(pl.multiple_of(info[at + k] * width, width), width)] = piece[...]
 
 
 def hand_out(total, mine_ref, other_ref):
+    mine_ref[...] = total[:, :HEAD]
+    other_ref[...] = total[:, HEAD:].astype(jnp.bfloat16)
+
+
+def project_body(split, info, *refs):
+    total = sum(split)
+    w_ref, lines = refs[total], refs[len(refs) - len(split) :]
+    outs = refs[total + 1 :]
+
     @pl.when(pl.program_id(0) == 0)
     def _():
-        other_ref[...] = total.astype(jnp.bfloat16)
-
-    @pl.when(pl.program_id(0) == 1)
-    def _():
-        mine_ref[...] = total
-
-
-def project_body(split, info, *refs):
-    groups, at = [], 0
-    for size in split:
-        groups.append(refs[at : at + size])
-        at += size
-    w_ref, outs = refs[at], refs[at + 1 :]
-    hand_out(share(info, 0, groups[0], w_ref), outs[0], outs[1])
-    if len(groups) == 2:
-        outs[2][...] = share(info, len(groups[0]), groups[1], w_ref)
+        at = 0
+        for size, line in zip(split, lines):
+            line_up(info, at, refs[at : at + size], line)
+            at += size
+
+    hand_out(jnp.dot(lines[0][...], w_ref[...], preferred_element_type=jnp.float32), outs[0], outs[1])
+    if len(split) == 2:
+        outs[2][...] = jnp.dot(lines[1][...], w_ref[...], preferred_element_type=jnp.float32)
 
 
 def project_last_body(info, piece, w_ref, so_far, mine_ref, other_ref):
-    hand_out(share(info, 1, [piece], w_ref) + so_far[...], mine_ref, other_ref)
+    part = jnp.dot(piece[...], w_ref[...], preferred_element_type=jnp.float32)
+    hand_out(part + so_far[...], mine_ref, other_ref)
 
 
 def project(order, whole, part, weight, so_far=None):
     rows, width = whole[0].shape
     depth, both = weight.shape
-    columns = both // 2
     fixed = lambda j, info: (0, 0)
-    side = lambda j, info: (0, 1 - j)
-    block = pl.BlockSpec((rows, columns), side)
+    side = lambda j, info: (0, j)
+    block = pl.BlockSpec((rows, 2 * HEAD), side)
     out_shape = [
-        jax.ShapeDtypeStruct((rows, columns), jnp.float32),
-        jax.ShapeDtypeStruct((rows, columns), jnp.bfloat16),
+        jax.ShapeDtypeStruct((rows, both // 2), jnp.float32),
+        jax.ShapeDtypeStruct((rows, both // 2), jnp.bfloat16),
     ]
-    out_specs = [pl.BlockSpec((rows, columns), fixed)] * 2
+    out_specs = [pl.BlockSpec((rows, HEAD), side)] * 2
     in_specs = [pl.BlockSpec((rows, width), fixed)] * (len(whole) + len(part))
+    scratch = []
     if part:
         out_shape.append(jax.ShapeDtypeStruct((rows, both), jnp.float32))
         out_specs.append(block)
     if so_far is None:
-        body, more = functools.partial(project_body, [len(g) for g in (whole, part) if g]), []
-        in_specs.append(pl.BlockSpec((depth, columns), side))
+        split = [len(g) for g in (whole, part) if g]
+        body, more = functools.partial(project_body, split), []
+        in_specs.append(pl.BlockSpec((depth, 2 * HEAD), side))
+        scratch = [pltpu.VMEM((rows, depth), jnp.bfloat16)] * len(split)
     else:
         body, more = project_last_body, [so_far]
-        in_specs += [pl.BlockSpec((width, columns), lambda j, info: (info[0], 1 - j)), block]
+        in_specs += [pl.BlockSpec((width, 2 * HEAD), lambda j, info: (info[0], j)), block]
     return pl.pallas_call(
         body,
         out_shape=out_shape,
         grid_spec=pltpu.PrefetchScalarGridSpec(
-            num_scalar_prefetch=1, grid=(2,), in_specs=in_specs, out_specs=out_specs
+            num_scalar_prefetch=1,
+            grid=(both // (2 * HEAD),),
+            in_specs=in_specs,
+            out_specs=out_specs,
+            scratch_shapes=scratch,
         ),
         compiler_params=pltpu.CompilerParams(vmem_limit_bytes=VMEM),
         cost_estimate=FREE,
@@ -219,30 +221,32 @@
             in_specs=frames,
             out_specs=[pl.BlockSpec((rows, width), lambda i, info: (0, 0)) for rows in heights],
         ),
-        compiler_params=pltpu.CompilerParams(vmem_limit_bytes=VMEM),
+        compiler_params=pltpu.CompilerParams(vmem_limit_bytes=60 * 1024 * 1024),
         cost_estimate=FREE,
     )(info, key, value, key, value)
 
 
-def lay_body(info, own_ref, beside_ref, across_ref, askew_ref, *rest):
+def lay_body(home, own_ref, over_ref, beside_ref, *rest):
     out_ref = rest[-1]
-    columns = own_ref.shape[1]
-    home = info[0] == 1
-    out_ref[:, :columns] = jnp.where(home, own_ref[...], across_ref[...])
-    out_ref[:, columns:] = jnp.where(home, beside_ref[...], askew_ref[...])
-
-
-def lay(info, own, beside, across, askew, after):
+    for j in range(own_ref.shape[1] // HEAD):
+        columns = slice(j * HEAD, (j + 1) * HEAD)
+        mine = jnp.where(home[0] == 1, own_ref[:, columns], over_ref[:, columns])
+        out_ref[:, 2 * j * HEAD : (2 * j + 1) * HEAD] = mine
+        out_ref[:, (2 * j + 1) * HEAD : (2 * j + 2) * HEAD] = beside_ref[:, columns]
+
+
+def lay(home, own, over, beside, after):
     rows, columns = own.shape
     vmem = pl.BlockSpec(memory_space=pltpu.VMEM)
     return pl.pallas_call(
         lay_body,
         out_shape=jax.ShapeDtypeStruct((rows, 2 * columns), own.dtype),
-        in_specs=[pl.BlockSpec(memory_space=pltpu.SMEM)] + [vmem] * 4
+        in_specs=[pl.BlockSpec(memory_space=pltpu.SMEM)]
+        + [vmem] * 3
         + [pl.BlockSpec(memory_space=pl.ANY)] * len(after),
         out_specs=vmem,
         cost_estimate=FREE,
-    )(info, own, beside, across, askew, *after)
+    )(home, own, over, beside, *after)
 
 
 def on_device(query, key, value, slab_counts, out_weight, out_bias):
@@ -306,12 +310,10 @@
     c1, c3 = along(c, 1), along(c, -1)
     c2 = along(c1, 1)
 
-    pair = ("core", "zh")
-    beside = lax.ppermute(out_weight, pair, [(2, 0), (1, 3)])
-    across = lax.ppermute(out_weight, pair, [(0, 1), (3, 2)])
-    askew = lax.ppermute(out_weight, pair, [(2, 1), (1, 2)])
-    home = (zh == core).astype(jnp.int32).reshape(1)
-    laid = lay(home, out_weight, beside, across, askew, [key_round, value_side, near, a1])
+    home = zh == core
+    over = lax.ppermute(out_weight, "zh", [(0, 1), (1, 0)])
+    beside = lax.ppermute(jnp.where(home, over, out_weight), "core", [(0, 1), (1, 0)])
+    laid = lay(home.astype(jnp.int32).reshape(1), out_weight, over, beside, [key_round, value_side, near, a1])
     weight = lax.all_gather(laid, ("y", "x"), axis=0, tiled=True)
 
     order = [((zl - k) % lines).astype(jnp.int32) for k in range(lines)]
@@ -327,7 +329,7 @@
     out = put([0], [own_a, swap(other_a)], None)
     turns = jnp.stack(order + [order[0], order[1], order[3]])
     own_b, other_b, so_far = project(turns, [b, b1, b2, b3], [c, c1, c3], weight)
-    own_c, other_c = project(jnp.stack([order[2], jnp.zeros_like(order[2])]), [c2], [], weight, so_far)
+    own_c, other_c = project(order[2].reshape(1), [c2], [], weight, so_far)
     out = put([1, 2], [own_b, swap(other_b), own_c, swap(other_c)], out)
     return out.T
 

time: 190 us -> 182 us (0.958)
  the two profiles are of different devices: /device:TPU:19 before, /device:TPU:27 now
where the time goes in v3:
time: 182 us; the launch traced here: 181 us
  waiting for transfers between devices  65 us (36%)
  Pallas kernels  52 us (29%)
  starting transfers between devices  40.9 us (22%)
  between operations  14.3 us (8%)
  local copies, waits for them, and re-layouts  6.49 us (4%)
  other arithmetic  2.45 us (1%)
    ppermute x9, waiting for transfers between devices, along(): lax.ppermute(value, 'zl', [(i, (i + steps) % lines) for i in range(lines)])  58.1 us
    pallas_call x3, Pallas kernels, attend(): pl.pallas_call(functools.partial(attend_body, len(halos)), out_shape=jax....  23.6 us
    pallas_call x3, Pallas kernels, project(): pl.pallas_call(body, out_shape=out_shape, grid_spec=pltpu.PrefetchScalarG...  19.7 us
    ppermute x2, starting transfers between devices, across_rows(): return lax.ppermute(value, SEQ, pairs)  10.2 us
    ppermute x9, starting transfers between devices, along(): lax.ppermute(value, 'zl', [(i, (i + steps) % lines) for i in range(lines)])  10.2 us
    ppermute x1, starting transfers between devices, on_device(): over = lax.ppermute(out_weight, 'zh', [(0, 1), (1, 0)])  6.91 us
    unnamed x20, local copies, waits for them, and re-layouts  6.16 us
    ppermute x1, waiting for transfers between devices, on_device(): value_side = lax.ppermute(away_value, 'x', [(0, 1), (3, 2)])  5.28 us
  transfers between devices with their start and end apart: 22, of which 10 were waited for; matrix products, arithmetic and copies ran while one was open for 1% of the time, Pallas kernels for 25%

profile of v3, /device:TPU:27, one launch (start us, length us, event | category | flops | bytes accessed | tf_op | source)
XLA Modules:
  0.0 181.0 jit_solution(16674764673941206044)
XLA Ops:
  7.9 3.5 %shard_map.64 = (bf16[1152,384]{1,0:T(8,128)(2,1)}, bf16[576,384]{1,0:T(8,128)(2,1)}, bf16[576,384]{1,0:T(8,128)(2,1)}) custom-call(s32[2]{0:T(128)} %pad_add_fusion.1.info, bf16[1728,384]{1,0:T(8,128)(2,1)} %k_ref.5, bf16[1728,384]{1,0:T(8,128)(2,1)} %v_ref.5, bf16[1728,384]{1,0:T(8,128)(2,1)} %k_ref.5, bf16[1728,384]{1,0:T(8,128)(2,1)} %v_ref.5), custom_call_target="tpu_custom_call" | custom-call | tf_op jit(solution)/shard_map/pallas_call | solution.py:215
  11.6 6.9 %collective-permute-start.14 = (bf16[96,640]{1,0:T(8,128)(2,1)}, bf16[96,640]{1,0:T(8,128)(2,1)}, u32[]{:S(2)}, u32[]{:S(2)}) collective-permute-start(bf16[96,640]{1,0:T(8,128)(2,1)} %own_ref.1), channel_id=1, source_target_pairs={{0,4},{4,0},{1,5},{5,1},{2,6},{6,2},{3,7},{7,3},{8,12},{12,8},{9,1... | collective-permute-start | bytes 368648 | tf_op jit(solution)/shard_map/ppermute | solution.py:314
  18.5 2.0 %collective-permute-start.4 = (bf16[576,384]{1,0:T(8,128)(2,1)}, bf16[576,384]{1,0:T(8,128)(2,1)}, u32[]{:S(2)}, u32[]{:S(2)}) collective-permute-start(bf16[576,384]{1,0:T(8,128)(2,1)} %get-tuple-element.16), channel_id=1, source_target_pairs={{0,3},{3,0},{1,2},{2,1},{4,7},{7,4},{5,6},{6,5},{8,11},{11,8},{9,1... | collective-permute-start | bytes 1327112 | tf_op jit(solution)/shard_map/ppermute | solution.py:264
  23.2 7.7 %shard_map.66.refs_0_ = bf16[576,384]{1,0:T(8,128)(2,1)} custom-call(s32[6]{0:T(128)S(1)} %stack.150.info, bf16[1728,384]{1,0:T(8,128)(2,1)S(1)} %copy-done.5, bf16[1728,384]{1,0:T(8,128)(2,1)S(1)} %copy-done, bf16[1728,384]{1,0:T(8,128)(2,1)S(1)} %copy-done.1), custom_call_target="tpu_custom_call" | custom-call | tf_op jit(solution)/shard_map/pallas_call | solution.py:80
  31.7 1.6 broadcast_select_fusion
  33.2 1.8 collective-permute-start.15
  36.3 5.3 %collective-permute-done.7.rest_1_ = bf16[576,384]{1,0:T(8,128)(2,1)} collective-permute-done((bf16[576,384]{1,0:T(8,128)(2,1)}, bf16[576,384]{1,0:T(8,128)(2,1)}, u32[]{:S(2)}, u32[]{:S(2)}) %collective-permute-start.7) | collective-permute-done | bytes 442400 | tf_op jit(solution)/shard_map/ppermute | solution.py:265
  41.6 1.5 collective-permute-done.10.rest_6_.rest_3_.refs_1_
  44.1 1.8 shard_map.68
  45.9 1.9 %collective-permute-start.5 = (bf16[576,384]{1,0:T(8,128)(2,1)}, bf16[576,384]{1,0:T(8,128)(2,1)}, u32[]{:S(2)}, u32[]{:S(2)}) collective-permute-start(bf16[576,384]{1,0:T(8,128)(2,1)} %get-tuple-element.17), channel_id=1, source_target_pairs={{1,2},{2,1},{5,6},{6,5},{9,10},{10,9},{13,14},{14,13},{17,18},{18,... | collective-permute-start | bytes 1327112 | tf_op jit(solution)/shard_map/ppermute | solution.py:266
  47.8 8.8 %collective-permute-start.8 = (bf16[576,384]{1,0:T(8,128)(2,1)}, bf16[576,384]{1,0:T(8,128)(2,1)}, u32[]{:S(2)}, u32[]{:S(2)}) collective-permute-start(bf16[576,384]{1,0:T(8,128)(2,1)} %collective-permute-done.7.rest_1_), channel_id=1, source_target_pairs={{2,6},{6,10},{10,14},{14,18},{18,22},{22,26},{26,30},{5,1},{9,5},{... | collective-permute-start | bytes 1327112 | tf_op jit(solution)/shard_map/ppermute | solution.py:272
  56.6 1.7 collective-permute-start.11
  58.4 1.4 collective-permute-start.6
  62.4 7.9 %shard_map.65.refs_0_ = bf16[576,384]{1,0:T(8,128)(2,1)} custom-call(s32[6]{0:T(128)S(1)} %stack.133.info, bf16[1728,384]{1,0:T(8,128)(2,1)S(1)} %copy-done.6, bf16[1728,384]{1,0:T(8,128)(2,1)S(1)} %copy-done, bf16[1728,384]{1,0:T(8,128)(2,1)S(1)} %copy-done.1, bf16[1152,384]{1,0:T(8,128)(2,1)S(1)} %copy-done.3, bf16[1152,384]{1,0:T(8,128)(2,1)S(1)} %copy-done.3), custom_call_target="tpu_custom_call" | custom-call | tf_op jit(solution)/shard_map/pallas_call | solution.py:80
  70.3 3.3 %collective-permute-start.3 = (bf16[576,384]{1,0:T(8,128)(2,1)}, bf16[576,384]{1,0:T(8,128)(2,1)S(1)}, u32[]{:S(2)}, u32[]{:S(2)}) collective-permute-start(bf16[576,384]{1,0:T(8,128)(2,1)} %shard_map.65.refs_0_), channel_id=1, source_target_pairs={{0,192},{64,0},{128,64},{192,128},{1,193},{65,1},{129,65},{193,129... | collective-permute-start | bytes 1327112 | tf_op jit(solution)/shard_map/ppermute | solution.py:302
  73.5 1.5 collective-permute-start.9
  75.1 11.2 %collective-permute-done.11.rest_7_.refs_3_ = bf16[576,384]{1,0:T(8,128)(2,1)} collective-permute-done((bf16[576,384]{1,0:T(8,128)(2,1)}, bf16[576,384]{1,0:T(8,128)(2,1)}, u32[]{:S(2)}, u32[]{:S(2)}) %collective-permute-start.11) | collective-permute-done | bytes 442400 | tf_op jit(solution)/shard_map/ppermute | solution.py:302
  86.3 7.7 %collective-permute-done.1.rest_8_.refs_1_ = bf16[576,384]{1,0:T(8,128)(2,1)S(1)} collective-permute-done((bf16[576,384]{1,0:T(8,128)(2,1)}, bf16[576,384]{1,0:T(8,128)(2,1)S(1)}, u32[]{:S(2)}, u32[]{:S(2)}) %collective-permute-start.1) | collective-permute-done | bytes 442400 | tf_op jit(solution)/shard_map/ppermute | solution.py:302
  94.1 10.4 %collective-permute-done.3.rest_9_.refs_3_ = bf16[576,384]{1,0:T(8,128)(2,1)S(1)} collective-permute-done((bf16[576,384]{1,0:T(8,128)(2,1)}, bf16[576,384]{1,0:T(8,128)(2,1)S(1)}, u32[]{:S(2)}, u32[]{:S(2)}) %collective-permute-start.3) | collective-permute-done | bytes 442400 | tf_op jit(solution)/shard_map/ppermute | solution.py:302
  104.5 1.4 copy-done.7
  105.8 8.0 %shard_map.67.refs_4_ = bf16[576,384]{1,0:T(8,128)(2,1)S(1)} custom-call(s32[6]{0:T(128)S(1)} %stack.143.info, bf16[1728,384]{1,0:T(8,128)(2,1)S(1)} %copy-done.7, bf16[1728,384]{1,0:T(8,128)(2,1)} %k_ref.5, bf16[1728,384]{1,0:T(8,128)(2,1)} %v_ref.5, bf16[1152,384]{1,0:T(8,128)(2,1)S(1)} %copy-done.4, bf16[1152,384]{1,0:T(8,128)(2,1)S(1)} %copy-done.4, ...), custom_call_target="tpu_custom_call" | custom-call | tf_op jit(solution)/shard_map/pallas_call | solution.py:80
  114.9 3.2 %collective-permute-start.13 = (bf16[576,384]{1,0:T(8,128)(2,1)S(1)}, bf16[576,384]{1,0:T(8,128)(2,1)S(1)}, u32[]{:S(2)}, u32[]{:S(2)}) collective-permute-start(bf16[576,384]{1,0:T(8,128)(2,1)S(1)} %shard_map.67.refs_4_), channel_id=1, source_target_pairs={{0,192},{64,0},{128,64},{192,128},{1,193},{65,1},{129,65},{193,129... | collective-permute-start | bytes 1327112 | tf_op jit(solution)/shard_map/ppermute | solution.py:302
  118.1 7.3 %collective-permute-done.12.refs_5_ = bf16[576,384]{1,0:T(8,128)(2,1)S(1)} collective-permute-done((bf16[576,384]{1,0:T(8,128)(2,1)S(1)}, bf16[576,384]{1,0:T(8,128)(2,1)S(1)}, u32[]{:S(2)}, u32[]{:S(2)}) %collective-permute-start.12) | collective-permute-done | bytes 442400 | tf_op jit(solution)/shard_map/ppermute | solution.py:302
  125.8 9.1 %collective-permute-done.2.refs_2_ = bf16[576,384]{1,0:T(8,128)(2,1)S(1)} collective-permute-done((bf16[576,384]{1,0:T(8,128)(2,1)S(1)}, bf16[576,384]{1,0:T(8,128)(2,1)S(1)}, u32[]{:S(2)}, u32[]{:S(2)}) %collective-permute-start.2) | collective-permute-done | bytes 442400 | tf_op jit(solution)/shard_map/ppermute | solution.py:302
  134.9 10.9 %collective-permute-done.13.refs_6_ = bf16[576,384]{1,0:T(8,128)(2,1)S(1)} collective-permute-done((bf16[576,384]{1,0:T(8,128)(2,1)S(1)}, bf16[576,384]{1,0:T(8,128)(2,1)S(1)}, u32[]{:S(2)}, u32[]{:S(2)}) %collective-permute-start.13) | collective-permute-done | bytes 442400 | tf_op jit(solution)/shard_map/ppermute | solution.py:302
  145.8 9.2 %shard_map.69 = (f32[576,640]{1,0:T(8,128)S(1)}, bf16[576,640]{1,0:T(8,128)(2,1)S(1)}, f32[576,1280]{1,0:T(8,128)}) custom-call(s32[7]{0:T(128)S(1)} %stack.126.info, bf16[576,384]{1,0:T(8,128)(2,1)} %shard_map.65.refs_0_, bf16[576,384]{1,0:T(8,128)(2,1)S(1)} %collective-permute-done.1.rest_8_.refs_1_, bf16[576,384]{1,0:T(8,128)(2,1)S(1)} %collective-permute-done.2.refs_2_, ...), custom_call_target="tpu_custom_call" | custom-call | tf_op jit(solution)/shard_map/pallas_call | solution.py:157
  154.9 2.4 %collective-permute-start.16 = (bf16[576,640]{1,0:T(8,128)(2,1)S(1)}, bf16[576,640]{1,0:T(8,128)(2,1)S(1)}, u32[]{:S(2)}, u32[]{:S(2)}) collective-permute-start(bf16[576,640]{1,0:T(8,128)(2,1)S(1)} %get-tuple-element.19), channel_id=1, source_target_pairs={{0,32},{32,0},{1,33},{33,1},{2,34},{34,2},{3,35},{35,3},{4,36},{36... | collective-permute-start | bytes 2211848 | tf_op jit(solution)/shard_map/ppermute | solution.py:322
  157.4 6.6 %shard_map.71 = (f32[576,640]{1,0:T(8,128)S(1)}, bf16[576,640]{1,0:T(8,128)(2,1)S(1)}) custom-call(s32[4]{0:T(128)S(1)} %pad_add_fusion.3.info, bf16[576,384]{1,0:T(8,128)(2,1)} %shard_map.66.refs_0_, bf16[576,384]{1,0:T(8,128)(2,1)} %collective-permute-done.10.rest_6_.rest_3_.refs_1_, bf16[576,384]{1,0:T(8,128)(2,1)S(1)} %collective-permute-done.19.refs_2_, ...), custom_call_target="tpu_custom_call" | custom-call | tf_op jit(solution)/shard_map/pallas_call | solution.py:157
  164.0 2.1 %collective-permute-start.20 = (bf16[576,640]{1,0:T(8,128)(2,1)S(1)}, bf16[576,640]{1,0:T(8,128)(2,1)S(1)}, u32[]{:S(2)}, u32[]{:S(2)}) collective-permute-start(bf16[576,640]{1,0:T(8,128)(2,1)S(1)} %get-tuple-element.24), channel_id=1, source_target_pairs={{0,32},{32,0},{1,33},{33,1},{2,34},{34,2},{3,35},{35,3},{4,36},{36... | collective-permute-start | bytes 2211848 | tf_op jit(solution)/shard_map/ppermute | solution.py:322
  166.1 3.9 %shard_map.70 = (f32[576,640]{1,0:T(8,128)S(1)}, bf16[576,640]{1,0:T(8,128)(2,1)S(1)}) custom-call(s32[1]{0:T(128)} %bitcast.6.info, bf16[576,384]{1,0:T(8,128)(2,1)S(1)} %collective-permute-done.17.piece, bf16[1536,1280]{1,0:T(8,128)(2,1)} %all-gather.2.cloned.1.call-done.refs_7_.w_ref.refs_4_, f32[576,1280]{1,0:T(8,128)S(1)} %copy-done.8), custom_call_target="tpu_custom_call" | custom-call | tf_op jit(solution)/shard_map/pallas_call | solution.py:157
  170.5 1.6 shard_map.72.refs_5_
  172.3 1.9 %shard_map.73 = bf16[1728,640]{1,0:T(8,128)(2,1)} custom-call(s32[4]{0:T(128)S(1)} %pad_add_fusion.info, f32[576,640]{1,0:T(8,128)S(1)} %get-tuple-element.18.refs_0_, bf16[576,640]{1,0:T(8,128)(2,1)S(1)} %collective-permute-done.16.refs_1_, f32[576,640]{1,0:T(8,128)S(1)} %get-tuple-element.21.refs_2_, ...), custom_call_target="tpu_custom_call", output_to_operand_aliasing={{}: (6, {})} | custom-call | tf_op jit(solution)/shard_map/pallas_call | solution.py:187
  (53 shorter events, 11.5 us)
Async XLA Ops:
  6.5 139.2 %all-gather.2.cloned.1.call-start = ((), (), s32[]{:S(2)}) async-start(), calls=%async_computation | async-start | bytes 4177920 | tf_op jit(solution)/shard_map/all_gather | solution.py:317
  7.9 14.0 %copy-start = (bf16[1728,384]{1,0:T(8,128)(2,1)S(1)}, bf16[1728,384]{1,0:T(8,128)(2,1)}, u32[]{:S(2)}) copy-start(bf16[1728,384]{1,0:T(8,128)(2,1)} %k_ref.5) | copy-start | bytes 3981316
  7.9 14.0 %copy-start.1 = (bf16[1728,384]{1,0:T(8,128)(2,1)S(1)}, bf16[1728,384]{1,0:T(8,128)(2,1)}, u32[]{:S(2)}) copy-start(bf16[1728,384]{1,0:T(8,128)(2,1)} %v_ref.5) | copy-start | bytes 3981316
  11.3 31.9 %collective-permute-start = (bf16[1152,384]{1,0:T(8,128)(2,1)}, bf16[1152,384]{1,0:T(8,128)(2,1)S(1)}, u32[]{:S(2)}, u32[]{:S(2)}) collective-permute-start(bf16[1152,384]{1,0:T(8,128)(2,1)} %get-tuple-element.15), channel_id=1, source_target_pairs={{0,1},{1,0},{2,3},{3,2},{4,5},{5,4},{6,7},{7,6},{8,9},{9,8},{10,11... | collective-permute-start | bytes 2654216 | tf_op jit(solution)/shard_map/ppermute | solution.py:263
  11.6 20.1 %collective-permute-start.14 = (bf16[96,640]{1,0:T(8,128)(2,1)}, bf16[96,640]{1,0:T(8,128)(2,1)}, u32[]{:S(2)}, u32[]{:S(2)}) collective-permute-start(bf16[96,640]{1,0:T(8,128)(2,1)} %own_ref.1), channel_id=1, source_target_pairs={{0,4},{4,0},{1,5},{5,1},{2,6},{6,2},{3,7},{7,3},{8,12},{12,8},{9,1... | collective-permute-start | bytes 368648 | tf_op jit(solution)/shard_map/ppermute | solution.py:314
  18.5 17.9 %collective-permute-start.4 = (bf16[576,384]{1,0:T(8,128)(2,1)}, bf16[576,384]{1,0:T(8,128)(2,1)}, u32[]{:S(2)}, u32[]{:S(2)}) collective-permute-start(bf16[576,384]{1,0:T(8,128)(2,1)} %get-tuple-element.16), channel_id=1, source_target_pairs={{0,3},{3,0},{1,2},{2,1},{4,7},{7,4},{5,6},{6,5},{8,11},{11,8},{9,1... | collective-permute-start | bytes 1327112 | tf_op jit(solution)/shard_map/ppermute | solution.py:264
  20.5 21.2 %collective-permute-start.7 = (bf16[576,384]{1,0:T(8,128)(2,1)}, bf16[576,384]{1,0:T(8,128)(2,1)}, u32[]{:S(2)}, u32[]{:S(2)}) collective-permute-start(bf16[576,384]{1,0:T(8,128)(2,1)} %get-tuple-element.17), channel_id=1, source_target_pairs={{0,1},{3,2},{4,5},{7,6},{8,9},{11,10},{12,13},{15,14},{16,17},{19,... | collective-permute-start | bytes 1327112 | tf_op jit(solution)/shard_map/ppermute | solution.py:265
  21.9 1.3 copy-start.5
  30.9 12.3 %collective-permute-start.10 = (bf16[576,384]{1,0:T(8,128)(2,1)}, bf16[576,384]{1,0:T(8,128)(2,1)}, u32[]{:S(2)}, u32[]{:S(2)}) collective-permute-start(bf16[576,384]{1,0:T(8,128)(2,1)} %shard_map.66.refs_0_), channel_id=1, source_target_pairs={{0,64},{64,128},{128,192},{192,0},{1,65},{65,129},{129,193},{193,1... | collective-permute-start | bytes 1327112 | tf_op jit(solution)/shard_map/ppermute | solution.py:302
  33.2 3.1 %collective-permute-start.15 = (bf16[96,640]{1,0:T(8,128)(2,1)}, bf16[96,640]{1,0:T(8,128)(2,1)}, u32[]{:S(2)}, u32[]{:S(2)}) collective-permute-start(bf16[96,640]{1,0:T(8,128)(2,1)} %broadcast_select_fusion), channel_id=1, source_target_pairs={{0,32},{32,0},{1,33},{33,1},{2,34},{34,2},{3,35},{35,3},{4,36},{36... | collective-permute-start | bytes 368648 | tf_op jit(solution)/shard_map/ppermute | solution.py:315
  43.2 0.9 copy-start.2
  45.9 24.4 %collective-permute-start.5 = (bf16[576,384]{1,0:T(8,128)(2,1)}, bf16[576,384]{1,0:T(8,128)(2,1)}, u32[]{:S(2)}, u32[]{:S(2)}) collective-permute-start(bf16[576,384]{1,0:T(8,128)(2,1)} %get-tuple-element.17), channel_id=1, source_target_pairs={{1,2},{2,1},{5,6},{6,5},{9,10},{10,9},{13,14},{14,13},{17,18},{18,... | collective-permute-start | bytes 1327112 | tf_op jit(solution)/shard_map/ppermute | solution.py:266
  47.8 25.7 %collective-permute-start.8 = (bf16[576,384]{1,0:T(8,128)(2,1)}, bf16[576,384]{1,0:T(8,128)(2,1)}, u32[]{:S(2)}, u32[]{:S(2)}) collective-permute-start(bf16[576,384]{1,0:T(8,128)(2,1)} %collective-permute-done.7.rest_1_), channel_id=1, source_target_pairs={{2,6},{6,10},{10,14},{14,18},{18,22},{22,26},{26,30},{5,1},{9,5},{... | collective-permute-start | bytes 1327112 | tf_op jit(solution)/shard_map/ppermute | solution.py:272
  56.6 29.7 %collective-permute-start.11 = (bf16[576,384]{1,0:T(8,128)(2,1)}, bf16[576,384]{1,0:T(8,128)(2,1)}, u32[]{:S(2)}, u32[]{:S(2)}) collective-permute-start(bf16[576,384]{1,0:T(8,128)(2,1)} %shard_map.66.refs_0_), channel_id=1, source_target_pairs={{0,192},{64,0},{128,64},{192,128},{1,193},{65,1},{129,65},{193,129... | collective-permute-start | bytes 1327112 | tf_op jit(solution)/shard_map/ppermute | solution.py:302
  58.4 27.9 %collective-permute-start.6 = (bf16[576,384]{1,0:T(8,128)(2,1)}, bf16[576,384]{1,0:T(8,128)(2,1)}, u32[]{:S(2)}, u32[]{:S(2)}) collective-permute-start(bf16[576,384]{1,0:T(8,128)(2,1)} %collective-permute-done.4.rest_2_.rest_0_), channel_id=1, source_target_pairs={{0,4},{4,8},{8,12},{12,16},{16,20},{20,24},{24,28},{7,3},{11,7},{1... | collective-permute-start | bytes 1327112 | tf_op jit(solution)/shard_map/ppermute | solution.py:272
  59.8 1.2 copy-start.3
  61.0 1.4 copy-start.6
  62.4 42.1 %copy-start.4 = (bf16[1152,384]{1,0:T(8,128)(2,1)S(1)}, bf16[1152,384]{1,0:T(8,128)(2,1)}, u32[]{:S(2)}) copy-start(bf16[1152,384]{1,0:T(8,128)(2,1)} %copy-done.2) | copy-start | bytes 2654212
  70.3 23.8 %collective-permute-start.1 = (bf16[576,384]{1,0:T(8,128)(2,1)}, bf16[576,384]{1,0:T(8,128)(2,1)S(1)}, u32[]{:S(2)}, u32[]{:S(2)}) collective-permute-start(bf16[576,384]{1,0:T(8,128)(2,1)} %shard_map.65.refs_0_), channel_id=1, source_target_pairs={{0,64},{64,128},{128,192},{192,0},{1,65},{65,129},{129,193},{193,1... | collective-permute-start | bytes 1327112 | tf_op jit(solution)/shard_map/ppermute | solution.py:302
  70.3 34.2 %collective-permute-start.3 = (bf16[576,384]{1,0:T(8,128)(2,1)}, bf16[576,384]{1,0:T(8,128)(2,1)S(1)}, u32[]{:S(2)}, u32[]{:S(2)}) collective-permute-start(bf16[576,384]{1,0:T(8,128)(2,1)} %shard_map.65.refs_0_), channel_id=1, source_target_pairs={{0,192},{64,0},{128,64},{192,128},{1,193},{65,1},{129,65},{193,129... | collective-permute-start | bytes 1327112 | tf_op jit(solution)/shard_map/ppermute | solution.py:302
  73.5 30.9 %collective-permute-start.9 = (bf16[576,384]{1,0:T(8,128)(2,1)}, bf16[576,384]{1,0:T(8,128)(2,1)S(1)}, u32[]{:S(2)}, u32[]{:S(2)}) collective-permute-start(bf16[576,384]{1,0:T(8,128)(2,1)} %collective-permute-done.8), channel_id=1, source_target_pairs={{2,0},{1,3},{6,4},{5,7},{10,8},{9,11},{14,12},{13,15},{18,16},{17,... | collective-permute-start | bytes 1327112 | tf_op jit(solution)/shard_map/ppermute | solution.py:275
  104.5 1.4 copy-start.7
  113.9 11.5 %collective-permute-start.12 = (bf16[576,384]{1,0:T(8,128)(2,1)S(1)}, bf16[576,384]{1,0:T(8,128)(2,1)S(1)}, u32[]{:S(2)}, u32[]{:S(2)}) collective-permute-start(bf16[576,384]{1,0:T(8,128)(2,1)S(1)} %shard_map.67.refs_4_), channel_id=1, source_target_pairs={{0,64},{64,128},{128,192},{192,0},{1,65},{65,129},{129,193},{193,1... | collective-permute-start | bytes 1327112 | tf_op jit(solution)/shard_map/ppermute | solution.py:302
  114.9 20.0 %collective-permute-start.2 = (bf16[576,384]{1,0:T(8,128)(2,1)S(1)}, bf16[576,384]{1,0:T(8,128)(2,1)S(1)}, u32[]{:S(2)}, u32[]{:S(2)}) collective-permute-start(bf16[576,384]{1,0:T(8,128)(2,1)S(1)} %collective-permute-done.1.rest_8_.refs_1_), channel_id=1, source_target_pairs={{0,64},{64,128},{128,192},{192,0},{1,65},{65,129},{129,193},{193,1... | collective-permute-start | bytes 1327112 | tf_op jit(solution)/shard_map/ppermute | solution.py:302
  114.9 30.8 %collective-permute-start.13 = (bf16[576,384]{1,0:T(8,128)(2,1)S(1)}, bf16[576,384]{1,0:T(8,128)(2,1)S(1)}, u32[]{:S(2)}, u32[]{:S(2)}) collective-permute-start(bf16[576,384]{1,0:T(8,128)(2,1)S(1)} %shard_map.67.refs_4_), channel_id=1, source_target_pairs={{0,192},{64,0},{128,64},{192,128},{1,193},{65,1},{129,65},{193,129... | collective-permute-start | bytes 1327112 | tf_op jit(solution)/shard_map/ppermute | solution.py:302
  118.1 39.3 %collective-permute-start.19 = (bf16[576,384]{1,0:T(8,128)(2,1)}, bf16[576,384]{1,0:T(8,128)(2,1)S(1)}, u32[]{:S(2)}, u32[]{:S(2)}) collective-permute-start(bf16[576,384]{1,0:T(8,128)(2,1)} %collective-permute-done.10.rest_6_.rest_3_.refs_1_), channel_id=1, source_target_pairs={{0,64},{64,128},{128,192},{192,0},{1,65},{65,129},{129,193},{193,1... | collective-permute-start | bytes 1327112 | tf_op jit(solution)/shard_map/ppermute | solution.py:302
  125.4 40.6 %collective-permute-start.17 = (bf16[576,384]{1,0:T(8,128)(2,1)S(1)}, bf16[576,384]{1,0:T(8,128)(2,1)S(1)}, u32[]{:S(2)}, u32[]{:S(2)}) collective-permute-start(bf16[576,384]{1,0:T(8,128)(2,1)S(1)} %collective-permute-done.12.refs_5_), channel_id=1, source_target_pairs={{0,64},{64,128},{128,192},{192,0},{1,65},{65,129},{129,193},{193,1... | collective-permute-start | bytes 1327112 | tf_op jit(solution)/shard_map/ppermute | solution.py:302
  154.9 11.1 %copy-start.8 = (f32[576,1280]{1,0:T(8,128)S(1)}, f32[576,1280]{1,0:T(8,128)}, u32[]{:S(2)}) copy-start(f32[576,1280]{1,0:T(8,128)} %get-tuple-element.20.so_far) | copy-start | bytes 8847364
  154.9 17.2 %collective-permute-start.16 = (bf16[576,640]{1,0:T(8,128)(2,1)S(1)}, bf16[576,640]{1,0:T(8,128)(2,1)S(1)}, u32[]{:S(2)}, u32[]{:S(2)}) collective-permute-start(bf16[576,640]{1,0:T(8,128)(2,1)S(1)} %get-tuple-element.19), channel_id=1, source_target_pairs={{0,32},{32,0},{1,33},{33,1},{2,34},{34,2},{3,35},{35,3},{4,36},{36... | collective-permute-start | bytes 2211848 | tf_op jit(solution)/shard_map/ppermute | solution.py:322
  164.0 6.5 %collective-permute-start.20 = (bf16[576,640]{1,0:T(8,128)(2,1)S(1)}, bf16[576,640]{1,0:T(8,128)(2,1)S(1)}, u32[]{:S(2)}, u32[]{:S(2)}) collective-permute-start(bf16[576,640]{1,0:T(8,128)(2,1)S(1)} %get-tuple-element.24), channel_id=1, source_target_pairs={{0,32},{32,0},{1,33},{33,1},{2,34},{34,2},{3,35},{35,3},{4,36},{36... | collective-permute-start | bytes 2211848 | tf_op jit(solution)/shard_map/ppermute | solution.py:322
  166.1 4.3 %copy-start.9 = (f32[640]{0:T(1024)S(1)}, f32[640]{0:T(1024)}, u32[]{:S(2)}) copy-start(f32[640]{0:T(1024)} %param.11) | copy-start | bytes 7684
  170.0 2.3 %collective-permute-start.18 = (bf16[576,640]{1,0:T(8,128)(2,1)S(1)}, bf16[576,640]{1,0:T(8,128)(2,1)S(1)}, u32[]{:S(2)}, u32[]{:S(2)}) collective-permute-start(bf16[576,640]{1,0:T(8,128)(2,1)S(1)} %get-tuple-element.22), channel_id=1, source_target_pairs={{0,32},{32,0},{1,33},{33,1},{2,34},{34,2},{3,35},{35,3},{4,36},{36... | collective-permute-start | bytes 2211848 | tf_op jit(solution)/shard_map/ppermute | solution.py:322
Sparse Core Ops, SparseCore 0:
  46.0 66.7 all-gather.1

commit v4 on v3

v4 whole, which is shorter than its diff:
```python
import functools

import jax
import jax.numpy as jnp
from jax import lax
from jax.experimental import pallas as pl
from jax.experimental.pallas import tpu as pltpu
from jax.sharding import Mesh
from jax.sharding import PartitionSpec as P

HEAD = 128
TILE = 192
FRAME = 576
LN2 = 0.6931471805599453
SCALE = HEAD**-0.5 / LN2
FAR = 1e30
SEQ = ("y", "zh", "x")
FSDP = ("zl", "core")
VMEM = 48 * 1024 * 1024
FREE = pl.CostEstimate(flops=0, bytes_accessed=0, transcendentals=0)


def attend_body(halo_total, info, q_ref, k_ref, v_ref, *rest):
    halos, (o_ref, kbuf, vbuf) = rest[:halo_total], rest[-3:]
    slot, prev_from, next_from, prev_ok, next_ok, active = (info[i] for i in range(6))

    @pl.when(active == 0)
    def _():
        o_ref[...] = jnp.zeros_like(o_ref)

    def fill(place, source):
        rows = pl.ds(place * FRAME, FRAME)

        @pl.when(source < 3)
        def _():
            local = pl.ds(pl.multiple_of(jnp.clip(source, 0, 2) * FRAME, FRAME), FRAME)
            kbuf[rows, :] = k_ref[local, :]
            vbuf[rows, :] = v_ref[local, :]

        for i in range(halo_total // 2):

            @pl.when(source == 3 + i)
            def _():
                kbuf[rows, :] = halos[2 * i][...]
                vbuf[rows, :] = halos[2 * i + 1][...]

    @pl.when(active == 1)
    def _():
        fill(0, prev_from)
        fill(1, slot)
        fill(2, next_from)
        off = [jnp.where(prev_ok == 1, 0.0, FAR), jnp.float32(0.0), jnp.where(next_ok == 1, 0.0, FAR)]
        for w in range(3):
            low, high = max(0, w - 1) * TILE, min(3, w + 2) * TILE
            q = q_ref[pl.ds(pl.multiple_of(slot * FRAME + w * TILE, TILE), TILE), :]
            scores, tops = [], []
            for f in range(3):
                keys = kbuf[f * FRAME + low : f * FRAME + high, :]
                s = lax.dot_general(q, keys, (((1,), (1,)), ((), ())), preferred_element_type=jnp.float32)
                scores.append(s)
                tops.append(jnp.max(s, axis=1, keepdims=True) * SCALE - off[f])
            top = jnp.maximum(jnp.maximum(tops[0], tops[1]), tops[2])
            total, mass = None, None
            for f in range(3):
                p = jnp.exp2(scores[f] * SCALE - (top + off[f]))
                values = vbuf[f * FRAME + low : f * FRAME + high, :]
                part = jnp.dot(p.astype(jnp.bfloat16), values, preferred_element_type=jnp.float32)
                row = jnp.sum(p, axis=1, keepdims=True)
                total, mass = (part, row) if total is None else (total + part, mass + row)
            o_ref[w * TILE : (w + 1) * TILE, :] = (total / mass).astype(jnp.bfloat16)


def attend(info, query, key, value, halos, after):
    rows, width = query.shape
    heads = width // HEAD
    column = lambda h, info: (0, h)
    whole = pl.BlockSpec((rows, HEAD), column)
    one = pl.BlockSpec((FRAME, HEAD), column)
    where = [pl.BlockSpec((FRAME, HEAD), lambda h, info, r=r: (r, h)) for _, r in halos]
    return pl.pallas_call(
        functools.partial(attend_body, len(halos)),
        out_shape=jax.ShapeDtypeStruct((FRAME, width), jnp.bfloat16),
        grid_spec=pltpu.PrefetchScalarGridSpec(
            num_scalar_prefetch=1,
            grid=(heads,),
            in_specs=[whole] * 3 + where + [pl.BlockSpec(memory_space=pl.ANY)] * len(after),
            out_specs=one,
            scratch_shapes=[
                pltpu.VMEM((3 * FRAME, HEAD), jnp.bfloat16),
                pltpu.VMEM((3 * FRAME, HEAD), jnp.bfloat16),
            ],
        ),
        compiler_params=pltpu.CompilerParams(vmem_limit_bytes=VMEM),
        cost_estimate=FREE,
    )(info, query, key, value, *[array for array, _ in halos], *after)


def line_up(info, at, pieces, line):
    width = pieces[0].shape[1]
    if len(pieces) * width < line.shape[1]:
        line[...] = jnp.zeros_like(line)
    for k, piece in enumerate(pieces):
        line[:, pl.ds(pl.multiple_of(info[at + k] * width, width), width)] = piece[...]


def project_body(split, info, *refs):
    total = sum(split)
    pieces, w_ref = refs[:total], refs[total]
    mine_ref, other_ref, line = refs[-3:]
    rows, columns = line.shape[0], mine_ref.shape[1]
    at = 0
    for c, size in enumerate(split):
        line_up(info, at, pieces[at : at + size], line)
        at += size
        share = jnp.dot(line[...], w_ref[...], preferred_element_type=jnp.float32)
        mine_ref[c * rows : (c + 1) * rows, :] = share[:, :columns].astype(mine_ref.dtype)
        other_ref[c * rows : (c + 1) * rows, :] = share[:, columns:].astype(other_ref.dtype)


def project_last_body(info, piece, w_ref, mine_far, other_far, mine_ref, other_ref):
    columns = mine_ref.shape[1]
    total = jnp.dot(piece[...], w_ref[...], preferred_element_type=jnp.float32)
    mine_ref[...] = total[:, :columns] + mine_far[...]
    other_ref[...] = (total[:, columns:] + other_far[...]).astype(other_ref.dtype)


def project(order, chunks, weight, dtypes, after=()):
    rows, width = chunks[0][0].shape
    depth, both = weight.shape
    fixed = lambda j, info: (0, 0)
    pieces = [piece for chunk in chunks for piece in chunk]
    tall = (len(chunks) * rows, both // 2)
    return pl.pallas_call(
        functools.partial(project_body, [len(chunk) for chunk in chunks]),
        out_shape=[jax.ShapeDtypeStruct(tall, dtype) for dtype in dtypes],
        grid_spec=pltpu.PrefetchScalarGridSpec(
            num_scalar_prefetch=1,
            grid=(1,),
            in_specs=[pl.BlockSpec((rows, width), fixed)] * len(pieces)
            + [pl.BlockSpec((depth, both), fixed)]
            + [pl.BlockSpec(memory_space=pl.ANY)] * len(after),
            out_specs=[pl.BlockSpec(tall, fixed)] * 2,
            scratch_shapes=[pltpu.VMEM((rows, depth), jnp.bfloat16)],
        ),
        compiler_params=pltpu.CompilerParams(vmem_limit_bytes=VMEM),
        cost_estimate=FREE,
    )(order, *pieces, weight, *after)


def project_last(order, piece, weight, mine_far, other_far):
    rows, width = piece.shape
    both = weight.shape[1]
    fixed = lambda j, info: (0, 0)
    out = pl.BlockSpec((rows, both // 2), fixed)
    return pl.pallas_call(
        project_last_body,
        out_shape=[jax.ShapeDtypeStruct((rows, both // 2), dtype) for dtype in (jnp.float32, jnp.bfloat16)],
        grid_spec=pltpu.PrefetchScalarGridSpec(
            num_scalar_prefetch=1,
            grid=(1,),
            in_specs=[
                pl.BlockSpec((rows, width), fixed),
                pl.BlockSpec((width, both), lambda j, info: (info[0], 0)),
                out,
                out,
            ],
            out_specs=[out] * 2,
        ),
        compiler_params=pltpu.CompilerParams(vmem_limit_bytes=VMEM),
        cost_estimate=FREE,
    )(order, piece, weight, mine_far, other_far)


def finish_body(total, info, mine_ref, received_ref, bias_ref, *rest):
    value = mine_ref[...] + received_ref[...].astype(jnp.float32) + bias_ref[...]
    active = info[total + pl.program_id(0)]
    rest[-1][...] = jnp.where(active == 1, value, 0.0).astype(jnp.bfloat16)


def finish(info, mine, received, bias, out):
    rows, columns = mine.shape
    total = rows // FRAME
    block = pl.BlockSpec((FRAME, columns), lambda j, info: (j, 0))
    extra = [] if out is None else [out]
    return pl.pallas_call(
        functools.partial(finish_body, total),
        out_shape=jax.ShapeDtypeStruct((3 * FRAME, columns), jnp.bfloat16),
        grid_spec=pltpu.PrefetchScalarGridSpec(
            num_scalar_prefetch=1,
            grid=(total,),
            in_specs=[block, block, pl.BlockSpec((1, columns), lambda j, info: (0, 0))]
            + [pl.BlockSpec(memory_space=pl.ANY)] * len(extra),
            out_specs=pl.BlockSpec((FRAME, columns), lambda j, info: (info[j], 0)),
        ),
        input_output_aliases={4: 0} if extra else {},
        compiler_params=pltpu.CompilerParams(vmem_limit_bytes=VMEM),
        cost_estimate=FREE,
    )(info, mine, received, bias.reshape(1, columns), *extra)


def pack_body(info, k0_ref, v0_ref, k1_ref, v1_ref, *rest):
    near_ref, key_ref, value_ref = rest[-3:]
    near_ref[:FRAME, :] = k0_ref[...]
    near_ref[FRAME:, :] = v0_ref[...]
    key_ref[...] = k1_ref[...]
    value_ref[...] = v1_ref[...]


def pack(info, key, value, after):
    width = key.shape[1]
    frames = [pl.BlockSpec((FRAME, width), lambda i, info, c=c: (info[c], 0)) for c in (0, 0, 1, 1)]
    heights = (2 * FRAME, FRAME, FRAME)
    return pl.pallas_call(
        pack_body,
        out_shape=[jax.ShapeDtypeStruct((rows, width), key.dtype) for rows in heights],
        grid_spec=pltpu.PrefetchScalarGridSpec(
            num_scalar_prefetch=1,
            grid=(1,),
            in_specs=frames + [pl.BlockSpec(memory_space=pl.ANY)] * len(after),
            out_specs=[pl.BlockSpec((rows, width), lambda i, info: (0, 0)) for rows in heights],
        ),
        compiler_params=pltpu.CompilerParams(vmem_limit_bytes=60 * 1024 * 1024),
        cost_estimate=FREE,
    )(info, key, value, key, value, *after)


def lay_body(home, own_ref, over_ref, beside_ref, *rest):
    out_ref = rest[-1]
    columns = own_ref.shape[1]
    out_ref[:, :columns] = jnp.where(home[0] == 1, own_ref[...], over_ref[...])
    out_ref[:, columns:] = beside_ref[...]


def lay(home, own, over, beside, after):
    rows, columns = own.shape
    vmem = pl.BlockSpec(memory_space=pltpu.VMEM)
    return pl.pallas_call(
        lay_body,
        out_shape=jax.ShapeDtypeStruct((rows, 2 * columns), own.dtype),
        in_specs=[pl.BlockSpec(memory_space=pltpu.SMEM)]
        + [vmem] * 3
        + [pl.BlockSpec(memory_space=pl.ANY)] * len(after),
        out_specs=vmem,
        cost_estimate=FREE,
    )(home, own, over, beside, *after)


def on_device(query, key, value, slab_counts, out_weight, out_bias):
    count = slab_counts[0]
    x, y, zh, zl, core = (lax.axis_index(name) for name in ("x", "y", "zh", "zl", "core"))
    seq = lax.axis_index(SEQ)
    seq_width, row = lax.axis_size(SEQ), lax.axis_size("x")
    even = x % 2 == 0
    last = count - 1

    near_slot = jnp.where(even, last, 0)
    away_slot = jnp.where(even, 0, last)

    slots = [
        jnp.where(count == 3, 1, jnp.where(count == 2, 2, 1)),
        jnp.where(count == 1, 2, near_slot),
        jnp.where(count == 1, 0, away_slot),
    ]
    actives = [count == 3, count >= 2, count >= 1]
    away_from = jnp.where((x == 1) | (x == 2), 4, 5)

    def frame(c, halos, after):
        slot = slots[c]
        prev_from = jnp.where(slot > 0, slot - 1, jnp.where(even, away_from, 3))
        next_from = jnp.where(slot < last, slot + 1, jnp.where(even, 3, away_from))
        prev_ok = (slot > 0) | (seq > 0)
        next_ok = (slot < last) | (seq < seq_width - 1)
        info = jnp.stack(
            [v.astype(jnp.int32) for v in (slot, prev_from, next_from, prev_ok, next_ok, actives[c])]
        )
        return attend(info, query, key, value, halos, after)

    lines = lax.axis_size("zl")

    def along(value, steps):
        return lax.ppermute(value, "zl", [(i, (i + steps) % lines) for i in range(lines)])

    a = frame(0, [], [])
    a1, a3 = along(a, 1), along(a, -1)
    near_pack, away_key, away_value = pack(jnp.stack([near_slot, away_slot]), key, value, [])
    near = lax.ppermute(near_pack, "x", [(0, 1), (1, 0), (2, 3), (3, 2)])
    key_round = lax.ppermute(away_key, "x", [(0, 3), (3, 0), (1, 2), (2, 1)])
    value_side = lax.ppermute(away_value, "x", [(0, 1), (3, 2)])
    value_inner = lax.ppermute(away_value, "x", [(1, 2), (2, 1)])

    def across_rows(value, up, down):
        rows = range(seq_width // row - 1)
        pairs = [(r * row + up, (r + 1) * row + up) for r in rows]
        pairs += [((r + 1) * row + down, r * row + down) for r in rows]
        return lax.ppermute(value, SEQ, pairs)

    key_far = across_rows(key_round, 0, 3)
    value_mid = across_rows(value_side, 2, 1)
    value_far = lax.ppermute(value_mid, "x", [(2, 0), (1, 3)])
    near_halo = [(near, 0), (near, 1)]
    inner_halo = [(key_round, 0), (value_inner, 0)]
    far_halo = [(key_far, 0), (value_far, 0)]

    b = frame(1, near_halo, [])
    b1, b3 = along(b, 1), along(b, -1)
    a2, b2 = along(a1, 1), along(b1, 1)
    home = zh == core
    over = lax.ppermute(out_weight, "zh", [(0, 1), (1, 0)])
    beside = lax.ppermute(jnp.where(home, over, out_weight), "core", [(0, 1), (1, 0)])
    laid = lay(home.astype(jnp.int32).reshape(1), out_weight, over, beside, [key_round, value_side, a])
    weight = lax.all_gather(laid, ("y", "x"), axis=0, tiled=True)

    c = frame(2, near_halo + inner_halo + far_halo, [b1])
    c1, c3 = along(c, 1), along(c, -1)
    c2 = along(c1, 1)

    order = [((zl - k) % lines).astype(jnp.int32) for k in range(lines)]

    def swap(value):
        return lax.ppermute(value, "core", [(0, 1), (1, 0)])

    def put(indices, mine, received, out):
        info = jnp.stack([v[i].astype(jnp.int32) for v in (slots, actives) for i in indices])
        return finish(info, mine, received, out_bias, out)

    types = (jnp.float32, jnp.bfloat16)
    own_a, other_a = project(jnp.stack(order), [[a, a1, a2, a3]], weight, types, [])
    own_b, other_b = project(jnp.stack(order), [[b, b1, b2, b3]], weight, types)
    so_far = project(
        jnp.stack([order[0], order[1], order[3]]), [[c, c1, c3]], weight, (jnp.bfloat16, jnp.bfloat16)
    )
    own_c, other_c = project_last(order[2].reshape(1), c2, weight, *so_far)
    out = put([0], own_a, swap(other_a), None)
    out = put([1], own_b, swap(other_b), out)
    out = put([2], own_c, swap(other_c), out)
    return out.T


def solution(mesh):
    fine = Mesh(mesh.devices.reshape(4, 2, 4, 2, 4), FSDP + SEQ)
    tiles = P(SEQ, FSDP)
    return jax.shard_map(
        on_device,
        mesh=fine,
        in_specs=(tiles, tiles, tiles, P(SEQ), tiles, P(FSDP)),
        out_specs=P(FSDP, SEQ),
        check_vma=False,
    )
```

time: 182 us -> 179 us (0.984)
  the two profiles are of different devices: /device:TPU:27 before, /device:TPU:9 now
where the time goes in v4:
time: 179 us; the launch traced here: 176 us
  waiting for transfers between devices  60.9 us (34%)
  Pallas kernels  52.9 us (30%)
  starting transfers between devices  39.3 us (22%)
  between operations  14.2 us (8%)
  local copies, waits for them, and re-layouts  7.84 us (4%)
    ppermute x9, waiting for transfers between devices, along(): lax.ppermute(value, 'zl', [(i, (i + steps) % lines) for i in range(lines)])  42.6 us
    pallas_call x3, Pallas kernels, attend(): pl.pallas_call(functools.partial(attend_body, len(halos)), out_shape=jax....  24.2 us
    ppermute x1, waiting for transfers between devices, on_device(): near = lax.ppermute(near_pack, 'x', [(0, 1), (1, 0), (2, 3), (3, 2)])  17.7 us
    pallas_call x3, Pallas kernels, project(): pl.pallas_call(functools.partial(project_body, [len(chunk) for chunk in c...  16.5 us
    ppermute x3, starting transfers between devices, swap(): return lax.ppermute(value, 'core', [(0, 1), (1, 0)])  10.4 us
    unnamed x26, local copies, waits for them, and re-layouts  7.59 us
    ppermute x9, starting transfers between devices, along(): lax.ppermute(value, 'zl', [(i, (i + steps) % lines) for i in range(lines)])  7.55 us
    ppermute x1, starting transfers between devices, on_device(): over = lax.ppermute(out_weight, 'zh', [(0, 1), (1, 0)])  6.91 us
  transfers between devices with their start and end apart: 22, of which 10 were waited for; matrix products, arithmetic and copies ran while one was open for 1% of the time, Pallas kernels for 28%

profile of v4, /device:TPU:9, one launch (start us, length us, event | category | flops | bytes accessed | tf_op | source)
XLA Modules:
  0.0 176.2 jit_solution(4776414629676290500)
XLA Ops:
  6.5 6.9 %collective-permute-start.10 = (bf16[96,640]{1,0:T(8,128)(2,1)}, bf16[96,640]{1,0:T(8,128)(2,1)S(1)}, u32[]{:S(2)}, u32[]{:S(2)}) collective-permute-start(bf16[96,640]{1,0:T(8,128)(2,1)} %own_ref.1), channel_id=1, source_target_pairs={{0,4},{4,0},{1,5},{5,1},{2,6},{6,2},{3,7},{7,3},{8,12},{12,8},{9,1... | collective-permute-start | bytes 368648 | tf_op jit(solution)/shard_map/ppermute | solution.py:308
  14.7 3.5 %shard_map.64 = (bf16[1152,384]{1,0:T(8,128)(2,1)}, bf16[576,384]{1,0:T(8,128)(2,1)}, bf16[576,384]{1,0:T(8,128)(2,1)}) custom-call(s32[2]{0:T(128)} %pad_add_fusion.1.info, bf16[1728,384]{1,0:T(8,128)(2,1)} %k_ref.5, bf16[1728,384]{1,0:T(8,128)(2,1)} %v_ref.5, bf16[1728,384]{1,0:T(8,128)(2,1)} %k_ref.5, bf16[1728,384]{1,0:T(8,128)(2,1)} %v_ref.5), custom_call_target="tpu_custom_call" | custom-call | tf_op jit(solution)/shard_map/pallas_call | solution.py:213
  18.3 2.5 %collective-permute-start.1 = (bf16[576,384]{1,0:T(8,128)(2,1)}, bf16[576,384]{1,0:T(8,128)(2,1)S(1)}, u32[]{:S(2)}, u32[]{:S(2)}) collective-permute-start(bf16[576,384]{1,0:T(8,128)(2,1)} %get-tuple-element.17), channel_id=1, source_target_pairs={{0,3},{3,0},{1,2},{2,1},{4,7},{7,4},{5,6},{6,5},{8,11},{11,8},{9,1... | collective-permute-start | bytes 1327112 | tf_op jit(solution)/shard_map/ppermute | solution.py:287
  20.7 2.6 %collective-permute-start.4 = (bf16[576,384]{1,0:T(8,128)(2,1)}, bf16[576,384]{1,0:T(8,128)(2,1)}, u32[]{:S(2)}, u32[]{:S(2)}) collective-permute-start(bf16[576,384]{1,0:T(8,128)(2,1)} %get-tuple-element.18), channel_id=1, source_target_pairs={{0,1},{3,2},{4,5},{7,6},{8,9},{11,10},{12,13},{15,14},{16,17},{19,... | collective-permute-start | bytes 1327112 | tf_op jit(solution)/shard_map/ppermute | solution.py:288
  23.4 1.6 collective-permute-start.11
  26.4 7.7 %shard_map.67.rest_2_.refs_0_ = bf16[576,384]{1,0:T(8,128)(2,1)} custom-call(s32[6]{0:T(128)S(1)} %stack.147.info, bf16[1728,384]{1,0:T(8,128)(2,1)S(1)} %copy-done.2, bf16[1728,384]{1,0:T(8,128)(2,1)S(1)} %copy-done, bf16[1728,384]{1,0:T(8,128)(2,1)S(1)} %copy-done.1), custom_call_target="tpu_custom_call" | custom-call | tf_op jit(solution)/shard_map/pallas_call | solution.py:80
  34.9 1.8 shard_map.68
  36.8 1.5 collective-permute-start.5
  38.2 1.4 collective-permute-start.2
  39.7 3.5 %collective-permute-start.3 = (bf16[576,384]{1,0:T(8,128)(2,1)}, bf16[576,384]{1,0:T(8,128)(2,1)}, u32[]{:S(2)}, u32[]{:S(2)}) collective-permute-start(bf16[576,384]{1,0:T(8,128)(2,1)} %copy-done.5), channel_id=1, source_target_pairs={{0,4},{4,8},{8,12},{12,16},{16,20},{20,24},{24,28},{7,3},{11,7},{1... | collective-permute-start | bytes 1327112 | tf_op jit(solution)/shard_map/ppermute | solution.py:295
  44.5 17.7 %collective-permute-done.rest_0_.rest_1_ = bf16[1152,384]{1,0:T(8,128)(2,1)S(1)} collective-permute-done((bf16[1152,384]{1,0:T(8,128)(2,1)}, bf16[1152,384]{1,0:T(8,128)(2,1)S(1)}, u32[]{:S(2)}, u32[]{:S(2)}) %collective-permute-start) | collective-permute-done | bytes 884768 | tf_op jit(solution)/shard_map/ppermute | solution.py:286
  63.6 7.8 %shard_map.65.refs_0_ = bf16[576,384]{1,0:T(8,128)(2,1)} custom-call(s32[6]{0:T(128)S(1)} %stack.140.info, bf16[1728,384]{1,0:T(8,128)(2,1)S(1)} %copy-done.3, bf16[1728,384]{1,0:T(8,128)(2,1)S(1)} %copy-done, bf16[1728,384]{1,0:T(8,128)(2,1)S(1)} %copy-done.1, bf16[1152,384]{1,0:T(8,128)(2,1)S(1)} %collective-permute-done.rest_0_.rest_1_, ...), custom_call_target="tpu_custom_call" | custom-call | tf_op jit(solution)/shard_map/pallas_call | solution.py:80
  73.0 2.8 %collective-permute-start.15 = (bf16[576,384]{1,0:T(8,128)(2,1)}, bf16[576,384]{1,0:T(8,128)(2,1)S(1)}, u32[]{:S(2)}, u32[]{:S(2)}) collective-permute-start(bf16[576,384]{1,0:T(8,128)(2,1)} %shard_map.65.refs_0_), channel_id=1, source_target_pairs={{0,192},{64,0},{128,64},{192,128},{1,193},{65,1},{129,65},{193,129... | collective-permute-start | bytes 1327112 | tf_op jit(solution)/shard_map/ppermute | solution.py:281
  76.4 7.7 %collective-permute-done.7.rest_6_.refs_1_ = bf16[576,384]{1,0:T(8,128)(2,1)} collective-permute-done((bf16[576,384]{1,0:T(8,128)(2,1)}, bf16[576,384]{1,0:T(8,128)(2,1)}, u32[]{:S(2)}, u32[]{:S(2)}) %collective-permute-start.7) | collective-permute-done | bytes 442400 | tf_op jit(solution)/shard_map/ppermute | solution.py:281
  86.4 8.7 %shard_map.66.refs_0_ = bf16[576,384]{1,0:T(8,128)(2,1)} custom-call(s32[6]{0:T(128)S(1)} %stack.129.info, bf16[1728,384]{1,0:T(8,128)(2,1)S(1)} %copy-done.4, bf16[1728,384]{1,0:T(8,128)(2,1)S(1)} %copy-done, bf16[1728,384]{1,0:T(8,128)(2,1)} %v_ref.5, bf16[1152,384]{1,0:T(8,128)(2,1)S(1)} %collective-permute-done.rest_0_.rest_1_, ...), custom_call_target="tpu_custom_call" | custom-call | tf_op jit(solution)/shard_map/pallas_call | solution.py:80
  95.2 3.1 %collective-permute-start.19 = (bf16[576,384]{1,0:T(8,128)(2,1)}, bf16[576,384]{1,0:T(8,128)(2,1)S(1)}, u32[]{:S(2)}, u32[]{:S(2)}) collective-permute-start(bf16[576,384]{1,0:T(8,128)(2,1)} %shard_map.67.rest_2_.refs_0_), channel_id=1, source_target_pairs={{0,192},{64,0},{128,64},{192,128},{1,193},{65,1},{129,65},{193,129... | collective-permute-start | bytes 1327112 | tf_op jit(solution)/shard_map/ppermute | solution.py:281
  98.3 7.6 %collective-permute-done.15.refs_3_ = bf16[576,384]{1,0:T(8,128)(2,1)S(1)} collective-permute-done((bf16[576,384]{1,0:T(8,128)(2,1)}, bf16[576,384]{1,0:T(8,128)(2,1)S(1)}, u32[]{:S(2)}, u32[]{:S(2)}) %collective-permute-start.15) | collective-permute-done | bytes 442400 | tf_op jit(solution)/shard_map/ppermute | solution.py:281
  106.7 5.7 %collective-permute-done.8.refs_1_ = bf16[576,384]{1,0:T(8,128)(2,1)S(1)} collective-permute-done((bf16[576,384]{1,0:T(8,128)(2,1)}, bf16[576,384]{1,0:T(8,128)(2,1)S(1)}, u32[]{:S(2)}, u32[]{:S(2)}) %collective-permute-start.8) | collective-permute-done | bytes 442400 | tf_op jit(solution)/shard_map/ppermute | solution.py:281
  112.5 9.3 %collective-permute-done.14.refs_2_ = bf16[576,384]{1,0:T(8,128)(2,1)S(1)} collective-permute-done((bf16[576,384]{1,0:T(8,128)(2,1)}, bf16[576,384]{1,0:T(8,128)(2,1)S(1)}, u32[]{:S(2)}, u32[]{:S(2)}) %collective-permute-start.14) | collective-permute-done | bytes 442400 | tf_op jit(solution)/shard_map/ppermute | solution.py:281
  122.9 5.5 %shard_map.71 = (f32[576,640]{1,0:T(8,128)S(1)}, bf16[576,640]{1,0:T(8,128)(2,1)S(1)}) custom-call(s32[4]{0:T(128)S(1)} %pad_add_fusion.4.info, bf16[576,384]{1,0:T(8,128)(2,1)} %shard_map.65.refs_0_, bf16[576,384]{1,0:T(8,128)(2,1)} %collective-permute-done.7.rest_6_.refs_1_, bf16[576,384]{1,0:T(8,128)(2,1)S(1)} %collective-permute-done.14.refs_2_, ...), custom_call_target="tpu_custom_call" | custom-call | tf_op jit(solution)/shard_map/pallas_call | solution.py:133
  128.4 4.0 %collective-permute-start.16 = (bf16[576,640]{1,0:T(8,128)(2,1)S(1)}, bf16[576,640]{1,0:T(8,128)(2,1)S(1)}, u32[]{:S(2)}, u32[]{:S(2)}) collective-permute-start(bf16[576,640]{1,0:T(8,128)(2,1)S(1)} %get-tuple-element.24), channel_id=1, source_target_pairs={{0,32},{32,0},{1,33},{33,1},{2,34},{34,2},{3,35},{35,3},{4,36},{36... | collective-permute-start | bytes 2211848 | tf_op jit(solution)/shard_map/ppermute | solution.py:320
  132.4 1.9 %collective-permute-done.19.refs_3_ = bf16[576,384]{1,0:T(8,128)(2,1)S(1)} collective-permute-done((bf16[576,384]{1,0:T(8,128)(2,1)}, bf16[576,384]{1,0:T(8,128)(2,1)S(1)}, u32[]{:S(2)}, u32[]{:S(2)}) %collective-permute-start.19) | collective-permute-done | bytes 442400 | tf_op jit(solution)/shard_map/ppermute | solution.py:281
  134.3 6.6 %collective-permute-done.18.refs_2_ = bf16[576,384]{1,0:T(8,128)(2,1)S(1)} collective-permute-done((bf16[576,384]{1,0:T(8,128)(2,1)}, bf16[576,384]{1,0:T(8,128)(2,1)S(1)}, u32[]{:S(2)}, u32[]{:S(2)}) %collective-permute-start.18) | collective-permute-done | bytes 442400 | tf_op jit(solution)/shard_map/ppermute | solution.py:281
  140.9 5.5 %shard_map.72 = (f32[576,640]{1,0:T(8,128)S(1)}, bf16[576,640]{1,0:T(8,128)(2,1)S(1)}) custom-call(s32[4]{0:T(128)S(1)} %pad_add_fusion.4.info, bf16[576,384]{1,0:T(8,128)(2,1)} %shard_map.67.rest_2_.refs_0_, bf16[576,384]{1,0:T(8,128)(2,1)} %collective-permute-done.17.refs_1_, bf16[576,384]{1,0:T(8,128)(2,1)S(1)} %collective-permute-done.18.refs_2_, ...), custom_call_target="tpu_custom_call" | custom-call | tf_op jit(solution)/shard_map/pallas_call | solution.py:133
  146.4 4.2 %collective-permute-start.20 = (bf16[576,640]{1,0:T(8,128)(2,1)S(1)}, bf16[576,640]{1,0:T(8,128)(2,1)S(1)}, u32[]{:S(2)}, u32[]{:S(2)}) collective-permute-start(bf16[576,640]{1,0:T(8,128)(2,1)S(1)} %get-tuple-element.26), channel_id=1, source_target_pairs={{0,32},{32,0},{1,33},{33,1},{2,34},{34,2},{3,35},{35,3},{4,36},{36... | collective-permute-start | bytes 2211848 | tf_op jit(solution)/shard_map/ppermute | solution.py:320
  150.6 2.6 %collective-permute-done.12.refs_2_ = bf16[576,384]{1,0:T(8,128)(2,1)S(1)} collective-permute-done((bf16[576,384]{1,0:T(8,128)(2,1)}, bf16[576,384]{1,0:T(8,128)(2,1)S(1)}, u32[]{:S(2)}, u32[]{:S(2)}) %collective-permute-start.12) | collective-permute-done | bytes 442400 | tf_op jit(solution)/shard_map/ppermute | solution.py:281
  153.2 5.4 %shard_map.69 = (bf16[576,640]{1,0:T(8,128)(2,1)S(1)}, bf16[576,640]{1,0:T(8,128)(2,1)S(1)}) custom-call(s32[3]{0:T(128)S(1)} %pad_add_fusion.2.info, bf16[576,384]{1,0:T(8,128)(2,1)} %shard_map.66.refs_0_, bf16[576,384]{1,0:T(8,128)(2,1)S(1)} %collective-permute-done.8.refs_1_, bf16[576,384]{1,0:T(8,128)(2,1)S(1)} %collective-permute-done.12.refs_2_, ...), custom_call_target="tpu_custom_call" | custom-call | tf_op jit(solution)/shard_map/pallas_call | solution.py:133
  159.8 2.1 %shard_map.70 = (f32[576,640]{1,0:T(8,128)S(1)}, bf16[576,640]{1,0:T(8,128)(2,1)S(1)}) custom-call(s32[1]{0:T(128)} %bitcast.3.info, bf16[576,384]{1,0:T(8,128)(2,1)S(1)} %collective-permute-done.9.piece, bf16[1536,1280]{1,0:T(8,128)(2,1)} %all-gather.2.cloned.1.call-done.refs_3_.w_ref.refs_4_, bf16[576,640]{1,0:T(8,128)(2,1)S(1)} %get-tuple-element.19.mine_far, ...), custom_call_target="tpu_custom_call" | custom-call | tf_op jit(solution)/shard_map/pallas_call | solution.py:155
  162.0 2.2 %collective-permute-start.13 = (bf16[576,640]{1,0:T(8,128)(2,1)S(1)}, bf16[576,640]{1,0:T(8,128)(2,1)S(1)}, u32[]{:S(2)}, u32[]{:S(2)}) collective-permute-start(bf16[576,640]{1,0:T(8,128)(2,1)S(1)} %get-tuple-element.22), channel_id=1, source_target_pairs={{0,32},{32,0},{1,33},{33,1},{2,34},{34,2},{3,35},{35,3},{4,36},{36... | collective-permute-start | bytes 2211848 | tf_op jit(solution)/shard_map/ppermute | solution.py:320
  164.5 1.6 shard_map.73.rest_0_
  166.1 1.6 shard_map.74.rest_0_
  167.7 1.6 shard_map.75
  (62 shorter events, 13.7 us)
Async XLA Ops:
  6.5 115.3 %all-gather.2.cloned.1.call-start = ((), (), s32[]{:S(2)}) async-start(), calls=%async_computation | async-start | bytes 4177920 | tf_op jit(solution)/shard_map/all_gather | solution.py:311
  6.5 16.8 %collective-permute-start.10 = (bf16[96,640]{1,0:T(8,128)(2,1)}, bf16[96,640]{1,0:T(8,128)(2,1)S(1)}, u32[]{:S(2)}, u32[]{:S(2)}) collective-permute-start(bf16[96,640]{1,0:T(8,128)(2,1)} %own_ref.1), channel_id=1, source_target_pairs={{0,4},{4,0},{1,5},{5,1},{2,6},{6,2},{3,7},{7,3},{8,12},{12,8},{9,1... | collective-permute-start | bytes 368648 | tf_op jit(solution)/shard_map/ppermute | solution.py:308
  14.7 8.6 %copy-start.9 = (bf16[96,640]{1,0:T(8,128)(2,1)S(1)}, bf16[96,640]{1,0:T(8,128)(2,1)}, u32[]{:S(2)}) copy-start(bf16[96,640]{1,0:T(8,128)(2,1)} %own_ref.1) | copy-start | bytes 368644
  14.7 10.3 %copy-start = (bf16[1728,384]{1,0:T(8,128)(2,1)S(1)}, bf16[1728,384]{1,0:T(8,128)(2,1)}, u32[]{:S(2)}) copy-start(bf16[1728,384]{1,0:T(8,128)(2,1)} %k_ref.5) | copy-start | bytes 3981316
  14.7 10.3 %copy-start.1 = (bf16[1728,384]{1,0:T(8,128)(2,1)S(1)}, bf16[1728,384]{1,0:T(8,128)(2,1)}, u32[]{:S(2)}) copy-start(bf16[1728,384]{1,0:T(8,128)(2,1)} %v_ref.5) | copy-start | bytes 3981316
  18.3 15.8 %collective-permute-start.1 = (bf16[576,384]{1,0:T(8,128)(2,1)}, bf16[576,384]{1,0:T(8,128)(2,1)S(1)}, u32[]{:S(2)}, u32[]{:S(2)}) collective-permute-start(bf16[576,384]{1,0:T(8,128)(2,1)} %get-tuple-element.17), channel_id=1, source_target_pairs={{0,3},{3,0},{1,2},{2,1},{4,7},{7,4},{5,6},{6,5},{8,11},{11,8},{9,1... | collective-permute-start | bytes 1327112 | tf_op jit(solution)/shard_map/ppermute | solution.py:287
  20.7 13.4 %collective-permute-start.4 = (bf16[576,384]{1,0:T(8,128)(2,1)}, bf16[576,384]{1,0:T(8,128)(2,1)}, u32[]{:S(2)}, u32[]{:S(2)}) collective-permute-start(bf16[576,384]{1,0:T(8,128)(2,1)} %get-tuple-element.18), channel_id=1, source_target_pairs={{0,1},{3,2},{4,5},{7,6},{8,9},{11,10},{12,13},{15,14},{16,17},{19,... | collective-permute-start | bytes 1327112 | tf_op jit(solution)/shard_map/ppermute | solution.py:288
  23.3 10.7 %copy-start.10 = (bf16[96,640]{1,0:T(8,128)(2,1)}, bf16[96,640]{1,0:T(8,128)(2,1)S(1)}, u32[]{:S(2)}) copy-start(bf16[96,640]{1,0:T(8,128)(2,1)S(1)} %collective-permute-done.10.over_ref) | copy-start | bytes 368644
  23.4 10.7 %collective-permute-start.11 = (bf16[96,640]{1,0:T(8,128)(2,1)S(1)}, bf16[96,640]{1,0:T(8,128)(2,1)S(1)}, u32[]{:S(2)}, u32[]{:S(2)}) collective-permute-start(bf16[96,640]{1,0:T(8,128)(2,1)S(1)} %broadcast_select_fusion), channel_id=1, source_target_pairs={{0,32},{32,0},{1,33},{33,1},{2,34},{34,2},{3,35},{35,3},{4,36},{36... | collective-permute-start | bytes 368648 | tf_op jit(solution)/shard_map/ppermute | solution.py:309
  25.1 1.3 copy-start.2
  36.7 25.6 %collective-permute-start = (bf16[1152,384]{1,0:T(8,128)(2,1)}, bf16[1152,384]{1,0:T(8,128)(2,1)S(1)}, u32[]{:S(2)}, u32[]{:S(2)}) collective-permute-start(bf16[1152,384]{1,0:T(8,128)(2,1)} %get-tuple-element.16), channel_id=1, source_target_pairs={{0,1},{1,0},{2,3},{3,2},{4,5},{5,4},{6,7},{7,6},{8,9},{9,8},{10,11... | collective-permute-start | bytes 2654216 | tf_op jit(solution)/shard_map/ppermute | solution.py:286
  36.8 6.4 %collective-permute-start.5 = (bf16[576,384]{1,0:T(8,128)(2,1)}, bf16[576,384]{1,0:T(8,128)(2,1)}, u32[]{:S(2)}, u32[]{:S(2)}) collective-permute-start(bf16[576,384]{1,0:T(8,128)(2,1)} %collective-permute-done.4.rest_1_), channel_id=1, source_target_pairs={{2,6},{6,10},{10,14},{14,18},{18,22},{22,26},{26,30},{5,1},{9,5},{... | collective-permute-start | bytes 1327112 | tf_op jit(solution)/shard_map/ppermute | solution.py:295
  38.2 34.7 %collective-permute-start.2 = (bf16[576,384]{1,0:T(8,128)(2,1)}, bf16[576,384]{1,0:T(8,128)(2,1)}, u32[]{:S(2)}, u32[]{:S(2)}) collective-permute-start(bf16[576,384]{1,0:T(8,128)(2,1)} %get-tuple-element.18), channel_id=1, source_target_pairs={{1,2},{2,1},{5,6},{6,5},{9,10},{10,9},{13,14},{14,13},{17,18},{18,... | collective-permute-start | bytes 1327112 | tf_op jit(solution)/shard_map/ppermute | solution.py:289
  39.7 36.0 %collective-permute-start.3 = (bf16[576,384]{1,0:T(8,128)(2,1)}, bf16[576,384]{1,0:T(8,128)(2,1)}, u32[]{:S(2)}, u32[]{:S(2)}) collective-permute-start(bf16[576,384]{1,0:T(8,128)(2,1)} %copy-done.5), channel_id=1, source_target_pairs={{0,4},{4,8},{8,12},{12,16},{16,20},{20,24},{24,28},{7,3},{11,7},{1... | collective-permute-start | bytes 1327112 | tf_op jit(solution)/shard_map/ppermute | solution.py:295
  43.2 33.1 %collective-permute-start.6 = (bf16[576,384]{1,0:T(8,128)(2,1)}, bf16[576,384]{1,0:T(8,128)(2,1)}, u32[]{:S(2)}, u32[]{:S(2)}) collective-permute-start(bf16[576,384]{1,0:T(8,128)(2,1)} %collective-permute-done.5), channel_id=1, source_target_pairs={{2,0},{1,3},{6,4},{5,7},{10,8},{9,11},{14,12},{13,15},{18,16},{17,... | collective-permute-start | bytes 1327112 | tf_op jit(solution)/shard_map/ppermute | solution.py:299
  62.3 1.3 copy-start.3
  71.4 12.6 %collective-permute-start.7 = (bf16[576,384]{1,0:T(8,128)(2,1)}, bf16[576,384]{1,0:T(8,128)(2,1)}, u32[]{:S(2)}, u32[]{:S(2)}) collective-permute-start(bf16[576,384]{1,0:T(8,128)(2,1)} %shard_map.65.refs_0_), channel_id=1, source_target_pairs={{0,64},{64,128},{128,192},{192,0},{1,65},{65,129},{129,193},{193,1... | collective-permute-start | bytes 1327112 | tf_op jit(solution)/shard_map/ppermute | solution.py:281
  72.2 26.2 %collective-permute-start.17 = (bf16[576,384]{1,0:T(8,128)(2,1)}, bf16[576,384]{1,0:T(8,128)(2,1)}, u32[]{:S(2)}, u32[]{:S(2)}) collective-permute-start(bf16[576,384]{1,0:T(8,128)(2,1)} %shard_map.67.rest_2_.refs_0_), channel_id=1, source_target_pairs={{0,64},{64,128},{128,192},{192,0},{1,65},{65,129},{129,193},{193,1... | collective-permute-start | bytes 1327112 | tf_op jit(solution)/shard_map/ppermute | solution.py:281
  73.0 32.9 %collective-permute-start.15 = (bf16[576,384]{1,0:T(8,128)(2,1)}, bf16[576,384]{1,0:T(8,128)(2,1)S(1)}, u32[]{:S(2)}, u32[]{:S(2)}) collective-permute-start(bf16[576,384]{1,0:T(8,128)(2,1)} %shard_map.65.refs_0_), channel_id=1, source_target_pairs={{0,192},{64,0},{128,64},{192,128},{1,193},{65,1},{129,65},{193,129... | collective-permute-start | bytes 1327112 | tf_op jit(solution)/shard_map/ppermute | solution.py:281
  84.0 1.3 copy-start.4
  85.3 1.0 copy-start.6
  95.0 17.4 %collective-permute-start.8 = (bf16[576,384]{1,0:T(8,128)(2,1)}, bf16[576,384]{1,0:T(8,128)(2,1)S(1)}, u32[]{:S(2)}, u32[]{:S(2)}) collective-permute-start(bf16[576,384]{1,0:T(8,128)(2,1)} %shard_map.66.refs_0_), channel_id=1, source_target_pairs={{0,64},{64,128},{128,192},{192,0},{1,65},{65,129},{129,193},{193,1... | collective-permute-start | bytes 1327112 | tf_op jit(solution)/shard_map/ppermute | solution.py:281
  95.0 26.8 %collective-permute-start.14 = (bf16[576,384]{1,0:T(8,128)(2,1)}, bf16[576,384]{1,0:T(8,128)(2,1)S(1)}, u32[]{:S(2)}, u32[]{:S(2)}) collective-permute-start(bf16[576,384]{1,0:T(8,128)(2,1)} %collective-permute-done.7.rest_6_.refs_1_), channel_id=1, source_target_pairs={{0,64},{64,128},{128,192},{192,0},{1,65},{65,129},{129,193},{193,1... | collective-permute-start | bytes 1327112 | tf_op jit(solution)/shard_map/ppermute | solution.py:281
  95.2 39.1 %collective-permute-start.19 = (bf16[576,384]{1,0:T(8,128)(2,1)}, bf16[576,384]{1,0:T(8,128)(2,1)S(1)}, u32[]{:S(2)}, u32[]{:S(2)}) collective-permute-start(bf16[576,384]{1,0:T(8,128)(2,1)} %shard_map.67.rest_2_.refs_0_), channel_id=1, source_target_pairs={{0,192},{64,0},{128,64},{192,128},{1,193},{65,1},{129,65},{193,129... | collective-permute-start | bytes 1327112 | tf_op jit(solution)/shard_map/ppermute | solution.py:281
  98.3 42.5 %collective-permute-start.18 = (bf16[576,384]{1,0:T(8,128)(2,1)}, bf16[576,384]{1,0:T(8,128)(2,1)S(1)}, u32[]{:S(2)}, u32[]{:S(2)}) collective-permute-start(bf16[576,384]{1,0:T(8,128)(2,1)} %collective-permute-done.17.refs_1_), channel_id=1, source_target_pairs={{0,64},{64,128},{128,192},{192,0},{1,65},{65,129},{129,193},{193,1... | collective-permute-start | bytes 1327112 | tf_op jit(solution)/shard_map/ppermute | solution.py:281
  106.7 46.6 %collective-permute-start.12 = (bf16[576,384]{1,0:T(8,128)(2,1)}, bf16[576,384]{1,0:T(8,128)(2,1)S(1)}, u32[]{:S(2)}, u32[]{:S(2)}) collective-permute-start(bf16[576,384]{1,0:T(8,128)(2,1)} %shard_map.66.refs_0_), channel_id=1, source_target_pairs={{0,192},{64,0},{128,64},{192,128},{1,193},{65,1},{129,65},{193,129... | collective-permute-start | bytes 1327112 | tf_op jit(solution)/shard_map/ppermute | solution.py:281
  112.4 47.4 %collective-permute-start.9 = (bf16[576,384]{1,0:T(8,128)(2,1)S(1)}, bf16[576,384]{1,0:T(8,128)(2,1)S(1)}, u32[]{:S(2)}, u32[]{:S(2)}) collective-permute-start(bf16[576,384]{1,0:T(8,128)(2,1)S(1)} %collective-permute-done.8.refs_1_), channel_id=1, source_target_pairs={{0,64},{64,128},{128,192},{192,0},{1,65},{65,129},{129,193},{193,1... | collective-permute-start | bytes 1327112 | tf_op jit(solution)/shard_map/ppermute | solution.py:281
  121.9 1.0 copy-start.8
  128.4 37.7 %collective-permute-start.16 = (bf16[576,640]{1,0:T(8,128)(2,1)S(1)}, bf16[576,640]{1,0:T(8,128)(2,1)S(1)}, u32[]{:S(2)}, u32[]{:S(2)}) collective-permute-start(bf16[576,640]{1,0:T(8,128)(2,1)S(1)} %get-tuple-element.24), channel_id=1, source_target_pairs={{0,32},{32,0},{1,33},{33,1},{2,34},{34,2},{3,35},{35,3},{4,36},{36... | collective-permute-start | bytes 2211848 | tf_op jit(solution)/shard_map/ppermute | solution.py:320
  146.4 18.1 %collective-permute-start.20 = (bf16[576,640]{1,0:T(8,128)(2,1)S(1)}, bf16[576,640]{1,0:T(8,128)(2,1)S(1)}, u32[]{:S(2)}, u32[]{:S(2)}) collective-permute-start(bf16[576,640]{1,0:T(8,128)(2,1)S(1)} %get-tuple-element.26), channel_id=1, source_target_pairs={{0,32},{32,0},{1,33},{33,1},{2,34},{34,2},{3,35},{35,3},{4,36},{36... | collective-permute-start | bytes 2211848 | tf_op jit(solution)/shard_map/ppermute | solution.py:320
  159.8 4.4 %copy-start.12 = (f32[640]{0:T(1024)S(1)}, f32[640]{0:T(1024)}, u32[]{:S(2)}) copy-start(f32[640]{0:T(1024)} %param.11) | copy-start | bytes 7684
  162.0 5.7 %collective-permute-start.13 = (bf16[576,640]{1,0:T(8,128)(2,1)S(1)}, bf16[576,640]{1,0:T(8,128)(2,1)S(1)}, u32[]{:S(2)}, u32[]{:S(2)}) collective-permute-start(bf16[576,640]{1,0:T(8,128)(2,1)S(1)} %get-tuple-element.22), channel_id=1, source_target_pairs={{0,32},{32,0},{1,33},{33,1},{2,34},{34,2},{3,35},{35,3},{4,36},{36... | collective-permute-start | bytes 2211848 | tf_op jit(solution)/shard_map/ppermute | solution.py:320
  (3 other events, 2.2 us)
Sparse Core Ops, SparseCore 0:
  36.8 60.6 all-gather.1

commit v5 on v4

--- a/solution.py
+++ b/solution.py
@@ -310,7 +310,7 @@
     laid = lay(home.astype(jnp.int32).reshape(1), out_weight, over, beside, [key_round, value_side, a])
     weight = lax.all_gather(laid, ("y", "x"), axis=0, tiled=True)
 
-    c = frame(2, near_halo + inner_halo + far_halo, [b1])
+    c = frame(2, near_halo + inner_halo + far_halo, [])
     c1, c3 = along(c, 1), along(c, -1)
     c2 = along(c1, 1)
 

time: 179 us -> 181 us (1.011)
  the two profiles are of different devices: /device:TPU:9 before, /device:TPU:3 now
where the time goes in v5:
time: 181 us
  starting transfers between devices  64.4 us (36%)
  Pallas kernels  47.8 us (26%)
  waiting for transfers between devices  46.4 us (26%)
  between operations  14.2 us (8%)
  local copies, waits for them, and re-layouts  7.12 us (4%)
    ppermute x9, waiting for transfers between devices, along(): lax.ppermute(value, 'zl', [(i, (i + steps) % lines) for i in range(lines)])  31.1 us
    ppermute x9, starting transfers between devices, along(): lax.ppermute(value, 'zl', [(i, (i + steps) % lines) for i in range(lines)])  28.3 us
    pallas_call x3, Pallas kernels, attend(): pl.pallas_call(functools.partial(attend_body, len(halos)), out_shape=jax....  19 us
    pallas_call x3, Pallas kernels, project(): pl.pallas_call(functools.partial(project_body, [len(chunk) for chunk in c...  16.5 us
    ppermute x3, starting transfers between devices, swap(): return lax.ppermute(value, 'core', [(0, 1), (1, 0)])  11.9 us
    ppermute x2, waiting for transfers between devices, across_rows(): return lax.ppermute(value, SEQ, pairs)  9.25 us
    ppermute x1, starting transfers between devices, on_device(): over = lax.ppermute(out_weight, 'zh', [(0, 1), (1, 0)])  6.91 us
    unnamed x26, local copies, waits for them, and re-layouts  6.87 us
  transfers between devices with their start and end apart: 22, of which 8 were waited for; matrix products, arithmetic and copies ran while one was open for 1% of the time, Pallas kernels for 25%

profile of v5, /device:TPU:3, one launch (start us, length us, event | category | flops | bytes accessed | tf_op | source)
XLA Modules:
  0.0 180.8 jit_solution(15143732975781898260)
XLA Ops:
  6.5 6.9 %collective-permute-start.9 = (bf16[96,640]{1,0:T(8,128)(2,1)}, bf16[96,640]{1,0:T(8,128)(2,1)S(1)}, u32[]{:S(2)}, u32[]{:S(2)}) collective-permute-start(bf16[96,640]{1,0:T(8,128)(2,1)} %own_ref.1), channel_id=1, source_target_pairs={{0,4},{4,0},{1,5},{5,1},{2,6},{6,2},{3,7},{7,3},{8,12},{12,8},{9,1... | collective-permute-start | bytes 368648 | tf_op jit(solution)/shard_map/ppermute | solution.py:308
  14.7 3.5 %shard_map.64 = (bf16[1152,384]{1,0:T(8,128)(2,1)}, bf16[576,384]{1,0:T(8,128)(2,1)}, bf16[576,384]{1,0:T(8,128)(2,1)}) custom-call(s32[2]{0:T(128)} %pad_add_fusion.1.info, bf16[1728,384]{1,0:T(8,128)(2,1)} %k_ref.5, bf16[1728,384]{1,0:T(8,128)(2,1)} %v_ref.5, bf16[1728,384]{1,0:T(8,128)(2,1)} %k_ref.5, bf16[1728,384]{1,0:T(8,128)(2,1)} %v_ref.5), custom_call_target="tpu_custom_call" | custom-call | tf_op jit(solution)/shard_map/pallas_call | solution.py:213
  23.5 2.5 %shard_map.66.rest_2_.refs_0_ = bf16[576,384]{1,0:T(8,128)(2,1)} custom-call(s32[6]{0:T(128)S(1)} %stack.139.info, bf16[1728,384]{1,0:T(8,128)(2,1)S(1)} %copy-done.2, bf16[1728,384]{1,0:T(8,128)(2,1)S(1)} %copy-done, bf16[1728,384]{1,0:T(8,128)(2,1)S(1)} %copy-done.1), custom_call_target="tpu_custom_call" | custom-call | tf_op jit(solution)/shard_map/pallas_call | solution.py:80
  26.0 3.3 %collective-permute-done.1.rest_2_.rest_0_ = bf16[576,384]{1,0:T(8,128)(2,1)S(1)} collective-permute-done((bf16[576,384]{1,0:T(8,128)(2,1)}, bf16[576,384]{1,0:T(8,128)(2,1)S(1)}, u32[]{:S(2)}, u32[]{:S(2)}) %collective-permute-start.1) | collective-permute-done | bytes 442400 | tf_op jit(solution)/shard_map/ppermute | solution.py:287
  29.3 2.8 %collective-permute-done.4.rest_1_ = bf16[576,384]{1,0:T(8,128)(2,1)} collective-permute-done((bf16[576,384]{1,0:T(8,128)(2,1)}, bf16[576,384]{1,0:T(8,128)(2,1)}, u32[]{:S(2)}, u32[]{:S(2)}) %collective-permute-start.4) | collective-permute-done | bytes 442400 | tf_op jit(solution)/shard_map/ppermute | solution.py:288
  32.1 1.8 shard_map.67
  33.9 3.2 %collective-permute-start = (bf16[1152,384]{1,0:T(8,128)(2,1)}, bf16[1152,384]{1,0:T(8,128)(2,1)S(1)}, u32[]{:S(2)}, u32[]{:S(2)}) collective-permute-start(bf16[1152,384]{1,0:T(8,128)(2,1)} %get-tuple-element.16), channel_id=1, source_target_pairs={{0,1},{1,0},{2,3},{3,2},{4,5},{5,4},{6,7},{7,6},{8,9},{9,8},{10,11... | collective-permute-start | bytes 2654216 | tf_op jit(solution)/shard_map/ppermute | solution.py:286
  38.3 5.5 %collective-permute-start.2 = (bf16[576,384]{1,0:T(8,128)(2,1)}, bf16[576,384]{1,0:T(8,128)(2,1)}, u32[]{:S(2)}, u32[]{:S(2)}) collective-permute-start(bf16[576,384]{1,0:T(8,128)(2,1)} %get-tuple-element.18), channel_id=1, source_target_pairs={{1,2},{2,1},{5,6},{6,5},{9,10},{10,9},{13,14},{14,13},{17,18},{18,... | collective-permute-start | bytes 1327112 | tf_op jit(solution)/shard_map/ppermute | solution.py:289
  43.8 1.5 collective-permute-start.3
  45.3 9.3 %collective-permute-done.5 = bf16[576,384]{1,0:T(8,128)(2,1)} collective-permute-done((bf16[576,384]{1,0:T(8,128)(2,1)}, bf16[576,384]{1,0:T(8,128)(2,1)}, u32[]{:S(2)}, u32[]{:S(2)}) %collective-permute-start.5) | collective-permute-done | bytes 442400 | tf_op jit(solution)/shard_map/ppermute | solution.py:295
  54.5 2.0 %collective-permute-start.6 = (bf16[576,384]{1,0:T(8,128)(2,1)}, bf16[576,384]{1,0:T(8,128)(2,1)}, u32[]{:S(2)}, u32[]{:S(2)}) collective-permute-start(bf16[576,384]{1,0:T(8,128)(2,1)} %collective-permute-done.5), channel_id=1, source_target_pairs={{2,0},{1,3},{6,4},{5,7},{10,8},{9,11},{14,12},{13,15},{18,16},{17,... | collective-permute-start | bytes 1327112 | tf_op jit(solution)/shard_map/ppermute | solution.py:299
  56.6 19.7 %collective-permute-start.17 = (bf16[576,384]{1,0:T(8,128)(2,1)}, bf16[576,384]{1,0:T(8,128)(2,1)}, u32[]{:S(2)}, u32[]{:S(2)}) collective-permute-start(bf16[576,384]{1,0:T(8,128)(2,1)} %shard_map.66.rest_2_.refs_0_), channel_id=1, source_target_pairs={{0,64},{64,128},{128,192},{192,0},{1,65},{65,129},{129,193},{193,1... | collective-permute-start | bytes 1327112 | tf_op jit(solution)/shard_map/ppermute | solution.py:281
  77.7 7.9 %shard_map.70.refs_0_ = bf16[576,384]{1,0:T(8,128)(2,1)} custom-call(s32[6]{0:T(128)S(1)} %stack.153.info, bf16[1728,384]{1,0:T(8,128)(2,1)S(1)} %copy-done.3, bf16[1728,384]{1,0:T(8,128)(2,1)S(1)} %copy-done, bf16[1728,384]{1,0:T(8,128)(2,1)S(1)} %copy-done.1, bf16[1152,384]{1,0:T(8,128)(2,1)S(1)} %collective-permute-done.rest_0_.rest_1_, ...), custom_call_target="tpu_custom_call" | custom-call | tf_op jit(solution)/shard_map/pallas_call | solution.py:80
  85.7 3.5 %collective-permute-start.15 = (bf16[576,384]{1,0:T(8,128)(2,1)}, bf16[576,384]{1,0:T(8,128)(2,1)S(1)}, u32[]{:S(2)}, u32[]{:S(2)}) collective-permute-start(bf16[576,384]{1,0:T(8,128)(2,1)} %shard_map.70.refs_0_), channel_id=1, source_target_pairs={{0,192},{64,0},{128,64},{192,128},{1,193},{65,1},{129,65},{193,129... | collective-permute-start | bytes 1327112 | tf_op jit(solution)/shard_map/ppermute | solution.py:281
  91.6 8.6 %shard_map.65.refs_0_ = bf16[576,384]{1,0:T(8,128)(2,1)} custom-call(s32[6]{0:T(128)S(1)} %stack.129.info, bf16[1728,384]{1,0:T(8,128)(2,1)S(1)} %copy-done.4, bf16[1728,384]{1,0:T(8,128)(2,1)S(1)} %copy-done, bf16[1728,384]{1,0:T(8,128)(2,1)} %v_ref.5, bf16[1152,384]{1,0:T(8,128)(2,1)S(1)} %collective-permute-done.rest_0_.rest_1_, ...), custom_call_target="tpu_custom_call" | custom-call | tf_op jit(solution)/shard_map/pallas_call | solution.py:80
  100.3 3.3 %collective-permute-start.19 = (bf16[576,384]{1,0:T(8,128)(2,1)}, bf16[576,384]{1,0:T(8,128)(2,1)S(1)}, u32[]{:S(2)}, u32[]{:S(2)}) collective-permute-start(bf16[576,384]{1,0:T(8,128)(2,1)} %shard_map.66.rest_2_.refs_0_), channel_id=1, source_target_pairs={{0,192},{64,0},{128,64},{192,128},{1,193},{65,1},{129,65},{193,129... | collective-permute-start | bytes 1327112 | tf_op jit(solution)/shard_map/ppermute | solution.py:281
  103.6 2.5 %collective-permute-done.15.refs_3_ = bf16[576,384]{1,0:T(8,128)(2,1)S(1)} collective-permute-done((bf16[576,384]{1,0:T(8,128)(2,1)}, bf16[576,384]{1,0:T(8,128)(2,1)S(1)}, u32[]{:S(2)}, u32[]{:S(2)}) %collective-permute-start.15) | collective-permute-done | bytes 442400 | tf_op jit(solution)/shard_map/ppermute | solution.py:281
  106.9 1.8 collective-permute-start.11
  108.6 8.1 %collective-permute-done.7.refs_1_ = bf16[576,384]{1,0:T(8,128)(2,1)S(1)} collective-permute-done((bf16[576,384]{1,0:T(8,128)(2,1)}, bf16[576,384]{1,0:T(8,128)(2,1)S(1)}, u32[]{:S(2)}, u32[]{:S(2)}) %collective-permute-start.7) | collective-permute-done | bytes 442400 | tf_op jit(solution)/shard_map/ppermute | solution.py:281
  116.9 9.3 %collective-permute-done.14.refs_2_ = bf16[576,384]{1,0:T(8,128)(2,1)S(1)} collective-permute-done((bf16[576,384]{1,0:T(8,128)(2,1)}, bf16[576,384]{1,0:T(8,128)(2,1)S(1)}, u32[]{:S(2)}, u32[]{:S(2)}) %collective-permute-start.14) | collective-permute-done | bytes 442400 | tf_op jit(solution)/shard_map/ppermute | solution.py:281
  127.3 5.5 %shard_map.71 = (f32[576,640]{1,0:T(8,128)S(1)}, bf16[576,640]{1,0:T(8,128)(2,1)S(1)}) custom-call(s32[4]{0:T(128)S(1)} %pad_add_fusion.4.info, bf16[576,384]{1,0:T(8,128)(2,1)} %shard_map.70.refs_0_, bf16[576,384]{1,0:T(8,128)(2,1)} %collective-permute-done.13.refs_1_, bf16[576,384]{1,0:T(8,128)(2,1)S(1)} %collective-permute-done.14.refs_2_, ...), custom_call_target="tpu_custom_call" | custom-call | tf_op jit(solution)/shard_map/pallas_call | solution.py:133
  132.8 4.6 %collective-permute-start.16 = (bf16[576,640]{1,0:T(8,128)(2,1)S(1)}, bf16[576,640]{1,0:T(8,128)(2,1)S(1)}, u32[]{:S(2)}, u32[]{:S(2)}) collective-permute-start(bf16[576,640]{1,0:T(8,128)(2,1)S(1)} %get-tuple-element.24), channel_id=1, source_target_pairs={{0,32},{32,0},{1,33},{33,1},{2,34},{34,2},{3,35},{35,3},{4,36},{36... | collective-permute-start | bytes 2211848 | tf_op jit(solution)/shard_map/ppermute | solution.py:320
  137.4 7.9 %collective-permute-done.18.refs_2_ = bf16[576,384]{1,0:T(8,128)(2,1)S(1)} collective-permute-done((bf16[576,384]{1,0:T(8,128)(2,1)}, bf16[576,384]{1,0:T(8,128)(2,1)S(1)}, u32[]{:S(2)}, u32[]{:S(2)}) %collective-permute-start.18) | collective-permute-done | bytes 442400 | tf_op jit(solution)/shard_map/ppermute | solution.py:281
  145.3 5.5 %shard_map.72 = (f32[576,640]{1,0:T(8,128)S(1)}, bf16[576,640]{1,0:T(8,128)(2,1)S(1)}) custom-call(s32[4]{0:T(128)S(1)} %pad_add_fusion.4.info, bf16[576,384]{1,0:T(8,128)(2,1)} %shard_map.66.rest_2_.refs_0_, bf16[576,384]{1,0:T(8,128)(2,1)} %collective-permute-done.17.refs_1_, bf16[576,384]{1,0:T(8,128)(2,1)S(1)} %collective-permute-done.18.refs_2_, ...), custom_call_target="tpu_custom_call" | custom-call | tf_op jit(solution)/shard_map/pallas_call | solution.py:133
  150.8 4.8 %collective-permute-start.20 = (bf16[576,640]{1,0:T(8,128)(2,1)S(1)}, bf16[576,640]{1,0:T(8,128)(2,1)S(1)}, u32[]{:S(2)}, u32[]{:S(2)}) collective-permute-start(bf16[576,640]{1,0:T(8,128)(2,1)S(1)} %get-tuple-element.26), channel_id=1, source_target_pairs={{0,32},{32,0},{1,33},{33,1},{2,34},{34,2},{3,35},{35,3},{4,36},{36... | collective-permute-start | bytes 2211848 | tf_op jit(solution)/shard_map/ppermute | solution.py:320
  155.6 5.4 %shard_map.68 = (bf16[576,640]{1,0:T(8,128)(2,1)S(1)}, bf16[576,640]{1,0:T(8,128)(2,1)S(1)}) custom-call(s32[3]{0:T(128)S(1)} %pad_add_fusion.2.info, bf16[576,384]{1,0:T(8,128)(2,1)} %shard_map.65.refs_0_, bf16[576,384]{1,0:T(8,128)(2,1)S(1)} %collective-permute-done.7.refs_1_, bf16[576,384]{1,0:T(8,128)(2,1)S(1)} %collective-permute-done.11.refs_2_, ...), custom_call_target="tpu_custom_call" | custom-call | tf_op jit(solution)/shard_map/pallas_call | solution.py:133
  161.0 3.2 %collective-permute-done.8.piece = bf16[576,384]{1,0:T(8,128)(2,1)S(1)} collective-permute-done((bf16[576,384]{1,0:T(8,128)(2,1)S(1)}, bf16[576,384]{1,0:T(8,128)(2,1)S(1)}, u32[]{:S(2)}, u32[]{:S(2)}) %collective-permute-start.8) | collective-permute-done | bytes 442400 | tf_op jit(solution)/shard_map/ppermute | solution.py:281
  164.2 2.1 %shard_map.69 = (f32[576,640]{1,0:T(8,128)S(1)}, bf16[576,640]{1,0:T(8,128)(2,1)S(1)}) custom-call(s32[1]{0:T(128)} %bitcast.3.info, bf16[576,384]{1,0:T(8,128)(2,1)S(1)} %collective-permute-done.8.piece, bf16[1536,1280]{1,0:T(8,128)(2,1)} %all-gather.2.cloned.1.call-done.refs_3_.w_ref.refs_4_, bf16[576,640]{1,0:T(8,128)(2,1)S(1)} %get-tuple-element.19.mine_far, ...), custom_call_target="tpu_custom_call" | custom-call | tf_op jit(solution)/shard_map/pallas_call | solution.py:155
  166.4 2.5 %collective-permute-start.12 = (bf16[576,640]{1,0:T(8,128)(2,1)S(1)}, bf16[576,640]{1,0:T(8,128)(2,1)S(1)}, u32[]{:S(2)}, u32[]{:S(2)}) collective-permute-start(bf16[576,640]{1,0:T(8,128)(2,1)S(1)} %get-tuple-element.22), channel_id=1, source_target_pairs={{0,32},{32,0},{1,33},{33,1},{2,34},{34,2},{3,35},{35,3},{4,36},{36... | collective-permute-start | bytes 2211848 | tf_op jit(solution)/shard_map/ppermute | solution.py:320
  169.1 1.6 shard_map.73.rest_0_
  170.8 1.6 shard_map.74.rest_0_
  172.4 1.6 shard_map.75
  (62 shorter events, 13.3 us)
Async XLA Ops:
  6.5 119.7 %all-gather.2.cloned.1.call-start = ((), (), s32[]{:S(2)}) async-start(), calls=%async_computation | async-start | bytes 4177920 | tf_op jit(solution)/shard_map/all_gather | solution.py:311
  6.5 14.2 %collective-permute-start.9 = (bf16[96,640]{1,0:T(8,128)(2,1)}, bf16[96,640]{1,0:T(8,128)(2,1)S(1)}, u32[]{:S(2)}, u32[]{:S(2)}) collective-permute-start(bf16[96,640]{1,0:T(8,128)(2,1)} %own_ref.1), channel_id=1, source_target_pairs={{0,4},{4,0},{1,5},{5,1},{2,6},{6,2},{3,7},{7,3},{8,12},{12,8},{9,1... | collective-permute-start | bytes 368648 | tf_op jit(solution)/shard_map/ppermute | solution.py:308
  14.7 6.1 %copy-start.9 = (bf16[96,640]{1,0:T(8,128)(2,1)S(1)}, bf16[96,640]{1,0:T(8,128)(2,1)}, u32[]{:S(2)}) copy-start(bf16[96,640]{1,0:T(8,128)(2,1)} %own_ref.1) | copy-start | bytes 368644
  14.7 7.5 %copy-start = (bf16[1728,384]{1,0:T(8,128)(2,1)S(1)}, bf16[1728,384]{1,0:T(8,128)(2,1)}, u32[]{:S(2)}) copy-start(bf16[1728,384]{1,0:T(8,128)(2,1)} %k_ref.5) | copy-start | bytes 3981316
  14.7 7.5 %copy-start.1 = (bf16[1728,384]{1,0:T(8,128)(2,1)S(1)}, bf16[1728,384]{1,0:T(8,128)(2,1)}, u32[]{:S(2)}) copy-start(bf16[1728,384]{1,0:T(8,128)(2,1)} %v_ref.5) | copy-start | bytes 3981316
  18.2 11.0 %collective-permute-start.1 = (bf16[576,384]{1,0:T(8,128)(2,1)}, bf16[576,384]{1,0:T(8,128)(2,1)S(1)}, u32[]{:S(2)}, u32[]{:S(2)}) collective-permute-start(bf16[576,384]{1,0:T(8,128)(2,1)} %get-tuple-element.17), channel_id=1, source_target_pairs={{0,3},{3,0},{1,2},{2,1},{4,7},{7,4},{5,6},{6,5},{8,11},{11,8},{9,1... | collective-permute-start | bytes 1327112 | tf_op jit(solution)/shard_map/ppermute | solution.py:287
  19.4 12.6 %collective-permute-start.4 = (bf16[576,384]{1,0:T(8,128)(2,1)}, bf16[576,384]{1,0:T(8,128)(2,1)}, u32[]{:S(2)}, u32[]{:S(2)}) collective-permute-start(bf16[576,384]{1,0:T(8,128)(2,1)} %get-tuple-element.18), channel_id=1, source_target_pairs={{0,1},{3,2},{4,5},{7,6},{8,9},{11,10},{12,13},{15,14},{16,17},{19,... | collective-permute-start | bytes 1327112 | tf_op jit(solution)/shard_map/ppermute | solution.py:288
  20.8 5.2 %copy-start.10 = (bf16[96,640]{1,0:T(8,128)(2,1)}, bf16[96,640]{1,0:T(8,128)(2,1)S(1)}, u32[]{:S(2)}) copy-start(bf16[96,640]{1,0:T(8,128)(2,1)S(1)} %collective-permute-done.9.over_ref) | copy-start | bytes 368644
  20.8 5.2 %collective-permute-start.10 = (bf16[96,640]{1,0:T(8,128)(2,1)S(1)}, bf16[96,640]{1,0:T(8,128)(2,1)S(1)}, u32[]{:S(2)}, u32[]{:S(2)}) collective-permute-start(bf16[96,640]{1,0:T(8,128)(2,1)S(1)} %broadcast_select_fusion), channel_id=1, source_target_pairs={{0,32},{32,0},{1,33},{33,1},{2,34},{34,2},{3,35},{35,3},{4,36},{36... | collective-permute-start | bytes 368648 | tf_op jit(solution)/shard_map/ppermute | solution.py:309
  22.2 1.3 copy-start.2
  26.0 6.1 %copy-start.11 = (bf16[96,640]{1,0:T(8,128)(2,1)}, bf16[96,640]{1,0:T(8,128)(2,1)S(1)}, u32[]{:S(2)}) copy-start(bf16[96,640]{1,0:T(8,128)(2,1)S(1)} %collective-permute-done.10.beside_ref) | copy-start | bytes 368644
  29.3 2.8 %copy-start.5 = (bf16[576,384]{1,0:T(8,128)(2,1)}, bf16[576,384]{1,0:T(8,128)(2,1)S(1)}, u32[]{:S(2)}) copy-start(bf16[576,384]{1,0:T(8,128)(2,1)S(1)} %collective-permute-done.1.rest_2_.rest_0_) | copy-start | bytes 1327108
  33.9 42.5 %collective-permute-start = (bf16[1152,384]{1,0:T(8,128)(2,1)}, bf16[1152,384]{1,0:T(8,128)(2,1)S(1)}, u32[]{:S(2)}, u32[]{:S(2)}) collective-permute-start(bf16[1152,384]{1,0:T(8,128)(2,1)} %get-tuple-element.16), channel_id=1, source_target_pairs={{0,1},{1,0},{2,3},{3,2},{4,5},{5,4},{6,7},{7,6},{8,9},{9,8},{10,11... | collective-permute-start | bytes 2654216 | tf_op jit(solution)/shard_map/ppermute | solution.py:286
  37.0 17.5 %collective-permute-start.5 = (bf16[576,384]{1,0:T(8,128)(2,1)}, bf16[576,384]{1,0:T(8,128)(2,1)}, u32[]{:S(2)}, u32[]{:S(2)}) collective-permute-start(bf16[576,384]{1,0:T(8,128)(2,1)} %collective-permute-done.4.rest_1_), channel_id=1, source_target_pairs={{2,6},{6,10},{10,14},{14,18},{18,22},{22,26},{26,30},{5,1},{9,5},{... | collective-permute-start | bytes 1327112 | tf_op jit(solution)/shard_map/ppermute | solution.py:295
  38.3 47.3 %collective-permute-start.2 = (bf16[576,384]{1,0:T(8,128)(2,1)}, bf16[576,384]{1,0:T(8,128)(2,1)}, u32[]{:S(2)}, u32[]{:S(2)}) collective-permute-start(bf16[576,384]{1,0:T(8,128)(2,1)} %get-tuple-element.18), channel_id=1, source_target_pairs={{1,2},{2,1},{5,6},{6,5},{9,10},{10,9},{13,14},{14,13},{17,18},{18,... | collective-permute-start | bytes 1327112 | tf_op jit(solution)/shard_map/ppermute | solution.py:289
  43.8 45.3 %collective-permute-start.3 = (bf16[576,384]{1,0:T(8,128)(2,1)}, bf16[576,384]{1,0:T(8,128)(2,1)}, u32[]{:S(2)}, u32[]{:S(2)}) collective-permute-start(bf16[576,384]{1,0:T(8,128)(2,1)} %copy-done.5), channel_id=1, source_target_pairs={{0,4},{4,8},{8,12},{12,16},{16,20},{20,24},{24,28},{7,3},{11,7},{1... | collective-permute-start | bytes 1327112 | tf_op jit(solution)/shard_map/ppermute | solution.py:295
  54.5 34.6 %collective-permute-start.6 = (bf16[576,384]{1,0:T(8,128)(2,1)}, bf16[576,384]{1,0:T(8,128)(2,1)}, u32[]{:S(2)}, u32[]{:S(2)}) collective-permute-start(bf16[576,384]{1,0:T(8,128)(2,1)} %collective-permute-done.5), channel_id=1, source_target_pairs={{2,0},{1,3},{6,4},{5,7},{10,8},{9,11},{14,12},{13,15},{18,16},{17,... | collective-permute-start | bytes 1327112 | tf_op jit(solution)/shard_map/ppermute | solution.py:299
  56.6 47.0 %collective-permute-start.17 = (bf16[576,384]{1,0:T(8,128)(2,1)}, bf16[576,384]{1,0:T(8,128)(2,1)}, u32[]{:S(2)}, u32[]{:S(2)}) collective-permute-start(bf16[576,384]{1,0:T(8,128)(2,1)} %shard_map.66.rest_2_.refs_0_), channel_id=1, source_target_pairs={{0,64},{64,128},{128,192},{192,0},{1,65},{65,129},{129,193},{193,1... | collective-permute-start | bytes 1327112 | tf_op jit(solution)/shard_map/ppermute | solution.py:281
  76.4 1.3 copy-start.3
  85.6 14.6 %collective-permute-start.13 = (bf16[576,384]{1,0:T(8,128)(2,1)}, bf16[576,384]{1,0:T(8,128)(2,1)}, u32[]{:S(2)}, u32[]{:S(2)}) collective-permute-start(bf16[576,384]{1,0:T(8,128)(2,1)} %shard_map.70.refs_0_), channel_id=1, source_target_pairs={{0,64},{64,128},{128,192},{192,0},{1,65},{65,129},{129,193},{193,1... | collective-permute-start | bytes 1327112 | tf_op jit(solution)/shard_map/ppermute | solution.py:281
  85.7 20.4 %collective-permute-start.15 = (bf16[576,384]{1,0:T(8,128)(2,1)}, bf16[576,384]{1,0:T(8,128)(2,1)S(1)}, u32[]{:S(2)}, u32[]{:S(2)}) collective-permute-start(bf16[576,384]{1,0:T(8,128)(2,1)} %shard_map.70.refs_0_), channel_id=1, source_target_pairs={{0,192},{64,0},{128,64},{192,128},{1,193},{65,1},{129,65},{193,129... | collective-permute-start | bytes 1327112 | tf_op jit(solution)/shard_map/ppermute | solution.py:281
  89.1 1.4 copy-start.4
  100.2 16.6 %collective-permute-start.7 = (bf16[576,384]{1,0:T(8,128)(2,1)}, bf16[576,384]{1,0:T(8,128)(2,1)S(1)}, u32[]{:S(2)}, u32[]{:S(2)}) collective-permute-start(bf16[576,384]{1,0:T(8,128)(2,1)} %shard_map.65.refs_0_), channel_id=1, source_target_pairs={{0,64},{64,128},{128,192},{192,0},{1,65},{65,129},{129,193},{193,1... | collective-permute-start | bytes 1327112 | tf_op jit(solution)/shard_map/ppermute | solution.py:281
  100.2 26.0 %collective-permute-start.14 = (bf16[576,384]{1,0:T(8,128)(2,1)}, bf16[576,384]{1,0:T(8,128)(2,1)S(1)}, u32[]{:S(2)}, u32[]{:S(2)}) collective-permute-start(bf16[576,384]{1,0:T(8,128)(2,1)} %collective-permute-done.13.refs_1_), channel_id=1, source_target_pairs={{0,64},{64,128},{128,192},{192,0},{1,65},{65,129},{129,193},{193,1... | collective-permute-start | bytes 1327112 | tf_op jit(solution)/shard_map/ppermute | solution.py:281
  100.3 37.1 %collective-permute-start.19 = (bf16[576,384]{1,0:T(8,128)(2,1)}, bf16[576,384]{1,0:T(8,128)(2,1)S(1)}, u32[]{:S(2)}, u32[]{:S(2)}) collective-permute-start(bf16[576,384]{1,0:T(8,128)(2,1)} %shard_map.66.rest_2_.refs_0_), channel_id=1, source_target_pairs={{0,192},{64,0},{128,64},{192,128},{1,193},{65,1},{129,65},{193,129... | collective-permute-start | bytes 1327112 | tf_op jit(solution)/shard_map/ppermute | solution.py:281
  103.6 41.7 %collective-permute-start.18 = (bf16[576,384]{1,0:T(8,128)(2,1)}, bf16[576,384]{1,0:T(8,128)(2,1)S(1)}, u32[]{:S(2)}, u32[]{:S(2)}) collective-permute-start(bf16[576,384]{1,0:T(8,128)(2,1)} %collective-permute-done.17.refs_1_), channel_id=1, source_target_pairs={{0,64},{64,128},{128,192},{192,0},{1,65},{65,129},{129,193},{193,1... | collective-permute-start | bytes 1327112 | tf_op jit(solution)/shard_map/ppermute | solution.py:281
  106.9 48.7 %collective-permute-start.11 = (bf16[576,384]{1,0:T(8,128)(2,1)}, bf16[576,384]{1,0:T(8,128)(2,1)S(1)}, u32[]{:S(2)}, u32[]{:S(2)}) collective-permute-start(bf16[576,384]{1,0:T(8,128)(2,1)} %shard_map.65.refs_0_), channel_id=1, source_target_pairs={{0,192},{64,0},{128,64},{192,128},{1,193},{65,1},{129,65},{193,129... | collective-permute-start | bytes 1327112 | tf_op jit(solution)/shard_map/ppermute | solution.py:281
  116.8 47.4 %collective-permute-start.8 = (bf16[576,384]{1,0:T(8,128)(2,1)S(1)}, bf16[576,384]{1,0:T(8,128)(2,1)S(1)}, u32[]{:S(2)}, u32[]{:S(2)}) collective-permute-start(bf16[576,384]{1,0:T(8,128)(2,1)S(1)} %collective-permute-done.7.refs_1_), channel_id=1, source_target_pairs={{0,64},{64,128},{128,192},{192,0},{1,65},{65,129},{129,193},{193,1... | collective-permute-start | bytes 1327112 | tf_op jit(solution)/shard_map/ppermute | solution.py:281
  132.8 38.0 %collective-permute-start.16 = (bf16[576,640]{1,0:T(8,128)(2,1)S(1)}, bf16[576,640]{1,0:T(8,128)(2,1)S(1)}, u32[]{:S(2)}, u32[]{:S(2)}) collective-permute-start(bf16[576,640]{1,0:T(8,128)(2,1)S(1)} %get-tuple-element.24), channel_id=1, source_target_pairs={{0,32},{32,0},{1,33},{33,1},{2,34},{34,2},{3,35},{35,3},{4,36},{36... | collective-permute-start | bytes 2211848 | tf_op jit(solution)/shard_map/ppermute | solution.py:320
  150.8 18.4 %collective-permute-start.20 = (bf16[576,640]{1,0:T(8,128)(2,1)S(1)}, bf16[576,640]{1,0:T(8,128)(2,1)S(1)}, u32[]{:S(2)}, u32[]{:S(2)}) collective-permute-start(bf16[576,640]{1,0:T(8,128)(2,1)S(1)} %get-tuple-element.26), channel_id=1, source_target_pairs={{0,32},{32,0},{1,33},{33,1},{2,34},{34,2},{3,35},{35,3},{4,36},{36... | collective-permute-start | bytes 2211848 | tf_op jit(solution)/shard_map/ppermute | solution.py:320
  164.2 4.7 %copy-start.12 = (f32[640]{0:T(1024)S(1)}, f32[640]{0:T(1024)}, u32[]{:S(2)}) copy-start(f32[640]{0:T(1024)} %param.11) | copy-start | bytes 7684
  166.4 6.0 %collective-permute-start.12 = (bf16[576,640]{1,0:T(8,128)(2,1)S(1)}, bf16[576,640]{1,0:T(8,128)(2,1)S(1)}, u32[]{:S(2)}, u32[]{:S(2)}) collective-permute-start(bf16[576,640]{1,0:T(8,128)(2,1)S(1)} %get-tuple-element.22), channel_id=1, source_target_pairs={{0,32},{32,0},{1,33},{33,1},{2,34},{34,2},{3,35},{35,3},{4,36},{36... | collective-permute-start | bytes 2211848 | tf_op jit(solution)/shard_map/ppermute | solution.py:320
  (3 other events, 2.8 us)
Sparse Core Ops, SparseCore 0:
  34.0 64.1 all-gather.1
